TPU v7x, 256 devices: a whole 4x4x8 slice. The times are simulated.
256 devices in a mesh: gx: 32 (over y_lo, z, core), row: 8 (over y_hi, x).
Axes of the slice: x: 4, y: 4 (y_hi: 2, y_lo: 2; y = y_hi * 2 + y_lo), z: 8, core: 2. Of those that a mesh axis runs over, the one named last changes fastest.
Arguments:
- config_fields: float32 [32, 3, 128, 96, 128], P('row', None, 'gx'), may hold values from -6 to 6
- velocity: float32 [3, 128, 96, 128], P(None, 'gx'), may hold values from -0.4 to 3.1
- noise_keys: int32 [32, 2], P('row'), may hold values from 0 to 1048575
Outputs:
- config_out: float32 [32, 3, 128, 96, 128], P('row', None, 'gx')
- velocity_out: float32 [3, 128, 96, 128], P(None, 'gx')
All inputs are finite; a program needn't handle non-finite values.
Results may differ from a plain program's by a relative error of at most 0.00017.
Values sent between devices are 32-bit elements; how exact they have to be, the bound alone decides.
No kernel may reach another device: no remote copies, remote signals or barrier semaphores. Data moves between devices by JAX's collectives and lax.ppermute only.
A program may use at most 128 MiB of HBM per device.

v0:
```python
import math

import jax
import jax.numpy as jnp
from jax import lax
from jax.sharding import PartitionSpec as P

STEPS = 2


time_step = 0.05
viscosity = 0.5
stress_coef = 4.0
relax_time = 0.5
spring_limit = 10.0
spring_floor = 0.2
bulk_target = 1.0


def extended_2(cells, sides, width):
    for axis, dim in sides:
        count = lax.axis_size(axis)
        head = lax.slice_in_dim(cells, 0, width, axis=dim)
        tail = lax.slice_in_dim(cells, cells.shape[dim] - width, cells.shape[dim], axis=dim)
        cells = jnp.concatenate(
            [
                lax.ppermute(tail, axis, [(i, (i + 1) % count) for i in range(count)]),
                cells,
                lax.ppermute(head, axis, [((i + 1) % count, i) for i in range(count)]),
            ],
            axis=dim,
        )
    return cells


def mix_bits(value):
    value = value ^ lax.shift_right_logical(value, jnp.int32(16))
    value = value * jnp.int32(73244475)
    value = value ^ lax.shift_right_logical(value, jnp.int32(16))
    value = value * jnp.int32(73244475)
    return value ^ lax.shift_right_logical(value, jnp.int32(16))


def gauss_noise(key, index):
    salted = mix_bits(key + jnp.int32(40503))
    first = mix_bits(index * 2 ^ salted)
    second = mix_bits(index * 2 + 1 ^ salted)
    mask = jnp.int32(16777215)
    upper = ((first & mask).astype(jnp.float32) + 0.5) / 16777216.0
    lower = ((second & mask).astype(jnp.float32) + 0.5) / 16777216.0
    return jnp.sqrt(-2.0 * jnp.log(upper)) * jnp.cos(6.283185307179586 * lower)


def cell_index(x_start, count, total_x, rows, depth):
    shape = (3, count, rows, depth)
    comp = lax.broadcasted_iota(jnp.int32, shape, 0)
    xpos = lax.broadcasted_iota(jnp.int32, shape, 1) + x_start
    ypos = lax.broadcasted_iota(jnp.int32, shape, 2)
    zpos = lax.broadcasted_iota(jnp.int32, shape, 3)
    return ((comp * total_x + xpos) * rows + ypos) * depth + zpos


def diff_x(extended):
    return 0.5 * (extended[..., 2:, :, :] - extended[..., :-2, :, :])


def diff_y(field):
    widths = [(0, 0)] * (field.ndim - 2) + [(1, 1), (0, 0)]
    padded = jnp.pad(field, widths)
    return 0.5 * (padded[..., 2:, :] - padded[..., :-2, :])


def diff_z(field):
    return 0.5 * (jnp.roll(field, -1, -1) - jnp.roll(field, 1, -1))


def spring_factor(extended):
    length = jnp.sum(extended * extended, axis=-4)
    return 1.0 / jnp.maximum(1.0 - length / spring_limit, spring_floor)


def divergence(stress):
    return diff_x(stress[:, 0]) + diff_y(stress[:, 1, 1:-1]) + diff_z(stress[:, 2, 1:-1])


def advance_config(field, field_ext, spring_ext, flow, slopes, noise):
    grad_x, grad_y, grad_z = slopes
    along = flow[0] * diff_x(field_ext) + flow[1] * diff_y(field) + flow[2] * diff_z(field)
    stretch = (
        grad_x * field[..., 0:1, :, :, :]
        + grad_y * field[..., 1:2, :, :, :]
        + grad_z * field[..., 2:3, :, :, :]
    )
    spring = spring_ext[..., None, 1:-1, :, :]
    drift = -along + stretch - spring * field / (2.0 * relax_time)
    return field + time_step * drift + math.sqrt(time_step / relax_time) * noise


def velocity_rate(flow_ext, stress_div):
    padded = jnp.pad(flow_ext, ((0, 0), (0, 0), (1, 1), (0, 0)))
    centre = padded[:, 1:-1, 1:-1]
    grad_x = 0.5 * (padded[:, 2:, 1:-1] - padded[:, :-2, 1:-1])
    grad_y = 0.5 * (padded[:, 1:-1, 2:] - padded[:, 1:-1, :-2])
    grad_z = 0.5 * (jnp.roll(centre, -1, 3) - jnp.roll(centre, 1, 3))
    along = centre[0] * grad_x + centre[1] * grad_y + centre[2] * grad_z
    lap = padded[:, 2:, 1:-1] + padded[:, :-2, 1:-1] - 2.0 * centre
    lap = lap + (padded[:, 1:-1, 2:] + padded[:, 1:-1, :-2] - 2.0 * centre)
    lap = lap + (jnp.roll(centre, -1, 3) + jnp.roll(centre, 1, 3) - 2.0 * centre)
    return -along + viscosity * lap + stress_coef * stress_div


def adjust_flux(start, flux, cells):
    return jnp.concatenate([start[:1] + (bulk_target - flux / cells), start[1:]], axis=0)


def shards(config_fields, velocity, noise_keys):
    fields_here, _, width, rows, depth = config_fields.shape
    total_fields = fields_here * lax.axis_size("row")
    total_x = width * lax.axis_size("gx")
    cells = total_x * rows * depth
    x_start = lax.axis_index("gx") * width
    index = cell_index(x_start, width, total_x, rows, depth)
    config, flow = (config_fields, velocity)
    for step in range(STEPS):
        config_rims = jnp.concatenate([config[:, :, :1], config[:, :, -1:]], axis=2)
        flow_rims = jnp.concatenate([flow[None, :, :1], flow[None, :, -1:]], axis=2)
        edges = jnp.concatenate([config_rims, flow_rims], axis=0)
        rims = extended_2(edges, (("gx", 2),), 1)
        config_ext = jnp.concatenate(
            [rims[:fields_here, :, :1], config, rims[:fields_here, :, 3:]], axis=2
        )
        flow_ext = jnp.concatenate(
            [rims[fields_here, :, :1], flow, rims[fields_here, :, 3:]], axis=1
        )
        slopes = (diff_x(flow_ext), diff_y(flow), diff_z(flow))
        spring_ext = spring_factor(config_ext)
        weighted = spring_ext[:, None] * config_ext
        stress = jnp.sum(weighted[:, :, None] * config_ext[:, None], axis=0) / total_fields
        local_div = divergence(stress)

        def draw_field(key):
            return gauss_noise(key, index)

        noise = jax.vmap(draw_field)(noise_keys[:, step])
        config = advance_config(config, config_ext, spring_ext, flow, slopes, noise)
        total_div = lax.psum(local_div, "row")
        start = flow + time_step * velocity_rate(flow_ext, total_div)
        flux = lax.psum(jnp.sum(start[0]), "gx")
        flow = adjust_flux(start, flux, cells)
    return (config, flow)


def solution(mesh):
    placed = (P("row", None, "gx", None, None), P(None, "gx", None, None), P("row", None))
    return jax.shard_map(
        shards,
        mesh=mesh,
        in_specs=placed,
        out_specs=(P("row", None, "gx", None, None), P(None, "gx", None, None)),
        check_vma=False,
    )
```

profile of v0, /device:TPU:1, one launch (start us, length us, event | category | flops | bytes accessed | tf_op | source)
XLA Modules:
  0.0 384.7 jit_solution(7158311933790168185)
XLA Ops:
  7.2 1.4 fusion.98
  8.8 1.2 fusion.100
  10.0 3.0 collective-permute-start.1
  13.0 0.2 collective-permute-start
  13.2 1.2 fusion.105
  14.4 1.2 fusion.106
  15.6 1.4 slice_bitcast_fusion.7
  17.1 3.1 fusion.96
  20.1 1.0 add_multiply_fusion
  21.2 0.9 multiply_bitcast_fusion.3
  22.1 1.6 copy.56
  23.7 3.0 fusion.97
  26.7 2.0 slice_bitcast_fusion.18
  28.6 2.0 slice_bitcast_fusion.19
  30.6 0.4 multiply_reduce_fusion.3
  31.1 0.2 maximum_divide_fusion.1
  31.3 0.9 broadcast_multiply_fusion.1
  32.1 0.1 copy-done.6
  32.3 1.1 multiply_reduce_fusion.1
  33.4 0.2 broadcast_multiply_fusion.2
  33.7 0.2 fusion.103
  33.9 0.2 fusion.104
  34.2 1.3 fusion.68
  35.6 0.9 slice_bitcast_fusion.14
  36.5 1.0 slice_bitcast_fusion.15
  37.6 1.2 fusion.80
  38.8 86.4 %all-reduce.11.cloned.1.call-done = f32[3,4,96,128]{3,2,1,0:T(8,128)} async-done(((f32[3,4,96,128]{3,2,1,0:T(8,128)}), f32[3,4,96,128]{3,2,1,0:T(8,128)}) %all-reduce.11.cloned.1.call-update) | async-done | bytes 589840 | tf_op jit(solution)/shard_map/psum | solution.py:146
  125.2 3.4 multiply_add_fusion.1
  128.6 0.6 slice_reduce_fusion.1
  129.3 58.5 %psum.29 = f32[]{:T(128)} all-reduce(f32[]{:T(128)} %slice_reduce_fusion.1), channel_id=1, replica_groups=mesh['gx'=32,'row'=8] {'gx'}, use_global_device_ids=true, to_apply=%region_4.5 | all-reduce | flops 1 | bytes 8 | tf_op jit(solution)/shard_map/psum | solution.py:148
  188.4 0.8 multiply_bitcast_fusion
  189.2 0.2 fusion.76
  189.5 0.2 fusion.75
  189.7 0.5 copy-done.5
  190.2 1.7 copy-done.4
  192.0 0.2 slice-done
  192.1 17.2 %fusion.9 = f32[4,3,4,96,128]{4,3,1,2,0:T(8,128)S(1)} fusion(f32[4,3,4,96,128]{4,3,1,2,0:T(8,128)S(1)} %copy-done.4, f32[4,3,1,96,128]{4,3,1,2,0:T(8,128)} %get-tuple-element.41, f32[4,3,1,96,128]{4,3,1,2,0:T(8,128)} %get-tuple-element.43, f32[4,3,4,96,1]{4,3,1,2,0:T(8,128)} %get-tuple-element.31, f32[4,3,4,96,127]{4,3,1,2,0:T(8,128)} %get-tuple-element.33, ...), kind=kLoop, calls=%fused_computation.32 | loop fusion | flops 31260672 | bytes 17301520 | tf_op jit(solution)/shard_map/add | solution.py:96
  209.4 3.0 fusion.93
  212.8 0.7 collective-permute-start.2
  213.5 1.2 broadcast_multiply_fusion.3
  214.8 1.5 slice_bitcast_fusion.4
  216.2 3.1 fusion.94
  219.3 4.8 %collective-permute-done.2 = f32[5,3,1,96,128]{4,3,1,2,0:T(8,128)S(1)} collective-permute-done((f32[5,3,1,96,128]{4,3,1,2,0:T(8,128)S(1)}, f32[5,3,1,96,128]{4,3,1,2,0:T(8,128)S(1)}, u32[]{:S(2)}, u32[]{:S(2)}) %collective-permute-start.2) | collective-permute-done | bytes 737312 | tf_op jit(solution)/shard_map/ppermute | solution.py:29
  224.1 0.8 copy-done.25
  225.0 0.9 copy-done.24
  225.9 0.4 multiply_reduce_fusion.2
  226.3 0.2 maximum_divide_fusion
  226.5 0.2 copy-done.2
  226.7 0.9 broadcast_multiply_fusion
  227.6 1.0 multiply_reduce_fusion
  228.7 0.2 copy_multiply_fusion
  229.0 0.2 fusion.101
  229.2 0.2 fusion.102
  229.5 1.3 fusion.74
  230.9 1.1 slice_bitcast_fusion.12
  232.0 1.0 slice_bitcast_fusion.13
  233.1 17.1 %fusion.19 = f32[4,3,4,96,128]{4,3,1,2,0:T(8,128)S(1)} fusion(f32[4,3,4,96,128]{4,3,1,2,0:T(8,128)S(1)} %fusion.9, f32[4,3,1,96,128]{4,3,1,2,0:T(8,128)S(1)} %copy-done.3, f32[4,3,1,96,128]{4,3,1,2,0:T(8,128)S(1)} %slice.495, f32[4,3,4,96,1]{4,3,1,2,0:T(8,128)} %get-tuple-element.20, f32[4,3,4,96,127]{4,3,1,2,0:T(8,128)} %get-tuple-element.22, ...), kind=kLoop, calls=%fused_computation.42 | loop fusion | flops 31555584 | bytes 17301520 | tf_op jit(solution)/shard_map/add | solution.py:96
  250.3 1.6 copy.72
  251.8 1.0 select_maximum_fusion
  252.9 61.8 %all-reduce.13.cloned.1.call-done = f32[3,4,96,128]{3,2,1,0:T(8,128)} async-done(((f32[3,4,96,128]{3,2,1,0:T(8,128)}), f32[3,4,96,128]{3,2,1,0:T(8,128)}) %all-reduce.13.cloned.1.call-update) | async-done | bytes 589840 | tf_op jit(solution)/shard_map/psum | solution.py:146
  314.7 2.4 multiply_add_fusion
  317.1 0.6 slice_reduce_fusion
  317.8 58.5 %psum.31 = f32[]{:T(128)} all-reduce(f32[]{:T(128)} %slice_reduce_fusion), channel_id=1, replica_groups=mesh['gx'=32,'row'=8] {'gx'}, use_global_device_ids=true, to_apply=%region_9.10 | all-reduce | flops 1 | bytes 8 | tf_op jit(solution)/shard_map/psum | solution.py:148
  377.0 0.9 pad_maximum_fusion.17
  (79 shorter events, 1.4 us)
Async XLA Ops:
  7.2 1.4 copy-start.1
  7.2 118.0 %all-reduce.11.cloned.1.call-start = ((), (), s32[]{:S(2)}) async-start(), calls=%async_computation | async-start | bytes 1179648 | tf_op jit(solution)/shard_map/psum | solution.py:146
  10.0 16.7 %collective-permute-start.1 = (f32[5,3,1,96,128]{4,3,1,2,0:T(8,128)}, f32[5,3,1,96,128]{4,3,1,2,0:T(8,128)}, u32[]{:S(2)}, u32[]{:S(2)}) collective-permute-start(f32[5,3,1,96,128]{4,3,1,2,0:T(8,128)} %get-tuple-element.39), channel_id=1, source_target_pairs={{0,8},{8,16},{16,24},{24,32},{32,40},{40,48},{48,56},{56,64},{64,7... | collective-permute-start | bytes 2211848 | tf_op jit(solution)/shard_map/ppermute | solution.py:27
  13.0 2.6 copy-start
  13.0 15.6 %collective-permute-start = (f32[5,3,1,96,128]{4,3,1,2,0:T(8,128)}, f32[5,3,1,96,128]{4,3,1,2,0:T(8,128)}, u32[]{:S(2)}, u32[]{:S(2)}) collective-permute-start(f32[5,3,1,96,128]{4,3,1,2,0:T(8,128)} %get-tuple-element.38), channel_id=1, source_target_pairs={{8,0},{16,8},{24,16},{32,24},{40,32},{48,40},{56,48},{64,56},{72,6... | collective-permute-start | bytes 2211848 | tf_op jit(solution)/shard_map/ppermute | solution.py:29
  20.1 1.9 copy-start.26
  21.2 168.5 %copy-start.8 = (s32[3,4,96,128]{3,2,0,1:T(8,128)}, s32[3,4,96,128]{3,2,0,1:T(8,128)S(1)}, u32[]{:S(2)}) copy-start(s32[3,4,96,128]{3,2,0,1:T(8,128)S(1)} %get-tuple-element.75) | copy-start | bytes 1769476
  31.2 1.0 copy-start.6
  35.5 279.2 %all-reduce.13.cloned.1.call-start = ((), (), s32[]{:S(2)}) async-start(), calls=%async_computation.1 | async-start | bytes 1179648 | tf_op jit(solution)/shard_map/psum | solution.py:146
  36.5 88.7 %copy-start.21 = (f32[4,96,128]{2,1,0:T(8,128)S(1)}, f32[4,96,128]{2,1,0:T(8,128)}, u32[]{:S(2)}) copy-start(f32[4,96,128]{2,1,0:T(8,128)} %get-tuple-element.62) | copy-start | bytes 589828
  36.5 88.7 %copy-start.23 = (f32[4,96,128]{2,1,0:T(8,128)S(1)}, f32[4,96,128]{2,1,0:T(8,128)}, u32[]{:S(2)}) copy-start(f32[4,96,128]{2,1,0:T(8,128)} %get-tuple-element.63) | copy-start | bytes 589828
  188.4 1.9 copy-start.5
  189.2 2.8 copy-start.4
  189.2 2.9 slice-start
  189.2 2.9 copy-start.22
  189.4 24.1 %copy-start.11 = (f32[3,4,96,1]{3,2,1,0:T(8,128)}, f32[3,4,96,1]{3,2,1,0:T(8,128)S(1)}, u32[]{:S(2)}) copy-start(f32[3,4,96,1]{3,2,1,0:T(8,128)S(1)} %get-tuple-element.54) | copy-start | bytes 13828
  189.5 24.1 %copy-start.13 = (f32[3,4,96,1]{3,2,1,0:T(8,128)}, f32[3,4,96,1]{3,2,1,0:T(8,128)S(1)}, u32[]{:S(2)}) copy-start(f32[3,4,96,1]{3,2,1,0:T(8,128)S(1)} %get-tuple-element.55) | copy-start | bytes 13828
  189.7 23.8 %copy-start.15 = (f32[3,4,96,127]{3,2,1,0:T(8,128)}, f32[3,4,96,127]{3,2,1,0:T(8,128)S(1)}, u32[]{:S(2)}) copy-start(f32[3,4,96,127]{3,2,1,0:T(8,128)S(1)} %get-tuple-element.52) | copy-start | bytes 1755652
  189.7 23.8 %copy-start.17 = (f32[3,4,96,127]{3,2,1,0:T(8,128)}, f32[3,4,96,127]{3,2,1,0:T(8,128)S(1)}, u32[]{:S(2)}) copy-start(f32[3,4,96,127]{3,2,1,0:T(8,128)S(1)} %get-tuple-element.53) | copy-start | bytes 1755652
  212.7 11.4 %collective-permute-start.3 = (f32[5,3,1,96,128]{4,3,1,2,0:T(8,128)S(1)}, f32[5,3,1,96,128]{4,3,1,2,0:T(8,128)S(1)}, u32[]{:S(2)}, u32[]{:S(2)}) collective-permute-start(f32[5,3,1,96,128]{4,3,1,2,0:T(8,128)S(1)} %get-tuple-element.37), channel_id=1, source_target_pairs={{0,8},{8,16},{16,24},{24,32},{32,40},{40,48},{48,56},{56,64},{64,7... | collective-permute-start | bytes 2211848 | tf_op jit(solution)/shard_map/ppermute | solution.py:27
  212.8 11.3 %collective-permute-start.2 = (f32[5,3,1,96,128]{4,3,1,2,0:T(8,128)S(1)}, f32[5,3,1,96,128]{4,3,1,2,0:T(8,128)S(1)}, u32[]{:S(2)}, u32[]{:S(2)}) collective-permute-start(f32[5,3,1,96,128]{4,3,1,2,0:T(8,128)S(1)} %get-tuple-element.36), channel_id=1, source_target_pairs={{8,0},{16,8},{24,16},{32,24},{40,32},{48,40},{56,48},{64,56},{72,6... | collective-permute-start | bytes 2211848 | tf_op jit(solution)/shard_map/ppermute | solution.py:29
  224.1 0.9 copy-start.25
  224.9 0.9 copy-start.24
  225.9 0.8 copy-start.2
  226.7 2.8 copy-start.7
  230.8 2.2 copy-start.3
  230.8 2.2 slice-start.1
  230.8 2.2 copy-start.9
  230.9 2.2 copy-start.10
  231.9 19.9 %copy-start.19 = (f32[3,1,96,128]{3,2,1,0:T(8,128)}, f32[3,1,96,128]{3,2,1,0:T(8,128)S(1)}, u32[]{:S(2)}) copy-start(f32[3,1,96,128]{3,2,1,0:T(8,128)S(1)} %slice_bitcast_fusion.12) | copy-start | bytes 442372
  232.9 18.9 %copy-start.20 = (f32[3,1,96,128]{3,2,1,0:T(8,128)}, f32[3,1,96,128]{3,2,1,0:T(8,128)S(1)}, u32[]{:S(2)}) copy-start(f32[3,1,96,128]{3,2,1,0:T(8,128)S(1)} %slice_bitcast_fusion.13) | copy-start | bytes 442372
  250.2 64.5 %copy-start.12 = (f32[3,4,96,1]{3,2,1,0:T(8,128)S(1)}, f32[3,4,96,1]{3,2,1,0:T(8,128)}, u32[]{:S(2)}) copy-start(f32[3,4,96,1]{3,2,1,0:T(8,128)} %copy-done.11) | copy-start | bytes 13828
  250.2 64.5 %copy-start.14 = (f32[3,4,96,1]{3,2,1,0:T(8,128)S(1)}, f32[3,4,96,1]{3,2,1,0:T(8,128)}, u32[]{:S(2)}) copy-start(f32[3,4,96,1]{3,2,1,0:T(8,128)} %copy-done.13) | copy-start | bytes 13828
  250.2 64.4 %copy-start.16 = (f32[3,4,96,127]{3,2,1,0:T(8,128)S(1)}, f32[3,4,96,127]{3,2,1,0:T(8,128)}, u32[]{:S(2)}) copy-start(f32[3,4,96,127]{3,2,1,0:T(8,128)} %copy-done.15) | copy-start | bytes 1755652
  250.3 64.4 %copy-start.18 = (f32[3,4,96,127]{3,2,1,0:T(8,128)S(1)}, f32[3,4,96,127]{3,2,1,0:T(8,128)}, u32[]{:S(2)}) copy-start(f32[3,4,96,127]{3,2,1,0:T(8,128)} %copy-done.17) | copy-start | bytes 1755652
Sparse Core Ops, SparseCore 0:
  35.6 89.5 all-reduce.10
  230.9 83.7 all-reduce.12
where the time goes:
time: 385 us
  waiting for transfers between devices  153 us (40%)
  blocking collectives  117 us (30%)
  other arithmetic  57.6 us (15%)
  local copies, waits for them, and re-layouts  37.1 us (10%)
  between operations  15.7 us (4%)
  starting transfers between devices  4.13 us (1%)
    psum x2, waiting for transfers between devices, shards(): total_div = lax.psum(local_div, 'row')  148 us
    psum x2, blocking collectives, shards(): flux = lax.psum(jnp.sum(start[0]), 'gx')  117 us
    add x2, other arithmetic, advance_config(): return field + time_step * drift + math.sqrt(time_step / relax_time) * noise  34.3 us
    slice x10, local copies, waits for them, and re-layouts, diff_z(): return 0.5 * (jnp.roll(field, -1, -1) - jnp.roll(field, 1, -1))  15.5 us
  transfers between devices with their start and end apart: 6, of which 3 were waited for; matrix products, arithmetic and copies ran while one was open for 12% of the time, Pallas kernels for 0%

commit v1 on v0

v1 whole, which is shorter than its diff:
```python
import functools
import math

import jax
import jax.numpy as jnp
from jax import lax
from jax.experimental import pallas as pl
from jax.experimental.pallas import tpu as pltpu
from jax.sharding import PartitionSpec as P

time_step = 0.05
viscosity = 0.5
stress_coef = 4.0
relax_time = 0.5
spring_limit = 10.0
spring_floor = 0.2
bulk_target = 1.0

SINE = (4.442882834149242, -7.308241154509167, 3.6062889576892747, -0.8457635932838079, 0.10920574854431932)
PAIRS = ((0, 0), (0, 1), (0, 2), (1, 1), (1, 2), (2, 2))
PLACE = ((0, 1, 2), (1, 3, 4), (2, 4, 5))
VMEM_LIMIT = 56 * 1024 * 1024
VMEM = pl.BlockSpec(memory_space=pltpu.VMEM)
SMEM = pl.BlockSpec(memory_space=pltpu.SMEM)


def params():
    return pltpu.CompilerParams(vmem_limit_bytes=VMEM_LIMIT)


def mix_bits(value):
    value = value ^ lax.shift_right_logical(value, jnp.int32(16))
    value = value * jnp.int32(73244475)
    value = value ^ lax.shift_right_logical(value, jnp.int32(16))
    value = value * jnp.int32(73244475)
    return value ^ lax.shift_right_logical(value, jnp.int32(16))


def noise_of(salted, even):
    mask = jnp.int32(16777215)
    first = mix_bits(even ^ salted)
    second = mix_bits(even ^ (salted ^ 1))
    upper = ((first & mask).astype(jnp.float32) + 0.5) * (1.0 / 16777216.0)
    turn = (second & mask).astype(jnp.float32) * (1.0 / 16777216.0) + (0.5 / 16777216.0 - 0.5)
    square = jnp.maximum(jnp.log(upper) * (-2.0 * time_step / relax_time), 1e-30)
    radius = square * lax.rsqrt(square)
    w = turn * turn
    q = jnp.float32(SINE[4])
    for coef in SINE[3::-1]:
        q = q * w + coef
    q = q * turn
    return radius * (q * q - 1.0)


def noise_kernel(step, total_x, keys_ref, out_ref):
    fields, _, width, rows, depth = out_ref.shape
    chunk = 32
    chunks = rows // chunk
    x_start = lax.axis_index("gx") * width
    salts = [mix_bits(keys_ref[k, step] + jnp.int32(40503)) for k in range(fields)]
    ypos = lax.broadcasted_iota(jnp.int32, (chunk, depth), 0)
    zpos = lax.broadcasted_iota(jnp.int32, (chunk, depth), 1)
    local = (ypos * depth + zpos) * 2

    def body(n, carry):
        comp = n // (width * chunks)
        rest = n - comp * (width * chunks)
        x = rest // chunks
        part = rest - x * chunks
        base = ((comp * total_x + x_start + x) * rows + part * chunk) * (2 * depth)
        even = local + base
        start = pl.multiple_of(part * chunk, chunk)
        for k in range(fields):
            out_ref[k, comp, x, pl.ds(start, chunk), :] = noise_of(salts[k], even)
        return carry

    lax.fori_loop(0, 3 * width * chunks, body, 0)


def draw_noise(keys, step, total_x, shape):
    return pl.pallas_call(
        functools.partial(noise_kernel, step, total_x),
        out_shape=jax.ShapeDtypeStruct(shape, jnp.float32),
        in_specs=[SMEM],
        out_specs=VMEM,
        compiler_params=params(),
        name="draw_noise",
    )(keys)


def up_z(f):
    return pltpu.roll(f, f.shape[-1] - 1, f.ndim - 1)


def down_z(f):
    return pltpu.roll(f, 1, f.ndim - 1)


def up_y(f):
    row = lax.broadcasted_iota(jnp.int32, f.shape, 0)
    return jnp.where(row == f.shape[0] - 1, 0.0, pltpu.roll(f, f.shape[0] - 1, 0))


def down_y(f):
    row = lax.broadcasted_iota(jnp.int32, f.shape, 0)
    return jnp.where(row == 0, 0.0, pltpu.roll(f, 1, 0))


def spring_of(q):
    length = q[0] * q[0] + q[1] * q[1] + q[2] * q[2]
    return 1.0 / jnp.maximum(1.0 - length * (1.0 / spring_limit), spring_floor)


def fill_stress(config_ref, stress_ref, total_fields):
    fields, _, width, rows, depth = config_ref.shape
    chunk = 32
    chunks = rows // chunk

    def body(n, carry):
        x = n // chunks
        start = pl.multiple_of((n - x * chunks) * chunk, chunk)
        totals = [None] * 6
        for k in range(fields):
            q = [config_ref[k, i, x, pl.ds(start, chunk), :] for i in range(3)]
            spring = spring_of(q) * (1.0 / total_fields)
            weighted = [spring * q[i] for i in range(3)]
            for p, (i, j) in enumerate(PAIRS):
                term = weighted[i] * q[j]
                totals[p] = term if k == 0 else totals[p] + term
        for p in range(6):
            stress_ref[p, x, pl.ds(start, chunk), :] = totals[p]
        return carry

    lax.fori_loop(0, width * chunks, body, 0)


def fill_divergence(stress_ref, div_ref, first_ref, last_ref):
    width = stress_ref.shape[1]
    for i in range(3):
        first_ref[i] = stress_ref[PLACE[i][0], 0]
        last_ref[i] = stress_ref[PLACE[i][0], width - 1]
        for x in range(width):
            sy = stress_ref[PLACE[i][1], x]
            sz = stress_ref[PLACE[i][2], x]
            total = up_y(sy) - down_y(sy) + up_z(sz) - down_z(sz)
            if x + 1 < width:
                total = total + stress_ref[PLACE[i][0], x + 1]
            if x > 0:
                total = total - stress_ref[PLACE[i][0], x - 1]
            div_ref[i, x] = 0.5 * total


def first_kernel(total_fields, config_ref, div_ref, first_ref, last_ref, stress_ref):
    fill_stress(config_ref, stress_ref, total_fields)
    fill_divergence(stress_ref, div_ref, first_ref, last_ref)


def first_stress(config, total_fields):
    _, _, width, rows, depth = config.shape
    end = jax.ShapeDtypeStruct((3, rows, depth), jnp.float32)
    return pl.pallas_call(
        functools.partial(first_kernel, total_fields),
        out_shape=[jax.ShapeDtypeStruct((3, width, rows, depth), jnp.float32), end, end],
        in_specs=[VMEM],
        out_specs=[VMEM] * 3,
        scratch_shapes=[pltpu.VMEM((6, width, rows, depth), jnp.float32)],
        compiler_params=params(),
        name="first_stress",
    )(config)


def advance_fields(config_ref, before_ref, after_ref, flow_ref, fbefore, fafter, noise_ref, new_ref, flow_at, slope_ref):
    fields, _, width, rows, depth = config_ref.shape
    half = 0.5 * time_step
    for x in range(width):
        for i in range(3):
            here = flow_at(i, x)
            below = flow_at(i, x - 1) if x > 0 else fbefore(i)
            above = flow_at(i, x + 1) if x + 1 < width else fafter(i)
            slope_ref[3 * i] = half * (above - below)
            slope_ref[3 * i + 1] = half * (up_y(here) - down_y(here))
            slope_ref[3 * i + 2] = half * (up_z(here) - down_z(here))
            slope_ref[9 + i] = half * here

        def body(k, carry, x=x):
            q = [config_ref[k, i, x] for i in range(3)]
            keep = 1.0 - (time_step / (2.0 * relax_time)) * spring_of(q)
            for i in range(3):
                below = config_ref[k, i, x - 1] if x > 0 else before_ref[k, i]
                above = config_ref[k, i, x + 1] if x + 1 < width else after_ref[k, i]
                along = slope_ref[9] * (above - below)
                along = along + slope_ref[10] * (up_y(q[i]) - down_y(q[i]))
                along = along + slope_ref[11] * (up_z(q[i]) - down_z(q[i]))
                stretch = slope_ref[3 * i] * q[0] + slope_ref[3 * i + 1] * q[1] + slope_ref[3 * i + 2] * q[2]
                new_ref[k, i, x] = q[i] * keep + (stretch - along) + noise_ref[k, i, x]
            return carry

        lax.fori_loop(0, fields, body, 0)


def second_kernel(
    total_fields, config_ref, before_ref, after_ref, flow_ref, fbefore_ref, fafter_ref, noise_ref,
    new_ref, div_ref, first_ref, last_ref, wall_ref, slope_ref, stress_ref,
):
    advance_fields(
        config_ref, before_ref, after_ref, flow_ref,
        lambda i: fbefore_ref[i], lambda i: fafter_ref[i], noise_ref, new_ref,
        lambda i, x: flow_ref[i, x], slope_ref,
    )
    fill_stress(new_ref, stress_ref, total_fields)
    fill_divergence(stress_ref, div_ref, first_ref, last_ref)
    width, rows, depth = stress_ref.shape[1:]
    wall = jnp.zeros((1, depth), jnp.float32)
    for x in range(width):
        wall = wall + (stress_ref[1, x, rows - 1:rows, :] - stress_ref[1, x, 0:1, :])
    wall_ref[...] = jnp.broadcast_to(0.5 * wall, (8, depth))


def second_fields(config, before, after, flow, fbefore, fafter, noise, total_fields):
    _, _, width, rows, depth = config.shape
    end = jax.ShapeDtypeStruct((3, rows, depth), jnp.float32)
    return pl.pallas_call(
        functools.partial(second_kernel, total_fields),
        out_shape=[
            jax.ShapeDtypeStruct(config.shape, jnp.float32),
            jax.ShapeDtypeStruct((3, width, rows, depth), jnp.float32),
            end,
            end,
            jax.ShapeDtypeStruct((8, depth), jnp.float32),
        ],
        in_specs=[VMEM] * 7,
        out_specs=[VMEM] * 5,
        scratch_shapes=[
            pltpu.VMEM((12, rows, depth), jnp.float32),
            pltpu.VMEM((6, width, rows, depth), jnp.float32),
        ],
        compiler_params=params(),
        name="second_fields",
    )(config, before, after, flow, fbefore, fafter, noise)


def flow_step(at, div_at, width, write):
    half = 0.5 * time_step
    for x in range(width):
        adv = [half * at(j, x) for j in range(3)]
        for i in range(3):
            here = at(i, x)
            below, above = at(i, x - 1), at(i, x + 1)
            left, right = down_y(here), up_y(here)
            back, front = down_z(here), up_z(here)
            along = adv[0] * (above - below) + adv[1] * (right - left) + adv[2] * (front - back)
            lap = (above + below) + (right + left) + (front + back) - 6.0 * here
            write(i, x, here - along + (time_step * viscosity) * lap + (time_step * stress_coef) * div_at(i, x))


def third_kernel(flow_ref, fbefore_ref, fafter_ref, div_ref, start_ref, first_ref, last_ref, sums_ref):
    _, width, rows, depth = flow_ref.shape

    def at(i, x):
        if x < 0:
            return fbefore_ref[i]
        if x >= width:
            return fafter_ref[i]
        return flow_ref[i, x]

    def write(i, x, value):
        start_ref[i, x] = value

    flow_step(at, lambda i, x: div_ref[i, x], width, write)
    total = jnp.zeros((8, depth), jnp.float32)
    bend = jnp.zeros((8, depth), jnp.float32)
    edge = jnp.zeros((1, depth), jnp.float32)
    gain = jnp.zeros((1, depth), jnp.float32)
    for x in range(width):
        s, v, w = start_ref[0, x], start_ref[1, x], start_ref[2, x]
        term = v * (0.5 * (up_y(s) - down_y(s))) + w * (0.5 * (up_z(s) - down_z(s)))
        for r in range(rows // 8):
            total = total + s[8 * r:8 * r + 8]
            bend = bend + term[8 * r:8 * r + 8]
        edge = edge + (s[0:1] + s[rows - 1:rows])
        gain = gain + (v[0:1] - v[rows - 1:rows])
    sums_ref[0:1] = jnp.sum(total, axis=0, keepdims=True)
    sums_ref[1:2] = jnp.sum(bend, axis=0, keepdims=True) + viscosity * edge
    sums_ref[2:3] = 0.5 * gain
    sums_ref[3:8] = jnp.zeros((5, depth), jnp.float32)
    for i in range(3):
        first_ref[i] = start_ref[i, 0]
        last_ref[i] = start_ref[i, width - 1]


def third_flow(flow, fbefore, fafter, div):
    _, width, rows, depth = flow.shape
    end = jax.ShapeDtypeStruct((3, rows, depth), jnp.float32)
    return pl.pallas_call(
        third_kernel,
        out_shape=[jax.ShapeDtypeStruct(flow.shape, jnp.float32), end, end, jax.ShapeDtypeStruct((8, depth), jnp.float32)],
        in_specs=[VMEM] * 4,
        out_specs=[VMEM] * 4,
        compiler_params=params(),
        name="third_flow",
    )(flow, fbefore, fafter, div)


def fourth_kernel(config_ref, before_ref, after_ref, start_ref, sbefore_ref, safter_ref, noise_ref, lift_ref, new_ref, slope_ref):
    lift = lift_ref[0]

    def flow_at(i, x):
        return start_ref[i, x] + lift if i == 0 else start_ref[i, x]

    advance_fields(
        config_ref, before_ref, after_ref, start_ref,
        lambda i: sbefore_ref[i] + lift if i == 0 else sbefore_ref[i],
        lambda i: safter_ref[i] + lift if i == 0 else safter_ref[i],
        noise_ref, new_ref, flow_at, slope_ref,
    )


def fourth_fields(config, before, after, start, sbefore, safter, noise, lift):
    rows, depth = config.shape[3:]
    return pl.pallas_call(
        fourth_kernel,
        out_shape=jax.ShapeDtypeStruct(config.shape, jnp.float32),
        in_specs=[VMEM] * 7 + [SMEM],
        out_specs=VMEM,
        scratch_shapes=[pltpu.VMEM((12, rows, depth), jnp.float32)],
        compiler_params=params(),
        name="fourth_fields",
    )(config, before, after, start, sbefore, safter, noise, lift)


def fifth_kernel(start_ref, sbefore_ref, safter_ref, div_ref, lift_ref, out_ref):
    width = start_ref.shape[1]
    lift = lift_ref[0]
    last_lift = lift_ref[1]

    def at(i, x):
        if x < 0:
            value = sbefore_ref[i]
        elif x >= width:
            value = safter_ref[i]
        else:
            value = start_ref[i, x]
        return value + lift if i == 0 else value

    def write(i, x, value):
        out_ref[i, x] = value + last_lift if i == 0 else value

    flow_step(at, lambda i, x: div_ref[i, x], width, write)


def fifth_flow(start, sbefore, safter, div, lift):
    return pl.pallas_call(
        fifth_kernel,
        out_shape=jax.ShapeDtypeStruct(start.shape, jnp.float32),
        in_specs=[VMEM] * 4 + [SMEM],
        out_specs=VMEM,
        compiler_params=params(),
        name="fifth_flow",
    )(start, sbefore, safter, div, lift)


def from_left(value):
    count = lax.axis_size("gx")
    return lax.ppermute(value, "gx", [(i, (i + 1) % count) for i in range(count)])


def from_right(value):
    count = lax.axis_size("gx")
    return lax.ppermute(value, "gx", [((i + 1) % count, i) for i in range(count)])


def row_sum(value):
    count = lax.axis_size("row")
    bit = 1
    while bit < count:
        value = value + lax.ppermute(value, "row", [(i, i ^ bit) for i in range(count)])
        bit *= 2
    return value


def with_ends(div, before, after):
    first = div[:, :1] - 0.5 * before[:, None]
    last = div[:, -1:] + 0.5 * after[:, None]
    return jnp.concatenate([first, div[:, 1:-1], last], axis=1)


def shards(config, flow, keys):
    fields, _, width, rows, depth = config.shape
    total_fields = fields * lax.axis_size("row")
    slabs = lax.axis_size("gx")
    total_x = width * slabs
    cells = total_x * rows * depth

    div, first, last = first_stress(config, total_fields)
    ends = from_left(last), from_right(first)
    head = jnp.concatenate([config[:, :, 0], flow[None, :, 0]], axis=0)
    tail = jnp.concatenate([config[:, :, -1], flow[None, :, -1]], axis=0)
    left, right = from_left(tail), from_right(head)
    noise = draw_noise(keys, 0, total_x, config.shape)
    later = draw_noise(keys, 1, total_x, config.shape)
    div = row_sum(with_ends(div, *ends))

    fleft, fright = left[fields], right[fields]
    config, next_div, first, last, wall = second_fields(
        config, left[:fields], right[:fields], flow, fleft, fright, noise, total_fields
    )
    ends = from_left(last), from_right(first)
    left, right = from_left(config[:, :, -1]), from_right(config[:, :, 0])
    next_div = row_sum(with_ends(next_div, *ends))
    wall = row_sum(wall)

    start, first, last, sums = third_flow(flow, fleft, fright, div)
    sleft, sright = from_left(last), from_right(first)
    mine = jnp.concatenate([sums[:3], wall[:1], sums[3:7]], axis=0)
    shared = lax.all_to_all(jnp.broadcast_to(mine[None], (slabs, 8, depth)), "gx", 0, 0)
    sums = jnp.sum(shared, axis=(0, 2))
    lift = bulk_target - sums[0] / cells
    change = time_step * (stress_coef * sums[3] - sums[1] - lift * (sums[2] + 2.0 * viscosity * total_x * depth))
    lifts = jnp.stack([lift, -change / cells])

    config = fourth_fields(config, left, right, start, sleft, sright, later, lifts)
    flow = fifth_flow(start, sleft, sright, next_div, lifts)
    return config, flow


def solution(mesh):
    placed = (P("row", None, "gx", None, None), P(None, "gx", None, None), P("row", None))
    return jax.shard_map(
        shards,
        mesh=mesh,
        in_specs=placed,
        out_specs=(P("row", None, "gx", None, None), P(None, "gx", None, None)),
        check_vma=False,
    )
```

time: 385 us -> 145 us (0.38)
  blocking collectives: 117 us -> 0 us
  waiting for transfers between devices: 153 us -> 37.4 us
  other arithmetic: 57.6 us -> 6.83 us
  starting transfers between devices: 4.13 us -> 44.4 us
  Pallas kernels: 0 us -> 39.3 us
  local copies, waits for them, and re-layouts: 37.1 us -> 10.9 us
  between operations: 15.7 us -> 3.44 us
    psum x2 -> x0, waiting for transfers between devices: 148 us -> none  [shards(): total_div = lax.psum(local_div, 'row')]
    psum x2 -> x0, blocking collectives: 117 us -> none  [shards(): flux = lax.psum(jnp.sum(start[0]), 'gx')]
    add x8 -> x10, other arithmetic: 42.7 us -> 3.13 us  [the longest x9 3.11 us: row_sum(): value + lax.ppermute(value, 'row', [(i, i ^ bit) for i in range(count)])]
    pallas_call x0 -> x7, Pallas kernels: none -> 39.3 us  [the longest x2 13.9 us: draw_noise(): pl.pallas_call(functools.partial(noise_kernel, step, total_x), out_shape=...]
    ppermute x4 -> x19, waiting for transfers between devices: 4.77 us -> 37 us  [the longest x9 33.8 us: row_sum(): lax.ppermute(value, 'row', [(i, i ^ bit) for i in range(count)])]
    ppermute x4 -> x19, starting transfers between devices: 4.05 us -> 33.1 us  [the longest x5 14.8 us: from_left(): lax.ppermute(value, 'gx', [(i, (i + 1) % count) for i in range(count)])]
    slice x24 -> x8, local copies, waits for them, and re-layouts: 22.5 us -> 5.7 us  [the longest x2 1.96 us: with_ends(): return jnp.concatenate([first, div[:, 1:-1], last], axis=1)]
    all_to_all x0 -> x1, starting transfers between devices: none -> 11.4 us  [shards(): lax.all_to_all(jnp.broadcast_to(mine[None], (slabs, 8, depth)), 'gx', 0, 0)]
  transfers between devices with their start and end apart: 6 -> 20, of which waited for: 3 -> 7; matrix products, arithmetic and copies ran while one was open for 12% -> 10% of each run, Pallas kernels for 0% -> 26%
where the time goes in v1:
time: 145 us; the launch traced here: 142 us
  starting transfers between devices  44.4 us (31%)
  Pallas kernels  39.3 us (27%)
  waiting for transfers between devices  37.4 us (26%)
  local copies, waits for them, and re-layouts  10.9 us (8%)
  other arithmetic  6.83 us (5%)
  between operations  3.44 us (2%)
    ppermute x9, waiting for transfers between devices, row_sum(): lax.ppermute(value, 'row', [(i, i ^ bit) for i in range(count)])  33.8 us
    ppermute x5, starting transfers between devices, from_left(): lax.ppermute(value, 'gx', [(i, (i + 1) % count) for i in range(count)])  14.8 us
    pallas_call x2, Pallas kernels, draw_noise(): pl.pallas_call(functools.partial(noise_kernel, step, total_x), out_shape=...  13.9 us
    ppermute x9, starting transfers between devices, row_sum(): lax.ppermute(value, 'row', [(i, i ^ bit) for i in range(count)])  11.6 us
    all_to_all x1, starting transfers between devices, shards(): lax.all_to_all(jnp.broadcast_to(mine[None], (slabs, 8, depth)), 'gx', 0, 0)  11.4 us
    pallas_call x1, Pallas kernels, second_fields(): pl.pallas_call(functools.partial(second_kernel, total_fields), out_shape=...  8.58 us
    pallas_call x1, Pallas kernels, fourth_fields(): pl.pallas_call(fourth_kernel, out_shape=jax.ShapeDtypeStruct(config.shape...  7.46 us
    ppermute x5, starting transfers between devices, from_right(): lax.ppermute(value, 'gx', [((i + 1) % count, i) for i in range(count)])  6.67 us
  transfers between devices with their start and end apart: 20, of which 7 were waited for; matrix products, arithmetic and copies ran while one was open for 10% of the time, Pallas kernels for 26%

profile of v1, /device:TPU:1, one launch (start us, length us, event | category | flops | bytes accessed | tf_op | source)
XLA Modules:
  0.0 142.3 jit_solution(10544821738184387644)
XLA Ops:
  0.6 0.0 copy-start.1
  0.6 1.4 slice_bitcast_fusion.2
  2.0 0.0 copy-done.1
  2.1 0.1 pad_maximum_fusion
  2.1 3.1 %collective-permute-start = (f32[5,3,96,128]{3,2,1,0:T(8,128)S(1)}, f32[5,3,96,128]{3,2,1,0:T(8,128)S(1)}, u32[]{:S(2)}, u32[]{:S(2)}) collective-permute-start(f32[5,3,96,128]{3,2,1,0:T(8,128)S(1)} %pad_maximum_fusion), channel_id=1, source_target_pairs={{0,8},{8,16},{16,24},{24,32},{32,40},{40,48},{48,56},{56,64},{64,7... | collective-permute-start | bytes 2211848 | tf_op jit(solution)/shard_map/ppermute | solution.py:364
  5.3 0.0 copy-start.6
  5.3 0.3 collective-permute-start.1
  5.6 3.8 %first_stress.1 = (f32[3,4,96,128]{3,2,1,0:T(8,128)}, f32[3,96,128]{2,1,0:T(8,128)}, f32[3,96,128]{2,1,0:T(8,128)}) custom-call(f32[4,3,4,96,128]{4,3,2,1,0:T(8,128)} %config_ref.3), custom_call_target="tpu_custom_call" | custom-call | tf_op jit(solution)/shard_map/first_stress/pallas_call | solution.py:161
  9.4 1.5 %collective-permute-start.4 = (f32[3,96,128]{2,1,0:T(8,128)}, f32[3,96,128]{2,1,0:T(8,128)S(1)}, u32[]{:S(2)}, u32[]{:S(2)}) collective-permute-start(f32[3,96,128]{2,1,0:T(8,128)} %get-tuple-element.16), channel_id=1, source_target_pairs={{0,8},{8,16},{16,24},{24,32},{32,40},{40,48},{48,56},{56,64},{64,7... | collective-permute-start | bytes 442376 | tf_op jit(solution)/shard_map/ppermute | solution.py:364
  10.9 3.1 %collective-permute-start.5 = (f32[3,96,128]{2,1,0:T(8,128)}, f32[3,96,128]{2,1,0:T(8,128)S(1)}, u32[]{:S(2)}, u32[]{:S(2)}) collective-permute-start(f32[3,96,128]{2,1,0:T(8,128)} %get-tuple-element.17), channel_id=1, source_target_pairs={{8,0},{16,8},{24,16},{32,24},{40,32},{48,40},{56,48},{64,56},{72,6... | collective-permute-start | bytes 442376 | tf_op jit(solution)/shard_map/ppermute | solution.py:369
  14.0 1.0 slice.80
  14.9 0.4 collective-permute-done.4
  15.3 2.8 %collective-permute-done.5 = f32[3,96,128]{2,1,0:T(8,128)S(1)} collective-permute-done((f32[3,96,128]{2,1,0:T(8,128)}, f32[3,96,128]{2,1,0:T(8,128)S(1)}, u32[]{:S(2)}, u32[]{:S(2)}) %collective-permute-start.5) | collective-permute-done | bytes 147488 | tf_op jit(solution)/shard_map/ppermute | solution.py:369
  18.1 1.0 fusion.2
  19.2 0.9 pad_maximum_fusion.2
  20.0 1.2 collective-permute-start.6
  21.2 0.7 copy.23.keys_ref
  21.9 6.9 %draw_noise.2.noise_ref = f32[4,3,4,96,128]{4,3,2,1,0:T(8,128)} custom-call(s32[4,2]{1,0:T(4,128)} %copy.23.keys_ref), custom_call_target="tpu_custom_call" | custom-call | tf_op jit(solution)/shard_map/draw_noise/pallas_call | solution.py:81
  28.9 0.0 collective-permute-done
  28.9 0.9 slice.92.before_ref
  29.7 0.0 collective-permute-done.1
  29.7 0.8 slice.93.after_ref
  30.6 0.7 slice_bitcast_fusion.4.fafter_ref
  31.2 0.7 slice_bitcast_fusion.5.fbefore_ref
  31.9 8.6 %second_fields.1 = (f32[4,3,4,96,128]{4,3,2,1,0:T(8,128)}, f32[3,4,96,128]{3,2,1,0:T(8,128)}, f32[3,96,128]{2,1,0:T(8,128)}, f32[3,96,128]{2,1,0:T(8,128)}, f32[8,128]{1,0:T(8,128)}) custom-call(f32[4,3,4,96,128]{4,3,2,1,0:T(8,128)} %config_ref.3, f32[4,3,96,128]{3,2,1,0:T(8,128)} %slice.92.before_ref, f32[4,3,96,128]{3,2,1,0:T(8,128)} %slice.93.after_ref, ...), custom_call_target="tpu_custom_call" | custom-call | tf_op jit(solution)/shard_map/second_fields/pallas_call | solution.py:222
  40.5 3.0 %collective-permute-start.15 = (f32[3,96,128]{2,1,0:T(8,128)}, f32[3,96,128]{2,1,0:T(8,128)S(1)}, u32[]{:S(2)}, u32[]{:S(2)}) collective-permute-start(f32[3,96,128]{2,1,0:T(8,128)} %get-tuple-element.25), channel_id=1, source_target_pairs={{8,0},{16,8},{24,16},{32,24},{40,32},{48,40},{56,48},{64,56},{72,6... | collective-permute-start | bytes 442376 | tf_op jit(solution)/shard_map/ppermute | solution.py:369
  43.5 1.0 slice.90
  44.5 1.1 fusion.4
  45.6 2.5 %collective-permute-start.7 = (f32[3,4,96,128]{3,2,1,0:T(8,128)S(1)}, f32[3,4,96,128]{3,2,1,0:T(8,128)S(1)}, u32[]{:S(2)}, u32[]{:S(2)}) collective-permute-start(f32[3,4,96,128]{3,2,1,0:T(8,128)S(1)} %fusion.4), channel_id=1, source_target_pairs={{0,2},{1,3},{2,0},{3,1},{4,6},{5,7},{6,4},{7,5},{8,10},{9,11},{10,... | collective-permute-start | bytes 1769480 | tf_op jit(solution)/shard_map/ppermute | solution.py:376
  48.2 0.0 collective-permute-done.14
  48.3 0.3 collective-permute-start.16
  48.6 9.8 %collective-permute-done.7 = f32[3,4,96,128]{3,2,1,0:T(8,128)S(1)} collective-permute-done((f32[3,4,96,128]{3,2,1,0:T(8,128)S(1)}, f32[3,4,96,128]{3,2,1,0:T(8,128)S(1)}, u32[]{:S(2)}, u32[]{:S(2)}) %collective-permute-start.7) | collective-permute-done | bytes 589856 | tf_op jit(solution)/shard_map/ppermute | solution.py:376
  58.4 0.1 add.39
  58.5 2.7 %collective-permute-start.8 = (f32[3,4,96,128]{3,2,1,0:T(8,128)S(1)}, f32[3,4,96,128]{3,2,1,0:T(8,128)S(1)}, u32[]{:S(2)}, u32[]{:S(2)}) collective-permute-start(f32[3,4,96,128]{3,2,1,0:T(8,128)S(1)} %add.39), channel_id=1, source_target_pairs={{0,4},{1,5},{2,6},{3,7},{4,0},{5,1},{6,2},{7,3},{8,12},{9,13},{10,... | collective-permute-start | bytes 1769480 | tf_op jit(solution)/shard_map/ppermute | solution.py:376
  61.2 9.3 %collective-permute-done.16 = f32[3,4,96,128]{3,2,1,0:T(8,128)S(1)} collective-permute-done((f32[3,4,96,128]{3,2,1,0:T(8,128)S(1)}, f32[3,4,96,128]{3,2,1,0:T(8,128)S(1)}, u32[]{:S(2)}, u32[]{:S(2)}) %collective-permute-start.16) | collective-permute-done | bytes 589856 | tf_op jit(solution)/shard_map/ppermute | solution.py:376
  70.5 0.1 fusion.3
  70.5 1.5 %collective-permute-start.17 = (f32[3,4,96,128]{3,2,1,0:T(8,128)S(1)}, f32[3,4,96,128]{3,2,1,0:T(8,128)S(1)}, u32[]{:S(2)}, u32[]{:S(2)}) collective-permute-start(f32[3,4,96,128]{3,2,1,0:T(8,128)S(1)} %fusion.3), channel_id=1, source_target_pairs={{0,2},{1,3},{2,0},{3,1},{4,6},{5,7},{6,4},{7,5},{8,10},{9,11},{10,... | collective-permute-start | bytes 1769480 | tf_op jit(solution)/shard_map/ppermute | solution.py:376
  72.1 0.2 collective-permute-start.11
  72.3 10.7 %collective-permute-done.11 = f32[8,128]{1,0:T(8,128)S(1)} collective-permute-done((f32[8,128]{1,0:T(8,128)S(1)}, f32[8,128]{1,0:T(8,128)S(1)}, u32[]{:S(2)}, u32[]{:S(2)}) %collective-permute-start.11) | collective-permute-done | bytes 4128 | tf_op jit(solution)/shard_map/ppermute | solution.py:376
  83.0 0.4 collective-permute-start.12
  83.3 4.0 %collective-permute-done.12 = f32[8,128]{1,0:T(8,128)S(1)} collective-permute-done((f32[8,128]{1,0:T(8,128)S(1)}, f32[8,128]{1,0:T(8,128)S(1)}, u32[]{:S(2)}, u32[]{:S(2)}) %collective-permute-start.12) | collective-permute-done | bytes 4128 | tf_op jit(solution)/shard_map/ppermute | solution.py:376
  87.3 2.6 %collective-permute-start.13 = (f32[8,128]{1,0:T(8,128)S(1)}, f32[8,128]{1,0:T(8,128)S(1)}, u32[]{:S(2)}, u32[]{:S(2)}) collective-permute-start(f32[8,128]{1,0:T(8,128)S(1)} %add.42), channel_id=1, source_target_pairs={{0,4},{1,5},{2,6},{3,7},{4,0},{5,1},{6,2},{7,3},{8,12},{9,13},{10,... | collective-permute-start | bytes 12296 | tf_op jit(solution)/shard_map/ppermute | solution.py:376
  90.0 0.1 slice_bitcast_fusion
  90.1 8.7 %collective-permute-start.2 = (f32[4,3,96,128]{3,2,1,0:T(8,128)S(1)}, f32[4,3,96,128]{3,2,1,0:T(8,128)S(1)}, u32[]{:S(2)}, u32[]{:S(2)}) collective-permute-start(f32[4,3,96,128]{3,2,1,0:T(8,128)S(1)} %get-tuple-element.27), channel_id=1, source_target_pairs={{0,8},{8,16},{16,24},{24,32},{32,40},{40,48},{48,56},{56,64},{64,7... | collective-permute-start | bytes 1769480 | tf_op jit(solution)/shard_map/ppermute | solution.py:364
  98.8 0.9 add.40.div_ref
  99.7 2.8 %third_flow.1 = (f32[3,4,96,128]{3,2,1,0:T(8,128)}, f32[3,96,128]{2,1,0:T(8,128)}, f32[3,96,128]{2,1,0:T(8,128)}, f32[8,128]{1,0:T(8,128)}) custom-call(f32[3,4,96,128]{3,2,1,0:T(8,128)} %flow_ref.3, f32[3,96,128]{2,1,0:T(8,128)} %slice_bitcast_fusion.5.fbefore_ref, f32[3,96,128]{2,1,0:T(8,128)} %slice_bitcast_fusion.4.fafter_ref, f32[3,4,96,128]{3,2,1,0:T(8,128)} %add.40.div_ref), custom_call_target="tpu_custom_call" | custom-call | tf_op jit(solution)/shard_map/third_flow/pallas_call | solution.py:294
  102.5 0.7 slice.82
  103.2 0.7 slice.84
  103.9 0.1 add.47
  103.9 0.1 collective-permute-start.18
  104.1 0.7 broadcast_in_dim.2
  104.7 11.4 %all-to-all-start = ((f32[32,8,128]{2,1,0:T(8,128)}), f32[32,8,128]{2,1,0:T(8,128)}, u32[]{:S(2)}, u32[]{:S(2)}) async-start(f32[32,8,128]{2,1,0:T(8,128)} %broadcast_in_dim.2), calls=%async_computation | async-start | bytes 262144 | tf_op jit(solution)/shard_map/all_to_all | solution.py:415
  116.1 7.0 %draw_noise.3.noise_ref = f32[4,3,4,96,128]{4,3,2,1,0:T(8,128)} custom-call(s32[4,2]{1,0:T(4,128)} %copy.23.keys_ref), custom_call_target="tpu_custom_call" | custom-call | tf_op jit(solution)/shard_map/draw_noise/pallas_call | solution.py:81
  123.1 0.3 collective-permute-start.10
  123.4 1.4 %collective-permute-start.9 = (f32[3,96,128]{2,1,0:T(8,128)}, f32[3,96,128]{2,1,0:T(8,128)}, u32[]{:S(2)}, u32[]{:S(2)}) collective-permute-start(f32[3,96,128]{2,1,0:T(8,128)} %get-tuple-element.19), channel_id=1, source_target_pairs={{0,8},{8,16},{16,24},{24,32},{32,40},{40,48},{48,56},{56,64},{64,7... | collective-permute-start | bytes 442376 | tf_op jit(solution)/shard_map/ppermute | solution.py:364
  124.8 0.4 all-to-all-done
  125.2 1.1 reduce_sum.9
  126.3 0.7 fusion.5
  129.6 0.6 pad_maximum_fusion.5.lift_ref
  130.2 0.8 copy-done.2
  131.0 0.2 copy-done.3
  131.2 7.5 %fourth_fields.1 = f32[4,3,4,96,128]{4,3,2,1,0:T(8,128)} custom-call(f32[4,3,4,96,128]{4,3,2,1,0:T(8,128)} %get-tuple-element.14.config_ref, f32[4,3,96,128]{3,2,1,0:T(8,128)} %copy-done.2, f32[4,3,96,128]{3,2,1,0:T(8,128)} %copy-done.3, f32[3,4,96,128]{3,2,1,0:T(8,128)} %get-tuple-element.18.start_ref, f32[3,96,128]{2,1,0:T(8,128)} %collective-permute-done.9.sbefore_ref, ...), custom_call_target="tpu_custom_call" | custom-call | tf_op jit(solution)/shard_map/fourth_fields/pallas_call | solution.py:320
  138.6 0.9 add.48.div_ref
  139.5 2.8 %fifth_flow.1 = f32[3,4,96,128]{3,2,1,0:T(8,128)} custom-call(f32[3,4,96,128]{3,2,1,0:T(8,128)} %get-tuple-element.18.start_ref, f32[3,96,128]{2,1,0:T(8,128)} %collective-permute-done.9.sbefore_ref, f32[3,96,128]{2,1,0:T(8,128)} %collective-permute-done.10.safter_ref, f32[3,4,96,128]{3,2,1,0:T(8,128)} %add.48.div_ref, f32[2]{0:T(128)} %pad_maximum_fusion.5.lift_ref), custom_call_target="tpu_custom_call" | custom-call | tf_op jit(solution)/shard_map/fifth_flow/pallas_call | solution.py:352
  (31 shorter events, 0.2 us)
Async XLA Ops:
  0.6 1.4 %copy-start.1 = (f32[3,4,96,128]{3,2,1,0:T(8,128)S(1)}, f32[3,4,96,128]{3,2,1,0:T(8,128)}, u32[]{:S(2)}) copy-start(f32[3,4,96,128]{3,2,1,0:T(8,128)} %flow_ref.3) | copy-start | bytes 1769476
  2.1 26.7 %collective-permute-start = (f32[5,3,96,128]{3,2,1,0:T(8,128)S(1)}, f32[5,3,96,128]{3,2,1,0:T(8,128)S(1)}, u32[]{:S(2)}, u32[]{:S(2)}) collective-permute-start(f32[5,3,96,128]{3,2,1,0:T(8,128)S(1)} %pad_maximum_fusion), channel_id=1, source_target_pairs={{0,8},{8,16},{16,24},{24,32},{32,40},{40,48},{48,56},{56,64},{64,7... | collective-permute-start | bytes 2211848 | tf_op jit(solution)/shard_map/ppermute | solution.py:364
  5.3 16.0 %copy-start.6 = (s32[4,2]{0,1:T(2,128)S(1)}, s32[4,2]{0,1:T(2,128)}, u32[]{:S(2)}) copy-start(s32[4,2]{0,1:T(2,128)} %param.5) | copy-start | bytes 100
  5.3 24.4 %collective-permute-start.1 = (f32[5,3,96,128]{3,2,1,0:T(8,128)S(1)}, f32[5,3,96,128]{3,2,1,0:T(8,128)S(1)}, u32[]{:S(2)}, u32[]{:S(2)}) collective-permute-start(f32[5,3,96,128]{3,2,1,0:T(8,128)S(1)} %pad_maximum_fusion.1), channel_id=1, source_target_pairs={{8,0},{16,8},{24,16},{32,24},{40,32},{48,40},{56,48},{64,56},{72,6... | collective-permute-start | bytes 2211848 | tf_op jit(solution)/shard_map/ppermute | solution.py:369
  9.4 6.0 %collective-permute-start.4 = (f32[3,96,128]{2,1,0:T(8,128)}, f32[3,96,128]{2,1,0:T(8,128)S(1)}, u32[]{:S(2)}, u32[]{:S(2)}) collective-permute-start(f32[3,96,128]{2,1,0:T(8,128)} %get-tuple-element.16), channel_id=1, source_target_pairs={{0,8},{8,16},{16,24},{24,32},{32,40},{40,48},{48,56},{56,64},{64,7... | collective-permute-start | bytes 442376 | tf_op jit(solution)/shard_map/ppermute | solution.py:364
  10.9 7.3 %collective-permute-start.5 = (f32[3,96,128]{2,1,0:T(8,128)}, f32[3,96,128]{2,1,0:T(8,128)S(1)}, u32[]{:S(2)}, u32[]{:S(2)}) collective-permute-start(f32[3,96,128]{2,1,0:T(8,128)} %get-tuple-element.17), channel_id=1, source_target_pairs={{8,0},{16,8},{24,16},{32,24},{40,32},{48,40},{56,48},{64,56},{72,6... | collective-permute-start | bytes 442376 | tf_op jit(solution)/shard_map/ppermute | solution.py:369
  20.0 24.4 %collective-permute-start.6 = (f32[3,4,96,128]{3,2,1,0:T(8,128)}, f32[3,4,96,128]{3,2,1,0:T(8,128)}, u32[]{:S(2)}, u32[]{:S(2)}) collective-permute-start(f32[3,4,96,128]{3,2,1,0:T(8,128)} %pad_maximum_fusion.2), channel_id=1, source_target_pairs={{0,1},{1,0},{2,3},{3,2},{4,5},{5,4},{6,7},{7,6},{8,9},{9,8},{10,11... | collective-permute-start | bytes 1769480 | tf_op jit(solution)/shard_map/ppermute | solution.py:376
  40.5 7.7 %copy-start.4 = (f32[3,4,96,128]{3,2,1,0:T(8,128)S(1)}, f32[3,4,96,128]{3,2,1,0:T(8,128)}, u32[]{:S(2)}) copy-start(f32[3,4,96,128]{3,2,1,0:T(8,128)} %get-tuple-element.23) | copy-start | bytes 1769476
  40.5 7.7 %collective-permute-start.15 = (f32[3,96,128]{2,1,0:T(8,128)}, f32[3,96,128]{2,1,0:T(8,128)S(1)}, u32[]{:S(2)}, u32[]{:S(2)}) collective-permute-start(f32[3,96,128]{2,1,0:T(8,128)} %get-tuple-element.25), channel_id=1, source_target_pairs={{8,0},{16,8},{24,16},{32,24},{40,32},{48,40},{56,48},{64,56},{72,6... | collective-permute-start | bytes 442376 | tf_op jit(solution)/shard_map/ppermute | solution.py:369
  43.5 4.7 %collective-permute-start.14 = (f32[3,96,128]{2,1,0:T(8,128)}, f32[3,96,128]{2,1,0:T(8,128)S(1)}, u32[]{:S(2)}, u32[]{:S(2)}) collective-permute-start(f32[3,96,128]{2,1,0:T(8,128)} %get-tuple-element.24), channel_id=1, source_target_pairs={{0,8},{8,16},{16,24},{24,32},{32,40},{40,48},{48,56},{56,64},{64,7... | collective-permute-start | bytes 442376 | tf_op jit(solution)/shard_map/ppermute | solution.py:364
  45.6 12.8 %collective-permute-start.7 = (f32[3,4,96,128]{3,2,1,0:T(8,128)S(1)}, f32[3,4,96,128]{3,2,1,0:T(8,128)S(1)}, u32[]{:S(2)}, u32[]{:S(2)}) collective-permute-start(f32[3,4,96,128]{3,2,1,0:T(8,128)S(1)} %fusion.4), channel_id=1, source_target_pairs={{0,2},{1,3},{2,0},{3,1},{4,6},{5,7},{6,4},{7,5},{8,10},{9,11},{10,... | collective-permute-start | bytes 1769480 | tf_op jit(solution)/shard_map/ppermute | solution.py:376
  48.2 23.8 %copy-start.5 = (f32[8,128]{1,0:T(8,128)S(1)}, f32[8,128]{1,0:T(8,128)}, u32[]{:S(2)}) copy-start(f32[8,128]{1,0:T(8,128)} %get-tuple-element.22) | copy-start | bytes 12292
  48.2 41.7 %copy-start = (f32[4,3,4,96,128]{4,3,2,1,0:T(8,128)S(1)}, f32[4,3,4,96,128]{4,3,2,1,0:T(8,128)}, u32[]{:S(2)}) copy-start(f32[4,3,4,96,128]{4,3,2,1,0:T(8,128)} %get-tuple-element.14.config_ref) | copy-start | bytes 7077892
  48.3 22.2 %collective-permute-start.16 = (f32[3,4,96,128]{3,2,1,0:T(8,128)S(1)}, f32[3,4,96,128]{3,2,1,0:T(8,128)S(1)}, u32[]{:S(2)}, u32[]{:S(2)}) collective-permute-start(f32[3,4,96,128]{3,2,1,0:T(8,128)S(1)} %pad_maximum_fusion.3), channel_id=1, source_target_pairs={{0,1},{1,0},{2,3},{3,2},{4,5},{5,4},{6,7},{7,6},{8,9},{9,8},{10,11... | collective-permute-start | bytes 1769480 | tf_op jit(solution)/shard_map/ppermute | solution.py:376
  58.5 40.3 %collective-permute-start.8 = (f32[3,4,96,128]{3,2,1,0:T(8,128)S(1)}, f32[3,4,96,128]{3,2,1,0:T(8,128)S(1)}, u32[]{:S(2)}, u32[]{:S(2)}) collective-permute-start(f32[3,4,96,128]{3,2,1,0:T(8,128)S(1)} %add.39), channel_id=1, source_target_pairs={{0,4},{1,5},{2,6},{3,7},{4,0},{5,1},{6,2},{7,3},{8,12},{9,13},{10,... | collective-permute-start | bytes 1769480 | tf_op jit(solution)/shard_map/ppermute | solution.py:376
  70.5 33.3 %collective-permute-start.17 = (f32[3,4,96,128]{3,2,1,0:T(8,128)S(1)}, f32[3,4,96,128]{3,2,1,0:T(8,128)S(1)}, u32[]{:S(2)}, u32[]{:S(2)}) collective-permute-start(f32[3,4,96,128]{3,2,1,0:T(8,128)S(1)} %fusion.3), channel_id=1, source_target_pairs={{0,2},{1,3},{2,0},{3,1},{4,6},{5,7},{6,4},{7,5},{8,10},{9,11},{10,... | collective-permute-start | bytes 1769480 | tf_op jit(solution)/shard_map/ppermute | solution.py:376
  72.1 10.9 %collective-permute-start.11 = (f32[8,128]{1,0:T(8,128)S(1)}, f32[8,128]{1,0:T(8,128)S(1)}, u32[]{:S(2)}, u32[]{:S(2)}) collective-permute-start(f32[8,128]{1,0:T(8,128)S(1)} %copy-done.5), channel_id=1, source_target_pairs={{0,1},{1,0},{2,3},{3,2},{4,5},{5,4},{6,7},{7,6},{8,9},{9,8},{10,11... | collective-permute-start | bytes 12296 | tf_op jit(solution)/shard_map/ppermute | solution.py:376
  83.0 4.4 %collective-permute-start.12 = (f32[8,128]{1,0:T(8,128)S(1)}, f32[8,128]{1,0:T(8,128)S(1)}, u32[]{:S(2)}, u32[]{:S(2)}) collective-permute-start(f32[8,128]{1,0:T(8,128)S(1)} %add.41), channel_id=1, source_target_pairs={{0,2},{1,3},{2,0},{3,1},{4,6},{5,7},{6,4},{7,5},{8,10},{9,11},{10,... | collective-permute-start | bytes 12296 | tf_op jit(solution)/shard_map/ppermute | solution.py:376
  87.3 11.4 %collective-permute-start.13 = (f32[8,128]{1,0:T(8,128)S(1)}, f32[8,128]{1,0:T(8,128)S(1)}, u32[]{:S(2)}, u32[]{:S(2)}) collective-permute-start(f32[8,128]{1,0:T(8,128)S(1)} %add.42), channel_id=1, source_target_pairs={{0,4},{1,5},{2,6},{3,7},{4,0},{5,1},{6,2},{7,3},{8,12},{9,13},{10,... | collective-permute-start | bytes 12296 | tf_op jit(solution)/shard_map/ppermute | solution.py:376
  90.1 40.1 %collective-permute-start.2 = (f32[4,3,96,128]{3,2,1,0:T(8,128)S(1)}, f32[4,3,96,128]{3,2,1,0:T(8,128)S(1)}, u32[]{:S(2)}, u32[]{:S(2)}) collective-permute-start(f32[4,3,96,128]{3,2,1,0:T(8,128)S(1)} %get-tuple-element.27), channel_id=1, source_target_pairs={{0,8},{8,16},{16,24},{24,32},{32,40},{40,48},{48,56},{56,64},{64,7... | collective-permute-start | bytes 1769480 | tf_op jit(solution)/shard_map/ppermute | solution.py:364
  98.8 31.4 %collective-permute-start.3 = (f32[4,3,96,128]{3,2,1,0:T(8,128)S(1)}, f32[4,3,96,128]{3,2,1,0:T(8,128)S(1)}, u32[]{:S(2)}, u32[]{:S(2)}) collective-permute-start(f32[4,3,96,128]{3,2,1,0:T(8,128)S(1)} %get-tuple-element.26), channel_id=1, source_target_pairs={{8,0},{16,8},{24,16},{32,24},{40,32},{48,40},{56,48},{64,56},{72,6... | collective-permute-start | bytes 1769480 | tf_op jit(solution)/shard_map/ppermute | solution.py:369
  103.9 34.7 %collective-permute-start.18 = (f32[3,4,96,128]{3,2,1,0:T(8,128)S(1)}, f32[3,4,96,128]{3,2,1,0:T(8,128)S(1)}, u32[]{:S(2)}, u32[]{:S(2)}) collective-permute-start(f32[3,4,96,128]{3,2,1,0:T(8,128)S(1)} %add.47), channel_id=1, source_target_pairs={{0,4},{1,5},{2,6},{3,7},{4,0},{5,1},{6,2},{7,3},{8,12},{9,13},{10,... | collective-permute-start | bytes 1769480 | tf_op jit(solution)/shard_map/ppermute | solution.py:376
  104.7 20.5 %all-to-all-start = ((f32[32,8,128]{2,1,0:T(8,128)}), f32[32,8,128]{2,1,0:T(8,128)}, u32[]{:S(2)}, u32[]{:S(2)}) async-start(f32[32,8,128]{2,1,0:T(8,128)} %broadcast_in_dim.2), calls=%async_computation | async-start | bytes 262144 | tf_op jit(solution)/shard_map/all_to_all | solution.py:415
  123.1 7.1 %collective-permute-start.10 = (f32[3,96,128]{2,1,0:T(8,128)}, f32[3,96,128]{2,1,0:T(8,128)}, u32[]{:S(2)}, u32[]{:S(2)}) collective-permute-start(f32[3,96,128]{2,1,0:T(8,128)} %get-tuple-element.20), channel_id=1, source_target_pairs={{8,0},{16,8},{24,16},{32,24},{40,32},{48,40},{56,48},{64,56},{72,6... | collective-permute-start | bytes 442376 | tf_op jit(solution)/shard_map/ppermute | solution.py:369
  123.4 6.8 %collective-permute-start.9 = (f32[3,96,128]{2,1,0:T(8,128)}, f32[3,96,128]{2,1,0:T(8,128)}, u32[]{:S(2)}, u32[]{:S(2)}) collective-permute-start(f32[3,96,128]{2,1,0:T(8,128)} %get-tuple-element.19), channel_id=1, source_target_pairs={{0,8},{8,16},{16,24},{24,32},{32,40},{40,48},{48,56},{56,64},{64,7... | collective-permute-start | bytes 442376 | tf_op jit(solution)/shard_map/ppermute | solution.py:364
  130.2 0.8 copy-start.2
  130.2 1.0 copy-start.3

commit v2 on v1

v2 whole, which is shorter than its diff:
```python
import functools
import math

import jax
import jax.numpy as jnp
from jax import lax
from jax.experimental import pallas as pl
from jax.experimental.pallas import tpu as pltpu
from jax.sharding import PartitionSpec as P

time_step = 0.05
viscosity = 0.5
stress_coef = 4.0
relax_time = 0.5
spring_limit = 10.0
spring_floor = 0.2
bulk_target = 1.0

SINE = (4.442882834149242, -7.308241154509167, 3.6062889576892747, -0.8457635932838079, 0.10920574854431932)
PAIRS = ((0, 0), (0, 1), (0, 2), (1, 1), (1, 2), (2, 2))
PLACE = ((0, 1, 2), (1, 3, 4), (2, 4, 5))
VMEM_LIMIT = 20 * 1024 * 1024
SMEM = pl.BlockSpec(memory_space=pltpu.SMEM)


def params():
    return pltpu.CompilerParams(vmem_limit_bytes=VMEM_LIMIT)


def mix_bits(value):
    value = value ^ lax.shift_right_logical(value, jnp.int32(16))
    value = value * jnp.int32(73244475)
    value = value ^ lax.shift_right_logical(value, jnp.int32(16))
    value = value * jnp.int32(73244475)
    return value ^ lax.shift_right_logical(value, jnp.int32(16))


def noise_of(salted, even):
    mask = jnp.int32(16777215)
    first = mix_bits(even ^ salted)
    second = mix_bits(even ^ (salted ^ 1))
    upper = ((first & mask).astype(jnp.float32) + 0.5) * (1.0 / 16777216.0)
    turn = (second & mask).astype(jnp.float32) * (1.0 / 16777216.0) + (0.5 / 16777216.0 - 0.5)
    square = jnp.maximum(jnp.log(upper) * (-2.0 * time_step / relax_time), 1e-30)
    radius = square * lax.rsqrt(square)
    w = turn * turn
    q = jnp.float32(SINE[4])
    for coef in SINE[3::-1]:
        q = q * w + coef
    q = q * turn
    return radius * (q * q - 1.0)


def noise_kernel(step, total_x, keys_ref, out_ref):
    _, _, width, rows, depth = out_ref.shape
    x_start = lax.axis_index("gx") * width
    salted = mix_bits(keys_ref[2 * pl.program_id(0) + step] + jnp.int32(40503))
    ypos = lax.broadcasted_iota(jnp.int32, (rows, depth), 0)
    zpos = lax.broadcasted_iota(jnp.int32, (rows, depth), 1)
    local = (ypos * depth + zpos) * 2

    def body(n, carry):
        comp = n // width
        x = n - comp * width
        even = local + ((comp * total_x + x_start + x) * rows) * (2 * depth)
        out_ref[0, comp, x] = noise_of(salted, even)
        return carry

    lax.fori_loop(0, 3 * width, body, 0)


def draw_noise(keys, step, total_x, shape):
    fields, comps, width, rows, depth = shape
    return pl.pallas_call(
        functools.partial(noise_kernel, step, total_x),
        grid=(fields,),
        out_shape=pltpu.HBM(shape, jnp.float32) if step else jax.ShapeDtypeStruct(shape, jnp.float32),
        in_specs=[SMEM],
        out_specs=pl.BlockSpec((1, comps, width, rows, depth), lambda k: (k, 0, 0, 0, 0)),
        compiler_params=params(),
        name="draw_noise",
    )(keys)


def up_z(f):
    return pltpu.roll(f, f.shape[-1] - 1, f.ndim - 1)


def down_z(f):
    return pltpu.roll(f, 1, f.ndim - 1)


def up_y(f):
    row = lax.broadcasted_iota(jnp.int32, f.shape, 0)
    return jnp.where(row == f.shape[0] - 1, 0.0, pltpu.roll(f, f.shape[0] - 1, 0))


def down_y(f):
    row = lax.broadcasted_iota(jnp.int32, f.shape, 0)
    return jnp.where(row == 0, 0.0, pltpu.roll(f, 1, 0))


def spring_of(q):
    length = q[0] * q[0] + q[1] * q[1] + q[2] * q[2]
    return 1.0 / jnp.maximum(1.0 - length * (1.0 / spring_limit), spring_floor)


def field_block(shape):
    return pl.BlockSpec((1,) + shape[1:], lambda k: (k,) + (0,) * (len(shape) - 1))


def whole_block(shape):
    return pl.BlockSpec(shape, lambda k: (0,) * len(shape))


def rim_block(shape, at=None):
    if at is None:
        return pl.BlockSpec((1,) + shape[1:], lambda k: (k, 0, 0, 0))
    return pl.BlockSpec((1,) + shape[1:], lambda k: (at, 0, 0, 0))


def quad_place():
    return lax.rem(lax.axis_index("row"), 4)


def div_kernel(total_fields, config_ref, before_ref, after_ref, *refs):
    outs, stress_ref, rim_ref, div_ref = refs[:4], refs[4], refs[5], refs[6]
    k = pl.program_id(0)
    _, _, width, rows, depth = config_ref.shape

    @pl.when(k == 0)
    def _():
        stress_ref[...] = jnp.zeros_like(stress_ref)
        rim_ref[...] = jnp.zeros_like(rim_ref)

    for x in range(width):
        q = [config_ref[0, i, x] for i in range(3)]
        spring = spring_of(q) * (0.5 / total_fields)
        weighted = [spring * q[i] for i in range(3)]
        for p, (i, j) in enumerate(PAIRS):
            stress_ref[p, x] += weighted[i] * q[j]
    for side, ref in enumerate((before_ref, after_ref)):
        q = [ref[0, i] for i in range(3)]
        weighted = spring_of(q) * (0.5 / total_fields) * q[0]
        for i in range(3):
            rim_ref[side, i] += weighted * q[i]

    @pl.when(k == pl.num_programs(0) - 1)
    def _():
        for x in range(width):
            for i in range(3):
                sy = stress_ref[PLACE[i][1], x]
                sz = stress_ref[PLACE[i][2], x]
                above = stress_ref[PLACE[i][0], x + 1] if x + 1 < width else rim_ref[1, i]
                below = stress_ref[PLACE[i][0], x - 1] if x > 0 else rim_ref[0, i]
                div_ref[x, i] = (above - below) + (up_y(sy) - down_y(sy)) + (up_z(sz) - down_z(sz))
        place = quad_place()
        for n, out in enumerate(outs):
            out[...] = div_ref[lax.rem(place + n, 4)]


def stress_parts(config, before, after, total_fields):
    fields, _, width, rows, depth = config.shape
    part = jax.ShapeDtypeStruct((3, rows, depth), jnp.float32)
    return pl.pallas_call(
        functools.partial(div_kernel, total_fields),
        grid=(fields,),
        out_shape=[part] * 4,
        in_specs=[field_block(config.shape), rim_block(before.shape), rim_block(after.shape)],
        out_specs=[whole_block(part.shape)] * 4,
        scratch_shapes=[
            pltpu.VMEM((6, width, rows, depth), jnp.float32),
            pltpu.VMEM((2, 3, rows, depth), jnp.float32),
            pltpu.VMEM((width, 3, rows, depth), jnp.float32),
        ],
        compiler_params=params(),
        name="stress_parts",
    )(config, before, after)


def fill_slopes(flow_at, slope_ref, width):
    half = 0.5 * time_step
    for x in range(width):
        for i in range(3):
            here = flow_at(i, x)
            slope_ref[x, 3 * i] = half * (flow_at(i, x + 1) - flow_at(i, x - 1))
            slope_ref[x, 3 * i + 1] = half * (up_y(here) - down_y(here))
            slope_ref[x, 3 * i + 2] = half * (up_z(here) - down_z(here))
            slope_ref[x, 9 + i] = half * here


def advance_field(config_ref, before_ref, after_ref, noise_ref, new_ref, slope_ref):
    _, _, width, rows, depth = config_ref.shape
    for x in range(width):
        q = [config_ref[0, i, x] for i in range(3)]
        keep = 1.0 - (time_step / (2.0 * relax_time)) * spring_of(q)
        for i in range(3):
            below = config_ref[0, i, x - 1] if x > 0 else before_ref[0, i]
            above = config_ref[0, i, x + 1] if x + 1 < width else after_ref[0, i]
            along = slope_ref[x, 9] * (above - below)
            along = along + slope_ref[x, 10] * (up_y(q[i]) - down_y(q[i]))
            along = along + slope_ref[x, 11] * (up_z(q[i]) - down_z(q[i]))
            stretch = slope_ref[x, 3 * i] * q[0] + slope_ref[x, 3 * i + 1] * q[1] + slope_ref[x, 3 * i + 2] * q[2]
            new_ref[0, i, x] = q[i] * keep + (stretch - along) + noise_ref[0, i, x]


def second_kernel(
    total_fields, config_ref, before_ref, after_ref, flow_ref, fbefore_ref, fafter_ref, noise_ref,
    new_ref, first_ref, last_ref, wall_ref, slope_ref,
):
    k = pl.program_id(0)
    _, _, width, rows, depth = config_ref.shape

    def flow_at(i, x):
        if x < 0:
            return fbefore_ref[0, i]
        if x >= width:
            return fafter_ref[0, i]
        return flow_ref[i, x]

    @pl.when(k == 0)
    def _():
        fill_slopes(flow_at, slope_ref, width)
        wall_ref[...] = jnp.zeros_like(wall_ref)

    advance_field(config_ref, before_ref, after_ref, noise_ref, new_ref, slope_ref)
    for i in range(3):
        first_ref[0, i] = new_ref[0, i, 0]
        last_ref[0, i] = new_ref[0, i, width - 1]
    wall = jnp.zeros((8, depth), jnp.float32)
    row = lax.broadcasted_iota(jnp.int32, (8, depth), 0)
    for x in range(width):
        low = [new_ref[0, i, x, 0:8, :] for i in range(3)]
        high = [new_ref[0, i, x, rows - 8:rows, :] for i in range(3)]
        wall = wall + jnp.where(row == 7, spring_of(high) * (high[0] * high[1]), 0.0)
        wall = wall - jnp.where(row == 0, spring_of(low) * (low[0] * low[1]), 0.0)
    wall_ref[...] += wall * (0.5 / total_fields)


def second_fields(config, before, after, flow, noise, total_fields):
    fields, _, width, rows, depth = config.shape
    rim = jax.ShapeDtypeStruct((fields, 3, rows, depth), jnp.float32)
    wall = jax.ShapeDtypeStruct((8, depth), jnp.float32)
    return pl.pallas_call(
        functools.partial(second_kernel, total_fields),
        grid=(fields,),
        out_shape=[pltpu.HBM(config.shape, jnp.float32), rim, rim, wall],
        in_specs=[
            field_block(config.shape), rim_block(before.shape), rim_block(after.shape), whole_block(flow.shape),
            rim_block(before.shape, fields), rim_block(after.shape, fields), field_block(noise.shape),
        ],
        out_specs=[field_block(config.shape), rim_block(rim.shape), rim_block(rim.shape), whole_block(wall.shape)],
        scratch_shapes=[pltpu.VMEM((width, 12, rows, depth), jnp.float32)],
        compiler_params=params(),
        name="second_fields",
    )(config, before, after, flow, before, after, noise)


def flow_step(at, div_at, width, write):
    half = 0.5 * time_step
    for x in range(width):
        adv = [half * at(j, x) for j in range(3)]
        for i in range(3):
            here = at(i, x)
            below, above = at(i, x - 1), at(i, x + 1)
            left, right = down_y(here), up_y(here)
            back, front = down_z(here), up_z(here)
            along = adv[0] * (above - below) + adv[1] * (right - left) + adv[2] * (front - back)
            lap = (above + below) + (right + left) + (front + back) - 6.0 * here
            write(i, x, here - along + (time_step * viscosity) * lap + (time_step * stress_coef) * div_at(i, x))


def gather_parts(parts, div_ref):
    place = quad_place()
    for n, part in enumerate(parts):
        at = lax.rem(place + 4 - n, 4)
        rows = div_ref.shape[2]
        for i in range(3):
            div_ref[at, i] = part[i * rows:(i + 1) * rows]


def third_kernel(flow_ref, fbefore_ref, fafter_ref, p0, p1, p2, p3, start_ref, first_ref, last_ref, sums_ref, div_ref):
    _, width, rows, depth = flow_ref.shape
    gather_parts((p0, p1, p2, p3), div_ref)

    def at(i, x):
        if x < 0:
            return fbefore_ref[0, i]
        if x >= width:
            return fafter_ref[0, i]
        return flow_ref[i, x]

    def write(i, x, value):
        start_ref[i, x] = value

    flow_step(at, lambda i, x: div_ref[x, i], width, write)
    total = jnp.zeros((8, depth), jnp.float32)
    bend = jnp.zeros((8, depth), jnp.float32)
    edge = jnp.zeros((1, depth), jnp.float32)
    gain = jnp.zeros((1, depth), jnp.float32)
    for x in range(width):
        s, v, w = start_ref[0, x], start_ref[1, x], start_ref[2, x]
        term = v * (0.5 * (up_y(s) - down_y(s))) + w * (0.5 * (up_z(s) - down_z(s)))
        for r in range(rows // 8):
            total = total + s[8 * r:8 * r + 8]
            bend = bend + term[8 * r:8 * r + 8]
        edge = edge + (s[0:1] + s[rows - 1:rows])
        gain = gain + (v[0:1] - v[rows - 1:rows])
    row = lax.broadcasted_iota(jnp.int32, (8, depth), 0)
    sums = [
        jnp.sum(total, axis=0, keepdims=True),
        jnp.sum(bend, axis=0, keepdims=True) + viscosity * edge,
        0.5 * gain,
        jnp.sum(sum(p[3 * rows:] for p in (p0, p1, p2, p3)), axis=0, keepdims=True),
    ]
    tile = jnp.zeros((8, depth), jnp.float32)
    for n, value in enumerate(sums):
        tile = jnp.where(row == n, value, tile)
    for n in range(sums_ref.shape[0]):
        sums_ref[n] = tile
    for i in range(3):
        first_ref[i] = start_ref[i, 0]
        last_ref[i] = start_ref[i, width - 1]


def third_flow(flow, left, right, parts, slabs):
    _, width, rows, depth = flow.shape
    end = jax.ShapeDtypeStruct((3, rows, depth), jnp.float32)
    sums = jax.ShapeDtypeStruct((slabs, 8, depth), jnp.float32)
    at = left.shape[0] - 1
    return pl.pallas_call(
        third_kernel,
        grid=(1,),
        out_shape=[pltpu.HBM(flow.shape, jnp.float32), end, end, sums],
        in_specs=[whole_block(flow.shape), rim_block(left.shape, at), rim_block(right.shape, at)]
        + [whole_block(parts[0].shape)] * 4,
        out_specs=[whole_block(flow.shape), whole_block(end.shape), whole_block(end.shape), whole_block(sums.shape)],
        scratch_shapes=[pltpu.VMEM((width, 3, rows, depth), jnp.float32)],
        compiler_params=params(),
        name="third_flow",
    )(flow, left, right, *parts)


def lifts_of(shared_ref, walls, cells):
    sums = jnp.sum(jnp.sum(shared_ref[...], axis=0), axis=1, keepdims=True)
    lift = bulk_target - sums[0:1] / cells
    change = time_step * (stress_coef * sums[3:4] - sums[1:2] - lift * (sums[2:3] + 2.0 * viscosity * walls))
    return lift, -change / cells


def fourth_kernel(walls, cells, config_ref, before_ref, after_ref, start_ref, sbefore_ref, safter_ref, noise_ref, shared_ref, new_ref, slope_ref):
    width = config_ref.shape[2]

    def flow_at(i, x):
        if x < 0:
            return sbefore_ref[i]
        if x >= width:
            return safter_ref[i]
        return start_ref[i, x]

    @pl.when(pl.program_id(0) == 0)
    def _():
        lift = lifts_of(shared_ref, walls, cells)[0]
        fill_slopes(lambda i, x: flow_at(i, x) + lift if i == 0 else flow_at(i, x), slope_ref, width)

    advance_field(config_ref, before_ref, after_ref, noise_ref, new_ref, slope_ref)


def fourth_fields(config, before, after, start, sbefore, safter, noise, shared, walls, cells):
    fields, _, width, rows, depth = config.shape
    return pl.pallas_call(
        functools.partial(fourth_kernel, walls, cells),
        grid=(fields,),
        out_shape=jax.ShapeDtypeStruct(config.shape, jnp.float32),
        in_specs=[
            field_block(config.shape), rim_block(before.shape), rim_block(after.shape), whole_block(start.shape),
            whole_block(sbefore.shape), whole_block(safter.shape), field_block(noise.shape), whole_block(shared.shape),
        ],
        out_specs=field_block(config.shape),
        scratch_shapes=[pltpu.VMEM((width, 12, rows, depth), jnp.float32)],
        compiler_params=params(),
        name="fourth_fields",
    )(config, before, after, start, sbefore, safter, noise, shared)


def fifth_kernel(walls, cells, start_ref, sbefore_ref, safter_ref, p0, p1, p2, p3, shared_ref, out_ref, div_ref):
    width = start_ref.shape[1]
    lift, last_lift = lifts_of(shared_ref, walls, cells)
    gather_parts((p0, p1, p2, p3), div_ref)

    def at(i, x):
        if x < 0:
            value = sbefore_ref[i]
        elif x >= width:
            value = safter_ref[i]
        else:
            value = start_ref[i, x]
        return value + lift if i == 0 else value

    def write(i, x, value):
        out_ref[i, x] = value + last_lift if i == 0 else value

    flow_step(at, lambda i, x: div_ref[x, i], width, write)


def fifth_flow(start, sbefore, safter, parts, shared, walls, cells):
    _, width, rows, depth = start.shape
    return pl.pallas_call(
        functools.partial(fifth_kernel, walls, cells),
        grid=(1,),
        out_shape=jax.ShapeDtypeStruct(start.shape, jnp.float32),
        in_specs=[whole_block(start.shape)] + [whole_block(sbefore.shape)] * 2 + [whole_block(parts[0].shape)] * 4 + [whole_block(shared.shape)],
        out_specs=whole_block(start.shape),
        scratch_shapes=[pltpu.VMEM((width, 3, rows, depth), jnp.float32)],
        compiler_params=params(),
        name="fifth_flow",
    )(start, sbefore, safter, *parts, shared)


def pack_kernel(first_ref, last_ref, ffirst_ref, flast_ref, head_ref, tail_ref):
    velocity = pl.program_id(0) == pl.num_programs(0) - 1

    @pl.when(velocity)
    def _():
        head_ref[0] = ffirst_ref[:, 0]
        tail_ref[0] = flast_ref[:, 0]

    @pl.when(jnp.logical_not(velocity))
    def _():
        head_ref[0] = first_ref[0, :, 0]
        tail_ref[0] = last_ref[0, :, 0]


def pack_ends(config, flow):
    fields, _, width, rows, depth = config.shape
    rim = jax.ShapeDtypeStruct((fields + 1, 3, rows, depth), jnp.float32)

    def layer(x):
        return pl.BlockSpec((1, 3, 1, rows, depth), lambda k: (jnp.minimum(k, fields - 1), 0, x, 0, 0))

    def flow_layer(x):
        return pl.BlockSpec((3, 1, rows, depth), lambda k: (0, x, 0, 0))

    return pl.pallas_call(
        pack_kernel,
        grid=(fields + 1,),
        out_shape=[rim, rim],
        in_specs=[layer(0), layer(width - 1), flow_layer(0), flow_layer(width - 1)],
        out_specs=[rim_block(rim.shape)] * 2,
        compiler_params=params(),
        name="pack_ends",
    )(config, config, flow, flow)


def from_left(value):
    count = lax.axis_size("gx")
    return lax.ppermute(value, "gx", [(i, (i + 1) % count) for i in range(count)])


def from_right(value):
    count = lax.axis_size("gx")
    return lax.ppermute(value, "gx", [((i + 1) % count, i) for i in range(count)])


def quad_shift(value, by):
    count = lax.axis_size("row")
    return lax.ppermute(value, "row", [(i, i - i % 4 + (i + by) % 4) for i in range(count)])


def pair_swap(value, bit):
    count = lax.axis_size("row")
    return lax.ppermute(value, "row", [(i, i ^ bit) for i in range(count)])


def in_hbm(value):
    return pltpu.with_memory_space_constraint(value, pltpu.HBM)


def flat(value):
    return value.reshape(-1, value.shape[-1])


def after(value, *others):
    return lax.optimization_barrier((value,) + others)[0]


def shards(config, flow, keys):
    fields, _, width, rows, depth = config.shape
    total_fields = fields * lax.axis_size("row")
    slabs = lax.axis_size("gx")
    total_x = width * slabs
    cells = total_x * rows * depth

    keys = keys.reshape(-1)

    head, tail = pack_ends(in_hbm(config), in_hbm(flow))
    left, right = from_left(tail), from_right(head)
    noise = draw_noise(keys, 0, total_x, config.shape)
    left, right = after(left, noise), after(right, noise)

    parts = stress_parts(config, left, right, total_fields)
    got = [quad_shift(parts[n], n) for n in (1, 2, 3)]
    config, first, last, wall = second_fields(config, after(left, parts[0]), right, flow, noise, total_fields)
    before, behind = from_left(last), from_right(first)
    got = [after(g, config) for g in got]
    own = jnp.concatenate([flat(parts[0] + got[0] + got[1] + got[2]), wall], axis=0)
    swap = pair_swap(own, 4)
    later = draw_noise(after(keys, own), 1, total_x, config.shape)
    own = own + after(swap, later)
    div = [own] + [quad_shift(own, n) for n in (1, 2, 3)]

    parts = stress_parts(after(config, own), before, behind, total_fields)
    got = [quad_shift(parts[n], n) for n in (1, 2, 3)]

    start, first, last, sums = third_flow(flow, left, right, [after(d, parts[0]) for d in div], slabs)
    sleft, sright = from_left(last), from_right(first)
    shared = lax.all_to_all(sums, "gx", 0, 0)
    own = flat(parts[0] + got[0] + got[1] + after(got[2], start))
    own = own + after(pair_swap(own, 4), shared)
    next_div = [own] + [quad_shift(own, n) for n in (1, 2, 3)]

    walls = total_x * depth
    config = fourth_fields(in_hbm(config), in_hbm(before), in_hbm(behind), in_hbm(start), sleft, sright, in_hbm(later), shared, walls, cells)
    flow = fifth_flow(in_hbm(start), sleft, sright, [after(d, config) for d in next_div], shared, walls, cells)
    return config, flow


def solution(mesh):
    placed = (P("row", None, "gx", None, None), P(None, "gx", None, None), P("row", None))
    return jax.shard_map(
        shards,
        mesh=mesh,
        in_specs=placed,
        out_specs=(P("row", None, "gx", None, None), P(None, "gx", None, None)),
        check_vma=False,
    )
```

time: 145 us -> 93.3 us (0.64); the launches traced: 142 us -> 92.2 us
  waiting for transfers between devices: 37.4 us -> 16.5 us
  local copies, waits for them, and re-layouts: 10.9 us -> 0.2 us
  other arithmetic: 6.83 us -> 0.12 us
  starting transfers between devices: 44.4 us -> 38 us
  Pallas kernels: 39.3 us -> 36.6 us
  between operations: 3.44 us -> 0.79 us
    ppermute x9 -> x14, waiting for transfers between devices: 33.8 us -> 5.06 us  [the longest x2 3.34 us: pair_swap(): return lax.ppermute(value, 'row', [(i, i ^ bit) for i in range(count)])]
    ppermute x5 -> x3, starting transfers between devices: 14.8 us -> 5.54 us  [from_left(): lax.ppermute(value, 'gx', [(i, (i + 1) % count) for i in range(count)])]
    ppermute x9 -> x14, starting transfers between devices: 11.6 us -> 18.1 us  [the longest x12 14 us: quad_shift(): lax.ppermute(value, 'row', [(i, i - i % 4 + (i + by) % 4) for i in range(...]
    slice x8 -> x0, local copies, waits for them, and re-layouts: 5.7 us -> none  [the longest x2 1.96 us: with_ends(): return jnp.concatenate([first, div[:, 1:-1], last], axis=1)]
    all_to_all x1, waiting for transfers between devices: 0.4 us -> 5.69 us  [shards(): shared = lax.all_to_all(sums, 'gx', 0, 0)]
    ppermute x5 -> x3, starting transfers between devices: 6.67 us -> 3.38 us  [from_right(): lax.ppermute(value, 'gx', [((i + 1) % count, i) for i in range(count)])]
    add x10 -> x4, other arithmetic: 3.13 us -> 0.11 us  [the longest x1 0.04 us: shards(): parts[0] + got[0] + got[1] + got[2]]
    squeeze x4 -> x0, local copies, waits for them, and re-layouts: 2.82 us -> none  [the longest x1 1.39 us: shards(): head = jnp.concatenate([config[:, :, 0], flow[None, :, 0]], axis=0)]
  transfers between devices with their start and end apart: 20 -> 21, of which waited for: 7 -> 5; matrix products, arithmetic and copies ran while one was open for 10% -> 0% of each run, Pallas kernels for 26% -> 29%
where the time goes in v2:
time: 93.3 us; the launch traced here: 92.2 us
  starting transfers between devices  38 us (41%)
  Pallas kernels  36.6 us (39%)
  waiting for transfers between devices  16.5 us (18%)
    ppermute x12, starting transfers between devices, quad_shift(): lax.ppermute(value, 'row', [(i, i - i % 4 + (i + by) % 4) for i in range(...  14 us
    pallas_call x2, Pallas kernels, draw_noise(): pl.pallas_call(functools.partial(noise_kernel, step, total_x), grid=(fiel...  11.2 us
    all_to_all x1, starting transfers between devices, shards(): shared = lax.all_to_all(sums, 'gx', 0, 0)  11 us
    pallas_call x1, Pallas kernels, fourth_fields(): pl.pallas_call(functools.partial(fourth_kernel, walls, cells), grid=(fiel...  6.25 us
    all_to_all x1, waiting for transfers between devices, shards(): shared = lax.all_to_all(sums, 'gx', 0, 0)  5.69 us
    ppermute x3, starting transfers between devices, from_left(): lax.ppermute(value, 'gx', [(i, (i + 1) % count) for i in range(count)])  5.54 us
    pallas_call x2, Pallas kernels, stress_parts(): pl.pallas_call(functools.partial(div_kernel, total_fields), grid=(fields,...  5.22 us
    pallas_call x1, Pallas kernels, second_fields(): pl.pallas_call(functools.partial(second_kernel, total_fields), grid=(fiel...  5.07 us
  transfers between devices with their start and end apart: 21, of which 5 were waited for; matrix products, arithmetic and copies ran while one was open for 0% of the time, Pallas kernels for 29%

profile of v2, /device:TPU:1, one launch (start us, length us, event | category | flops | bytes accessed | tf_op | source)
XLA Modules:
  0.0 92.2 jit_solution(5140501594311845471)
XLA Ops:
  0.6 0.0 copy-start.5
  0.6 3.9 %pack_ends.1 = (f32[5,3,96,128]{3,2,1,0:T(8,128)}, f32[5,3,96,128]{3,2,1,0:T(8,128)}) custom-call(f32[4,3,4,96,128]{4,3,2,1,0:T(8,128)} %config_ref.3, f32[4,3,4,96,128]{4,3,2,1,0:T(8,128)} %config_ref.3, f32[3,4,96,128]{3,2,1,0:T(8,128)} %flow_ref.3, f32[3,4,96,128]{3,2,1,0:T(8,128)} %flow_ref.3), custom_call_target="tpu_custom_call" | custom-call | tf_op jit(solution)/shard_map/pack_ends/pallas_call | solution.py:444
  4.5 0.0 copy-start
  4.5 3.1 %collective-permute-start = (f32[5,3,96,128]{3,2,1,0:T(8,128)}, f32[5,3,96,128]{3,2,1,0:T(8,128)S(1)}, u32[]{:S(2)}, u32[]{:S(2)}) collective-permute-start(f32[5,3,96,128]{3,2,1,0:T(8,128)} %get-tuple-element.39), channel_id=1, source_target_pairs={{0,8},{8,16},{16,24},{24,32},{32,40},{40,48},{48,56},{56,64},{64,7... | collective-permute-start | bytes 2211848 | tf_op jit(solution)/shard_map/ppermute | solution.py:457
  7.6 0.3 collective-permute-start.1
  7.9 0.0 copy-done.5
  7.9 0.1 copy.6
  8.0 0.1 reshape.13.keys_ref
  8.1 5.2 %draw_noise.2.noise_ref = f32[4,3,4,96,128]{4,3,2,1,0:T(8,128)S(1)} custom-call(s32[8]{0:T(128)S(1)} %reshape.13.keys_ref), custom_call_target="tpu_custom_call" | custom-call | tf_op jit(solution)/shard_map/draw_noise/pallas_call | solution.py:74
  13.2 0.0 copy-start.1
  13.3 3.1 %collective-permute-done.before_ref.fbefore_ref = f32[5,3,96,128]{3,2,1,0:T(8,128)S(1)} collective-permute-done((f32[5,3,96,128]{3,2,1,0:T(8,128)}, f32[5,3,96,128]{3,2,1,0:T(8,128)S(1)}, u32[]{:S(2)}, u32[]{:S(2)}) %collective-permute-start) | collective-permute-done | bytes 737312 | tf_op jit(solution)/shard_map/ppermute | solution.py:457
  16.3 2.7 %collective-permute-done.1.after_ref.fafter_ref = f32[5,3,96,128]{3,2,1,0:T(8,128)} collective-permute-done((f32[5,3,96,128]{3,2,1,0:T(8,128)}, f32[5,3,96,128]{3,2,1,0:T(8,128)}, u32[]{:S(2)}, u32[]{:S(2)}) %collective-permute-start.1) | collective-permute-done | bytes 737312 | tf_op jit(solution)/shard_map/ppermute | solution.py:462
  19.0 0.0 copy-done
  19.0 3.1 %stress_parts.2 = (f32[3,96,128]{2,1,0:T(8,128)S(1)}, f32[3,96,128]{2,1,0:T(8,128)S(1)}, f32[3,96,128]{2,1,0:T(8,128)S(1)}, f32[3,96,128]{2,1,0:T(8,128)S(1)}) custom-call(f32[4,3,4,96,128]{4,3,2,1,0:T(8,128)S(1)} %copy-done, f32[5,3,96,128]{3,2,1,0:T(8,128)S(1)} %collective-permute-done.before_ref.fbefore_ref, ...), custom_call_target="tpu_custom_call" | custom-call | tf_op jit(solution)/shard_map/stress_parts/pallas_call | solution.py:165
  22.1 1.3 %collective-permute-start.4 = (f32[3,96,128]{2,1,0:T(8,128)S(1)}, f32[3,96,128]{2,1,0:T(8,128)S(1)}, u32[]{:S(2)}, u32[]{:S(2)}) collective-permute-start(f32[3,96,128]{2,1,0:T(8,128)S(1)} %get-tuple-element.48), channel_id=1, source_target_pairs={{0,1},{1,2},{2,3},{3,0},{4,5},{5,6},{6,7},{7,4},{8,9},{9,10},{10,1... | collective-permute-start | bytes 442376 | tf_op jit(solution)/shard_map/ppermute | solution.py:467
  23.4 2.5 %collective-permute-start.5 = (f32[3,96,128]{2,1,0:T(8,128)S(1)}, f32[3,96,128]{2,1,0:T(8,128)S(1)}, u32[]{:S(2)}, u32[]{:S(2)}) collective-permute-start(f32[3,96,128]{2,1,0:T(8,128)S(1)} %get-tuple-element.50), channel_id=1, source_target_pairs={{0,2},{1,3},{2,0},{3,1},{4,6},{5,7},{6,4},{7,5},{8,10},{9,11},{10,... | collective-permute-start | bytes 442376 | tf_op jit(solution)/shard_map/ppermute | solution.py:467
  25.8 1.2 %collective-permute-start.6 = (f32[3,96,128]{2,1,0:T(8,128)S(1)}, f32[3,96,128]{2,1,0:T(8,128)S(1)}, u32[]{:S(2)}, u32[]{:S(2)}) collective-permute-start(f32[3,96,128]{2,1,0:T(8,128)S(1)} %get-tuple-element.52), channel_id=1, source_target_pairs={{0,3},{1,0},{2,1},{3,2},{4,7},{5,4},{6,5},{7,6},{8,11},{9,8},{10,9... | collective-permute-start | bytes 442376 | tf_op jit(solution)/shard_map/ppermute | solution.py:467
  27.0 0.0 copy-done.1
  27.0 5.1 %second_fields.1 = (f32[4,3,4,96,128]{4,3,2,1,0:T(8,128)}, f32[4,3,96,128]{3,2,1,0:T(8,128)S(1)}, f32[4,3,96,128]{3,2,1,0:T(8,128)S(1)}, f32[8,128]{1,0:T(8,128)S(1)}) custom-call(f32[4,3,4,96,128]{4,3,2,1,0:T(8,128)S(1)} %copy-done, f32[5,3,96,128]{3,2,1,0:T(8,128)S(1)} %collective-permute-done.before_ref.fbefore_ref, ...), custom_call_target="tpu_custom_call" | custom-call | tf_op jit(solution)/shard_map/second_fields/pallas_call | solution.py:244
  32.0 0.0 copy-start.2
  32.0 0.5 collective-permute-start.2
  32.6 3.1 %collective-permute-start.3 = (f32[4,3,96,128]{3,2,1,0:T(8,128)S(1)}, f32[4,3,96,128]{3,2,1,0:T(8,128)S(1)}, u32[]{:S(2)}, u32[]{:S(2)}) collective-permute-start(f32[4,3,96,128]{3,2,1,0:T(8,128)S(1)} %get-tuple-element.47), channel_id=1, source_target_pairs={{8,0},{16,8},{24,16},{32,24},{40,32},{48,40},{56,48},{64,56},{72,6... | collective-permute-start | bytes 1769480 | tf_op jit(solution)/shard_map/ppermute | solution.py:462
  35.7 0.0 collective-permute-done.4
  35.7 0.0 collective-permute-done.5
  35.7 0.0 collective-permute-done.6
  35.7 2.7 %collective-permute-start.7 = (f32[296,128]{1,0:T(8,128)S(1)}, f32[296,128]{1,0:T(8,128)S(1)}, u32[]{:S(2)}, u32[]{:S(2)}) collective-permute-start(f32[296,128]{1,0:T(8,128)S(1)} %pad_maximum_fusion), channel_id=1, source_target_pairs={{0,4},{1,5},{2,6},{3,7},{4,0},{5,1},{6,2},{7,3},{8,12},{9,13},{10,... | collective-permute-start | bytes 454664 | tf_op jit(solution)/shard_map/ppermute | solution.py:472
  38.4 6.0 %draw_noise.3.noise_ref = f32[4,3,4,96,128]{4,3,2,1,0:T(8,128)} custom-call(s32[8]{0:T(128)S(1)} %reshape.13.keys_ref), custom_call_target="tpu_custom_call" | custom-call | tf_op jit(solution)/shard_map/draw_noise/pallas_call | solution.py:74
  44.5 3.3 %collective-permute-done.7 = f32[296,128]{1,0:T(8,128)S(1)} collective-permute-done((f32[296,128]{1,0:T(8,128)S(1)}, f32[296,128]{1,0:T(8,128)S(1)}, u32[]{:S(2)}, u32[]{:S(2)}) %collective-permute-start.7) | collective-permute-done | bytes 151584 | tf_op jit(solution)/shard_map/ppermute | solution.py:472
  47.8 0.1 collective-permute-start.10
  47.9 2.1 %collective-permute-start.9 = (f32[296,128]{1,0:T(8,128)S(1)}, f32[296,128]{1,0:T(8,128)S(1)}, u32[]{:S(2)}, u32[]{:S(2)}) collective-permute-start(f32[296,128]{1,0:T(8,128)S(1)} %fusion.p0), channel_id=1, source_target_pairs={{0,2},{1,3},{2,0},{3,1},{4,6},{5,7},{6,4},{7,5},{8,10},{9,11},{10,... | collective-permute-start | bytes 454664 | tf_op jit(solution)/shard_map/ppermute | solution.py:467
  50.0 0.0 collective-permute-start.8
  50.0 0.0 collective-permute-done.2.before_ref
  50.0 0.0 collective-permute-done.3.after_ref
  50.0 0.0 copy-done.2
  50.0 0.0 copy-start.4
  50.0 2.2 %stress_parts.3 = (f32[3,96,128]{2,1,0:T(8,128)S(1)}, f32[3,96,128]{2,1,0:T(8,128)S(1)}, f32[3,96,128]{2,1,0:T(8,128)S(1)}, f32[3,96,128]{2,1,0:T(8,128)}) custom-call(f32[4,3,4,96,128]{4,3,2,1,0:T(8,128)S(1)} %copy-done.2, f32[4,3,96,128]{3,2,1,0:T(8,128)S(1)} %collective-permute-done.2.before_ref, f32[4,3,96,128]{3,2,1,0:T(8,128)S(1)} %collective-permute-done.3.after_ref), custom_call_target="tpu_custom_call" | custom-call | tf_op jit(solution)/shard_map/stress_parts/pallas_call | solution.py:165
  52.2 2.7 %collective-permute-start.15 = (f32[3,96,128]{2,1,0:T(8,128)}, f32[3,96,128]{2,1,0:T(8,128)S(1)}, u32[]{:S(2)}, u32[]{:S(2)}) collective-permute-start(f32[3,96,128]{2,1,0:T(8,128)} %get-tuple-element.69), channel_id=1, source_target_pairs={{0,3},{1,0},{2,1},{3,2},{4,7},{5,4},{6,5},{7,6},{8,11},{9,8},{10,9... | collective-permute-start | bytes 442376 | tf_op jit(solution)/shard_map/ppermute | solution.py:467
  54.9 0.0 collective-permute-start.13
  54.9 0.0 collective-permute-done.10.p3
  54.9 1.7 %collective-permute-start.14 = (f32[3,96,128]{2,1,0:T(8,128)S(1)}, f32[3,96,128]{2,1,0:T(8,128)S(1)}, u32[]{:S(2)}, u32[]{:S(2)}) collective-permute-start(f32[3,96,128]{2,1,0:T(8,128)S(1)} %get-tuple-element.68), channel_id=1, source_target_pairs={{0,2},{1,3},{2,0},{3,1},{4,6},{5,7},{6,4},{7,5},{8,10},{9,11},{10,... | collective-permute-start | bytes 442376 | tf_op jit(solution)/shard_map/ppermute | solution.py:467
  56.6 0.0 collective-permute-done.9.p2
  56.6 0.0 collective-permute-done.8.p1
  56.6 2.4 %third_flow.1 = (f32[3,4,96,128]{3,2,1,0:T(8,128)}, f32[3,96,128]{2,1,0:T(8,128)S(1)}, f32[3,96,128]{2,1,0:T(8,128)S(1)}, f32[32,8,128]{2,1,0:T(8,128)}) custom-call(f32[3,4,96,128]{3,2,1,0:T(8,128)S(1)} %copy-done.1, f32[5,3,96,128]{3,2,1,0:T(8,128)S(1)} %collective-permute-done.before_ref.fbefore_ref, ...), custom_call_target="tpu_custom_call" | custom-call | tf_op jit(solution)/shard_map/third_flow/pallas_call | solution.py:331
  59.0 0.0 copy-done.3
  59.0 0.0 copy-done.4
  59.1 11.0 %all-to-all-start = ((f32[32,8,128]{2,1,0:T(8,128)}), f32[32,8,128]{2,1,0:T(8,128)S(1)}, u32[]{:S(2)}, u32[]{:S(2)}) async-start(f32[32,8,128]{2,1,0:T(8,128)} %get-tuple-element.66), calls=%async_computation | async-start | bytes 262144 | tf_op jit(solution)/shard_map/all_to_all | solution.py:517
  70.1 0.0 collective-permute-done.15
  70.1 0.0 collective-permute-done.13
  70.1 0.0 collective-permute-done.14
  70.1 1.4 %collective-permute-start.16 = (f32[288,128]{1,0:T(8,128)S(1)}, f32[288,128]{1,0:T(8,128)S(1)}, u32[]{:S(2)}, u32[]{:S(2)}) collective-permute-start(f32[288,128]{1,0:T(8,128)S(1)} %bitcast.5), channel_id=1, source_target_pairs={{0,4},{1,5},{2,6},{3,7},{4,0},{5,1},{6,2},{7,3},{8,12},{9,13},{10,... | collective-permute-start | bytes 442376 | tf_op jit(solution)/shard_map/ppermute | solution.py:472
  71.5 1.9 %collective-permute-start.11 = (f32[3,96,128]{2,1,0:T(8,128)S(1)}, f32[3,96,128]{2,1,0:T(8,128)S(1)}, u32[]{:S(2)}, u32[]{:S(2)}) collective-permute-start(f32[3,96,128]{2,1,0:T(8,128)S(1)} %get-tuple-element.64), channel_id=1, source_target_pairs={{0,8},{8,16},{16,24},{24,32},{32,40},{40,48},{48,56},{56,64},{64,7... | collective-permute-start | bytes 442376 | tf_op jit(solution)/shard_map/ppermute | solution.py:457
  73.5 0.0 collective-permute-start.12
  73.5 5.7 %all-to-all-done.shared_ref = f32[32,8,128]{2,1,0:T(8,128)S(1)} async-done(((f32[32,8,128]{2,1,0:T(8,128)}), f32[32,8,128]{2,1,0:T(8,128)S(1)}, u32[]{:S(2)}, u32[]{:S(2)}) %all-to-all-start) | async-done | bytes 131104 | tf_op jit(solution)/shard_map/all_to_all | solution.py:517
  79.1 0.0 collective-permute-done.16
  79.2 1.4 %collective-permute-start.19 = (f32[288,128]{1,0:T(8,128)S(1)}, f32[288,128]{1,0:T(8,128)S(1)}, u32[]{:S(2)}, u32[]{:S(2)}) collective-permute-start(f32[288,128]{1,0:T(8,128)S(1)} %bitcast_add_fusion.p0), channel_id=1, source_target_pairs={{0,3},{1,0},{2,1},{3,2},{4,7},{5,4},{6,5},{7,6},{8,11},{9,8},{10,9... | collective-permute-start | bytes 442376 | tf_op jit(solution)/shard_map/ppermute | solution.py:467
  80.6 1.1 %collective-permute-start.18 = (f32[288,128]{1,0:T(8,128)S(1)}, f32[288,128]{1,0:T(8,128)S(1)}, u32[]{:S(2)}, u32[]{:S(2)}) collective-permute-start(f32[288,128]{1,0:T(8,128)S(1)} %bitcast_add_fusion.p0), channel_id=1, source_target_pairs={{0,2},{1,3},{2,0},{3,1},{4,6},{5,7},{6,4},{7,5},{8,10},{9,11},{10,... | collective-permute-start | bytes 442376 | tf_op jit(solution)/shard_map/ppermute | solution.py:467
  81.7 0.0 collective-permute-start.17
  81.7 0.0 collective-permute-done.11.sbefore_ref
  81.7 0.0 collective-permute-done.12.safter_ref
  81.7 6.2 %fourth_fields.1 = f32[4,3,4,96,128]{4,3,2,1,0:T(8,128)} custom-call(f32[4,3,4,96,128]{4,3,2,1,0:T(8,128)} %get-tuple-element.57.config_ref, f32[4,3,96,128]{3,2,1,0:T(8,128)} %copy-done.3, f32[4,3,96,128]{3,2,1,0:T(8,128)} %copy-done.4, f32[3,4,96,128]{3,2,1,0:T(8,128)} %get-tuple-element.63.start_ref, ...), custom_call_target="tpu_custom_call" | custom-call | tf_op jit(solution)/shard_map/fourth_fields/pallas_call | solution.py:371
  87.9 0.0 collective-permute-done.19.p3
  87.9 0.0 collective-permute-done.18.p2
  87.9 1.7 %collective-permute-done.17.p1 = f32[288,128]{1,0:T(8,128)S(1)} collective-permute-done((f32[288,128]{1,0:T(8,128)S(1)}, f32[288,128]{1,0:T(8,128)S(1)}, u32[]{:S(2)}, u32[]{:S(2)}) %collective-permute-start.17) | collective-permute-done | bytes 147488 | tf_op jit(solution)/shard_map/ppermute | solution.py:467
  89.6 2.6 %fifth_flow.1 = f32[3,4,96,128]{3,2,1,0:T(8,128)} custom-call(f32[3,4,96,128]{3,2,1,0:T(8,128)} %get-tuple-element.63.start_ref, f32[3,96,128]{2,1,0:T(8,128)S(1)} %collective-permute-done.11.sbefore_ref, f32[3,96,128]{2,1,0:T(8,128)S(1)} %collective-permute-done.12.safter_ref, f32[288,128]{1,0:T(8,128)S(1)} %bitcast_add_fusion.p0, ...), custom_call_target="tpu_custom_call" | custom-call | tf_op jit(solution)/shard_map/fifth_flow/pallas_call | solution.py:408
  (6 shorter events, 0.1 us)
Async XLA Ops:
  0.6 7.3 %copy-start.5 = (s32[4,2]{0,1:T(2,128)S(1)}, s32[4,2]{0,1:T(2,128)}, u32[]{:S(2)}) copy-start(s32[4,2]{0,1:T(2,128)} %param.5) | copy-start | bytes 100
  4.5 14.5 %copy-start = (f32[4,3,4,96,128]{4,3,2,1,0:T(8,128)S(1)}, f32[4,3,4,96,128]{4,3,2,1,0:T(8,128)}, u32[]{:S(2)}) copy-start(f32[4,3,4,96,128]{4,3,2,1,0:T(8,128)} %config_ref.3) | copy-start | bytes 7077892
  4.5 11.8 %collective-permute-start = (f32[5,3,96,128]{3,2,1,0:T(8,128)}, f32[5,3,96,128]{3,2,1,0:T(8,128)S(1)}, u32[]{:S(2)}, u32[]{:S(2)}) collective-permute-start(f32[5,3,96,128]{3,2,1,0:T(8,128)} %get-tuple-element.39), channel_id=1, source_target_pairs={{0,8},{8,16},{16,24},{24,32},{32,40},{40,48},{48,56},{56,64},{64,7... | collective-permute-start | bytes 2211848 | tf_op jit(solution)/shard_map/ppermute | solution.py:457
  7.6 11.4 %collective-permute-start.1 = (f32[5,3,96,128]{3,2,1,0:T(8,128)}, f32[5,3,96,128]{3,2,1,0:T(8,128)}, u32[]{:S(2)}, u32[]{:S(2)}) collective-permute-start(f32[5,3,96,128]{3,2,1,0:T(8,128)} %get-tuple-element.41), channel_id=1, source_target_pairs={{8,0},{16,8},{24,16},{32,24},{40,32},{48,40},{56,48},{64,56},{72,6... | collective-permute-start | bytes 2211848 | tf_op jit(solution)/shard_map/ppermute | solution.py:462
  13.2 13.7 %copy-start.1 = (f32[3,4,96,128]{3,2,1,0:T(8,128)S(1)}, f32[3,4,96,128]{3,2,1,0:T(8,128)}, u32[]{:S(2)}) copy-start(f32[3,4,96,128]{3,2,1,0:T(8,128)} %flow_ref.3) | copy-start | bytes 1769476
  22.1 13.6 %collective-permute-start.4 = (f32[3,96,128]{2,1,0:T(8,128)S(1)}, f32[3,96,128]{2,1,0:T(8,128)S(1)}, u32[]{:S(2)}, u32[]{:S(2)}) collective-permute-start(f32[3,96,128]{2,1,0:T(8,128)S(1)} %get-tuple-element.48), channel_id=1, source_target_pairs={{0,1},{1,2},{2,3},{3,0},{4,5},{5,6},{6,7},{7,4},{8,9},{9,10},{10,1... | collective-permute-start | bytes 442376 | tf_op jit(solution)/shard_map/ppermute | solution.py:467
  23.4 12.3 %collective-permute-start.5 = (f32[3,96,128]{2,1,0:T(8,128)S(1)}, f32[3,96,128]{2,1,0:T(8,128)S(1)}, u32[]{:S(2)}, u32[]{:S(2)}) collective-permute-start(f32[3,96,128]{2,1,0:T(8,128)S(1)} %get-tuple-element.50), channel_id=1, source_target_pairs={{0,2},{1,3},{2,0},{3,1},{4,6},{5,7},{6,4},{7,5},{8,10},{9,11},{10,... | collective-permute-start | bytes 442376 | tf_op jit(solution)/shard_map/ppermute | solution.py:467
  25.8 9.9 %collective-permute-start.6 = (f32[3,96,128]{2,1,0:T(8,128)S(1)}, f32[3,96,128]{2,1,0:T(8,128)S(1)}, u32[]{:S(2)}, u32[]{:S(2)}) collective-permute-start(f32[3,96,128]{2,1,0:T(8,128)S(1)} %get-tuple-element.52), channel_id=1, source_target_pairs={{0,3},{1,0},{2,1},{3,2},{4,7},{5,4},{6,5},{7,6},{8,11},{9,8},{10,9... | collective-permute-start | bytes 442376 | tf_op jit(solution)/shard_map/ppermute | solution.py:467
  32.0 18.0 %copy-start.2 = (f32[4,3,4,96,128]{4,3,2,1,0:T(8,128)S(1)}, f32[4,3,4,96,128]{4,3,2,1,0:T(8,128)}, u32[]{:S(2)}) copy-start(f32[4,3,4,96,128]{4,3,2,1,0:T(8,128)} %get-tuple-element.57.config_ref) | copy-start | bytes 7077892
  32.0 18.0 %collective-permute-start.2 = (f32[4,3,96,128]{3,2,1,0:T(8,128)S(1)}, f32[4,3,96,128]{3,2,1,0:T(8,128)S(1)}, u32[]{:S(2)}, u32[]{:S(2)}) collective-permute-start(f32[4,3,96,128]{3,2,1,0:T(8,128)S(1)} %get-tuple-element.46), channel_id=1, source_target_pairs={{0,8},{8,16},{16,24},{24,32},{32,40},{40,48},{48,56},{56,64},{64,7... | collective-permute-start | bytes 1769480 | tf_op jit(solution)/shard_map/ppermute | solution.py:457
  32.6 17.4 %collective-permute-start.3 = (f32[4,3,96,128]{3,2,1,0:T(8,128)S(1)}, f32[4,3,96,128]{3,2,1,0:T(8,128)S(1)}, u32[]{:S(2)}, u32[]{:S(2)}) collective-permute-start(f32[4,3,96,128]{3,2,1,0:T(8,128)S(1)} %get-tuple-element.47), channel_id=1, source_target_pairs={{8,0},{16,8},{24,16},{32,24},{40,32},{48,40},{56,48},{64,56},{72,6... | collective-permute-start | bytes 1769480 | tf_op jit(solution)/shard_map/ppermute | solution.py:462
  35.7 12.1 %collective-permute-start.7 = (f32[296,128]{1,0:T(8,128)S(1)}, f32[296,128]{1,0:T(8,128)S(1)}, u32[]{:S(2)}, u32[]{:S(2)}) collective-permute-start(f32[296,128]{1,0:T(8,128)S(1)} %pad_maximum_fusion), channel_id=1, source_target_pairs={{0,4},{1,5},{2,6},{3,7},{4,0},{5,1},{6,2},{7,3},{8,12},{9,13},{10,... | collective-permute-start | bytes 454664 | tf_op jit(solution)/shard_map/ppermute | solution.py:472
  47.8 7.1 %collective-permute-start.10 = (f32[296,128]{1,0:T(8,128)S(1)}, f32[296,128]{1,0:T(8,128)S(1)}, u32[]{:S(2)}, u32[]{:S(2)}) collective-permute-start(f32[296,128]{1,0:T(8,128)S(1)} %fusion.p0), channel_id=1, source_target_pairs={{0,3},{1,0},{2,1},{3,2},{4,7},{5,4},{6,5},{7,6},{8,11},{9,8},{10,9... | collective-permute-start | bytes 454664 | tf_op jit(solution)/shard_map/ppermute | solution.py:467
  47.9 8.7 %collective-permute-start.9 = (f32[296,128]{1,0:T(8,128)S(1)}, f32[296,128]{1,0:T(8,128)S(1)}, u32[]{:S(2)}, u32[]{:S(2)}) collective-permute-start(f32[296,128]{1,0:T(8,128)S(1)} %fusion.p0), channel_id=1, source_target_pairs={{0,2},{1,3},{2,0},{3,1},{4,6},{5,7},{6,4},{7,5},{8,10},{9,11},{10,... | collective-permute-start | bytes 454664 | tf_op jit(solution)/shard_map/ppermute | solution.py:467
  50.0 6.6 %collective-permute-start.8 = (f32[296,128]{1,0:T(8,128)S(1)}, f32[296,128]{1,0:T(8,128)S(1)}, u32[]{:S(2)}, u32[]{:S(2)}) collective-permute-start(f32[296,128]{1,0:T(8,128)S(1)} %fusion.p0), channel_id=1, source_target_pairs={{0,1},{1,2},{2,3},{3,0},{4,5},{5,6},{6,7},{7,4},{8,9},{9,10},{10,1... | collective-permute-start | bytes 454664 | tf_op jit(solution)/shard_map/ppermute | solution.py:467
  50.0 9.0 %copy-start.3 = (f32[4,3,96,128]{3,2,1,0:T(8,128)}, f32[4,3,96,128]{3,2,1,0:T(8,128)S(1)}, u32[]{:S(2)}) copy-start(f32[4,3,96,128]{3,2,1,0:T(8,128)S(1)} %collective-permute-done.2.before_ref) | copy-start | bytes 1769476
  50.0 9.0 %copy-start.4 = (f32[4,3,96,128]{3,2,1,0:T(8,128)}, f32[4,3,96,128]{3,2,1,0:T(8,128)S(1)}, u32[]{:S(2)}) copy-start(f32[4,3,96,128]{3,2,1,0:T(8,128)S(1)} %collective-permute-done.3.after_ref) | copy-start | bytes 1769476
  52.2 17.9 %collective-permute-start.15 = (f32[3,96,128]{2,1,0:T(8,128)}, f32[3,96,128]{2,1,0:T(8,128)S(1)}, u32[]{:S(2)}, u32[]{:S(2)}) collective-permute-start(f32[3,96,128]{2,1,0:T(8,128)} %get-tuple-element.69), channel_id=1, source_target_pairs={{0,3},{1,0},{2,1},{3,2},{4,7},{5,4},{6,5},{7,6},{8,11},{9,8},{10,9... | collective-permute-start | bytes 442376 | tf_op jit(solution)/shard_map/ppermute | solution.py:467
  54.9 15.2 %collective-permute-start.13 = (f32[3,96,128]{2,1,0:T(8,128)S(1)}, f32[3,96,128]{2,1,0:T(8,128)S(1)}, u32[]{:S(2)}, u32[]{:S(2)}) collective-permute-start(f32[3,96,128]{2,1,0:T(8,128)S(1)} %get-tuple-element.67), channel_id=1, source_target_pairs={{0,1},{1,2},{2,3},{3,0},{4,5},{5,6},{6,7},{7,4},{8,9},{9,10},{10,1... | collective-permute-start | bytes 442376 | tf_op jit(solution)/shard_map/ppermute | solution.py:467
  54.9 15.2 %collective-permute-start.14 = (f32[3,96,128]{2,1,0:T(8,128)S(1)}, f32[3,96,128]{2,1,0:T(8,128)S(1)}, u32[]{:S(2)}, u32[]{:S(2)}) collective-permute-start(f32[3,96,128]{2,1,0:T(8,128)S(1)} %get-tuple-element.68), channel_id=1, source_target_pairs={{0,2},{1,3},{2,0},{3,1},{4,6},{5,7},{6,4},{7,5},{8,10},{9,11},{10,... | collective-permute-start | bytes 442376 | tf_op jit(solution)/shard_map/ppermute | solution.py:467
  59.1 20.1 %all-to-all-start = ((f32[32,8,128]{2,1,0:T(8,128)}), f32[32,8,128]{2,1,0:T(8,128)S(1)}, u32[]{:S(2)}, u32[]{:S(2)}) async-start(f32[32,8,128]{2,1,0:T(8,128)} %get-tuple-element.66), calls=%async_computation | async-start | bytes 262144 | tf_op jit(solution)/shard_map/all_to_all | solution.py:517
  70.1 9.0 %collective-permute-start.16 = (f32[288,128]{1,0:T(8,128)S(1)}, f32[288,128]{1,0:T(8,128)S(1)}, u32[]{:S(2)}, u32[]{:S(2)}) collective-permute-start(f32[288,128]{1,0:T(8,128)S(1)} %bitcast.5), channel_id=1, source_target_pairs={{0,4},{1,5},{2,6},{3,7},{4,0},{5,1},{6,2},{7,3},{8,12},{9,13},{10,... | collective-permute-start | bytes 442376 | tf_op jit(solution)/shard_map/ppermute | solution.py:472
  71.5 10.1 %collective-permute-start.11 = (f32[3,96,128]{2,1,0:T(8,128)S(1)}, f32[3,96,128]{2,1,0:T(8,128)S(1)}, u32[]{:S(2)}, u32[]{:S(2)}) collective-permute-start(f32[3,96,128]{2,1,0:T(8,128)S(1)} %get-tuple-element.64), channel_id=1, source_target_pairs={{0,8},{8,16},{16,24},{24,32},{32,40},{40,48},{48,56},{56,64},{64,7... | collective-permute-start | bytes 442376 | tf_op jit(solution)/shard_map/ppermute | solution.py:457
  73.5 8.2 %collective-permute-start.12 = (f32[3,96,128]{2,1,0:T(8,128)S(1)}, f32[3,96,128]{2,1,0:T(8,128)S(1)}, u32[]{:S(2)}, u32[]{:S(2)}) collective-permute-start(f32[3,96,128]{2,1,0:T(8,128)S(1)} %get-tuple-element.65), channel_id=1, source_target_pairs={{8,0},{16,8},{24,16},{32,24},{40,32},{48,40},{56,48},{64,56},{72,6... | collective-permute-start | bytes 442376 | tf_op jit(solution)/shard_map/ppermute | solution.py:462
  79.2 8.8 %collective-permute-start.19 = (f32[288,128]{1,0:T(8,128)S(1)}, f32[288,128]{1,0:T(8,128)S(1)}, u32[]{:S(2)}, u32[]{:S(2)}) collective-permute-start(f32[288,128]{1,0:T(8,128)S(1)} %bitcast_add_fusion.p0), channel_id=1, source_target_pairs={{0,3},{1,0},{2,1},{3,2},{4,7},{5,4},{6,5},{7,6},{8,11},{9,8},{10,9... | collective-permute-start | bytes 442376 | tf_op jit(solution)/shard_map/ppermute | solution.py:467
  80.6 7.3 %collective-permute-start.18 = (f32[288,128]{1,0:T(8,128)S(1)}, f32[288,128]{1,0:T(8,128)S(1)}, u32[]{:S(2)}, u32[]{:S(2)}) collective-permute-start(f32[288,128]{1,0:T(8,128)S(1)} %bitcast_add_fusion.p0), channel_id=1, source_target_pairs={{0,2},{1,3},{2,0},{3,1},{4,6},{5,7},{6,4},{7,5},{8,10},{9,11},{10,... | collective-permute-start | bytes 442376 | tf_op jit(solution)/shard_map/ppermute | solution.py:467
  81.7 8.0 %collective-permute-start.17 = (f32[288,128]{1,0:T(8,128)S(1)}, f32[288,128]{1,0:T(8,128)S(1)}, u32[]{:S(2)}, u32[]{:S(2)}) collective-permute-start(f32[288,128]{1,0:T(8,128)S(1)} %bitcast_add_fusion.p0), channel_id=1, source_target_pairs={{0,1},{1,2},{2,3},{3,0},{4,5},{5,6},{6,7},{7,4},{8,9},{9,10},{10,1... | collective-permute-start | bytes 442376 | tf_op jit(solution)/shard_map/ppermute | solution.py:467

commit v3 on v2

--- a/solution.py
+++ b/solution.py
@@ -123,59 +123,79 @@
     return lax.rem(lax.axis_index("row"), 4)
 
 
-def div_kernel(total_fields, config_ref, before_ref, after_ref, *refs):
-    outs, stress_ref, rim_ref, div_ref = refs[:4], refs[4], refs[5], refs[6]
+def inner_kernel(total_fields, config_ref, stress_ref):
     k = pl.program_id(0)
-    _, _, width, rows, depth = config_ref.shape
+
+    def add(first):
+        for x in range(config_ref.shape[2]):
+            q = [config_ref[0, i, x] for i in range(3)]
+            spring = spring_of(q) * (0.5 / total_fields)
+            weighted = [spring * q[i] for i in range(3)]
+            for p, (i, j) in enumerate(PAIRS):
+                term = weighted[i] * q[j]
+                stress_ref[p, x] = term if first else stress_ref[p, x] + term
 
     @pl.when(k == 0)
     def _():
-        stress_ref[...] = jnp.zeros_like(stress_ref)
-        rim_ref[...] = jnp.zeros_like(rim_ref)
-
+        add(True)
+
+    @pl.when(k > 0)
+    def _():
+        add(False)
+
+
+def inner_stress(config, total_fields):
+    fields, _, width, rows, depth = config.shape
+    stress = jax.ShapeDtypeStruct((6, width, rows, depth), jnp.float32)
+    return pl.pallas_call(
+        functools.partial(inner_kernel, total_fields),
+        grid=(fields,),
+        out_shape=stress,
+        in_specs=[field_block(config.shape)],
+        out_specs=whole_block(stress.shape),
+        compiler_params=params(),
+        name="inner_stress",
+    )(config)
+
+
+def parts_kernel(total_fields, fields, stress_ref, before_ref, after_ref, *refs):
+    outs, rim_ref = refs[:4], refs[4]
+    width = stress_ref.shape[1]
+    for side, ref in enumerate((before_ref, after_ref)):
+        totals = None
+        for k in range(fields):
+            q = [ref[k, i] for i in range(3)]
+            weighted = spring_of(q) * (0.5 / total_fields) * q[0]
+            terms = [weighted * q[i] for i in range(3)]
+            totals = terms if k == 0 else [t + u for t, u in zip(totals, terms)]
+        for i in range(3):
+            rim_ref[(width + 1) * side, i] = totals[i]
     for x in range(width):
-        q = [config_ref[0, i, x] for i in range(3)]
-        spring = spring_of(q) * (0.5 / total_fields)
-        weighted = [spring * q[i] for i in range(3)]
-        for p, (i, j) in enumerate(PAIRS):
-            stress_ref[p, x] += weighted[i] * q[j]
-    for side, ref in enumerate((before_ref, after_ref)):
-        q = [ref[0, i] for i in range(3)]
-        weighted = spring_of(q) * (0.5 / total_fields) * q[0]
-        for i in range(3):
-            rim_ref[side, i] += weighted * q[i]
-
-    @pl.when(k == pl.num_programs(0) - 1)
-    def _():
-        for x in range(width):
-            for i in range(3):
-                sy = stress_ref[PLACE[i][1], x]
-                sz = stress_ref[PLACE[i][2], x]
-                above = stress_ref[PLACE[i][0], x + 1] if x + 1 < width else rim_ref[1, i]
-                below = stress_ref[PLACE[i][0], x - 1] if x > 0 else rim_ref[0, i]
-                div_ref[x, i] = (above - below) + (up_y(sy) - down_y(sy)) + (up_z(sz) - down_z(sz))
-        place = quad_place()
-        for n, out in enumerate(outs):
-            out[...] = div_ref[lax.rem(place + n, 4)]
-
-
-def stress_parts(config, before, after, total_fields):
-    fields, _, width, rows, depth = config.shape
+        for i in range(3):
+            rim_ref[x + 1, i] = stress_ref[PLACE[i][0], x]
+    place = quad_place()
+    for n, out in enumerate(outs):
+        x = lax.rem(place + n, 4)
+        for i in range(3):
+            sy = stress_ref[PLACE[i][1], x]
+            sz = stress_ref[PLACE[i][2], x]
+            out[i] = (rim_ref[x + 2, i] - rim_ref[x, i]) + (up_y(sy) - down_y(sy)) + (up_z(sz) - down_z(sz))
+
+
+def stress_parts(stress, before, after, fields, total_fields):
+    _, width, rows, depth = stress.shape
     part = jax.ShapeDtypeStruct((3, rows, depth), jnp.float32)
-    return pl.pallas_call(
-        functools.partial(div_kernel, total_fields),
-        grid=(fields,),
+    rim = (fields,) + before.shape[1:]
+    return pl.pallas_call(
+        functools.partial(parts_kernel, total_fields, fields),
+        grid=(1,),
         out_shape=[part] * 4,
-        in_specs=[field_block(config.shape), rim_block(before.shape), rim_block(after.shape)],
+        in_specs=[whole_block(stress.shape), whole_block(rim), whole_block(rim)],
         out_specs=[whole_block(part.shape)] * 4,
-        scratch_shapes=[
-            pltpu.VMEM((6, width, rows, depth), jnp.float32),
-            pltpu.VMEM((2, 3, rows, depth), jnp.float32),
-            pltpu.VMEM((width, 3, rows, depth), jnp.float32),
-        ],
+        scratch_shapes=[pltpu.VMEM((width + 2, 3, rows, depth), jnp.float32)],
         compiler_params=params(),
         name="stress_parts",
-    )(config, before, after)
+    )(stress, before, after)
 
 
 def fill_slopes(flow_at, slope_ref, width):
@@ -244,7 +264,7 @@
     return pl.pallas_call(
         functools.partial(second_kernel, total_fields),
         grid=(fields,),
-        out_shape=[pltpu.HBM(config.shape, jnp.float32), rim, rim, wall],
+        out_shape=[jax.ShapeDtypeStruct(config.shape, jnp.float32), rim, rim, wall],
         in_specs=[
             field_block(config.shape), rim_block(before.shape), rim_block(after.shape), whole_block(flow.shape),
             rim_block(before.shape, fields), rim_block(after.shape, fields), field_block(noise.shape),
@@ -279,9 +299,12 @@
             div_ref[at, i] = part[i * rows:(i + 1) * rows]
 
 
-def third_kernel(flow_ref, fbefore_ref, fafter_ref, p0, p1, p2, p3, start_ref, first_ref, last_ref, sums_ref, div_ref):
+def third_kernel(flow_ref, fbefore_ref, fafter_ref, p0, p1, p2, p3, start_ref, first_ref, last_ref, sums_ref, div_ref, wall_ref):
     _, width, rows, depth = flow_ref.shape
     gather_parts((p0, p1, p2, p3), div_ref)
+    place = quad_place()
+    for n, part in enumerate((p0, p1, p2, p3)):
+        wall_ref[lax.rem(place + 4 - n, 4)] = part[3 * rows:]
 
     def at(i, x):
         if x < 0:
@@ -311,7 +334,7 @@
         jnp.sum(total, axis=0, keepdims=True),
         jnp.sum(bend, axis=0, keepdims=True) + viscosity * edge,
         0.5 * gain,
-        jnp.sum(sum(p[3 * rows:] for p in (p0, p1, p2, p3)), axis=0, keepdims=True),
+        jnp.sum((wall_ref[0] + wall_ref[1]) + (wall_ref[2] + wall_ref[3]), axis=0, keepdims=True),
     ]
     tile = jnp.zeros((8, depth), jnp.float32)
     for n, value in enumerate(sums):
@@ -331,11 +354,11 @@
     return pl.pallas_call(
         third_kernel,
         grid=(1,),
-        out_shape=[pltpu.HBM(flow.shape, jnp.float32), end, end, sums],
+        out_shape=[jax.ShapeDtypeStruct(flow.shape, jnp.float32), end, end, sums],
         in_specs=[whole_block(flow.shape), rim_block(left.shape, at), rim_block(right.shape, at)]
         + [whole_block(parts[0].shape)] * 4,
         out_specs=[whole_block(flow.shape), whole_block(end.shape), whole_block(end.shape), whole_block(sums.shape)],
-        scratch_shapes=[pltpu.VMEM((width, 3, rows, depth), jnp.float32)],
+        scratch_shapes=[pltpu.VMEM((width, 3, rows, depth), jnp.float32), pltpu.VMEM((4, 8, depth), jnp.float32)],
         compiler_params=params(),
         name="third_flow",
     )(flow, left, right, *parts)
@@ -496,9 +519,10 @@
     head, tail = pack_ends(in_hbm(config), in_hbm(flow))
     left, right = from_left(tail), from_right(head)
     noise = draw_noise(keys, 0, total_x, config.shape)
-    left, right = after(left, noise), after(right, noise)
-
-    parts = stress_parts(config, left, right, total_fields)
+    inner = inner_stress(after(config, noise), total_fields)
+    left, right = after(left, inner), after(right, inner)
+
+    parts = stress_parts(inner, left, right, fields, total_fields)
     got = [quad_shift(parts[n], n) for n in (1, 2, 3)]
     config, first, last, wall = second_fields(config, after(left, parts[0]), right, flow, noise, total_fields)
     before, behind = from_left(last), from_right(first)
@@ -506,22 +530,23 @@
     own = jnp.concatenate([flat(parts[0] + got[0] + got[1] + got[2]), wall], axis=0)
     swap = pair_swap(own, 4)
     later = draw_noise(after(keys, own), 1, total_x, config.shape)
-    own = own + after(swap, later)
+    inner = inner_stress(after(config, later), total_fields)
+    own = own + after(swap, inner)
     div = [own] + [quad_shift(own, n) for n in (1, 2, 3)]
 
-    parts = stress_parts(after(config, own), before, behind, total_fields)
+    parts = stress_parts(inner, after(before, own), behind, fields, total_fields)
     got = [quad_shift(parts[n], n) for n in (1, 2, 3)]
 
     start, first, last, sums = third_flow(flow, left, right, [after(d, parts[0]) for d in div], slabs)
     sleft, sright = from_left(last), from_right(first)
     shared = lax.all_to_all(sums, "gx", 0, 0)
     own = flat(parts[0] + got[0] + got[1] + after(got[2], start))
-    own = own + after(pair_swap(own, 4), shared)
-    next_div = [own] + [quad_shift(own, n) for n in (1, 2, 3)]
+    own = own + pair_swap(own, 4)
+    next_div = [own, quad_shift(after(own, shared), 1), quad_shift(own, 2), quad_shift(own, 3)]
 
     walls = total_x * depth
     config = fourth_fields(in_hbm(config), in_hbm(before), in_hbm(behind), in_hbm(start), sleft, sright, in_hbm(later), shared, walls, cells)
-    flow = fifth_flow(in_hbm(start), sleft, sright, [after(d, config) for d in next_div], shared, walls, cells)
+    flow = fifth_flow(start, sleft, sright, [after(d, config) for d in next_div], shared, walls, cells)
     return config, flow
 
 

time: 93.3 us -> 91.5 us (0.981)
  Pallas kernels: 36.6 us -> 32.7 us
    ppermute x2, starting transfers between devices: 4.1 us -> 8.13 us  [pair_swap(): return lax.ppermute(value, 'row', [(i, i ^ bit) for i in range(count)])]
    all_to_all x1, starting transfers between devices: 11 us -> 7.3 us  [shards(): shared = lax.all_to_all(sums, 'gx', 0, 0)]
    ppermute x12, waiting for transfers between devices: 1.72 us -> 4.25 us  [quad_shift(): lax.ppermute(value, 'row', [(i, i - i % 4 + (i + by) % 4) for i in range(...]
    pallas_call x3 -> x5, Pallas kernels: 7.67 us -> 5.92 us  [the longest x1 2.33 us: third_flow(): pl.pallas_call(third_kernel, grid=(1,), out_shape=[jax.ShapeDtypeStruct(f...]
    pallas_call x1, Pallas kernels: 2.59 us -> 1.53 us  [fifth_flow(): pl.pallas_call(functools.partial(fifth_kernel, walls, cells), grid=(1,),...]
    pallas_call x1, Pallas kernels: 5.07 us -> 4.01 us  [second_fields(): pl.pallas_call(functools.partial(second_kernel, total_fields), grid=(fiel...]
    all_to_all x1, waiting for transfers between devices: 5.69 us -> 4.73 us  [shards(): shared = lax.all_to_all(sums, 'gx', 0, 0)]
  transfers between devices with their start and end apart: 21 -> 21, of which waited for: 5 -> 7; matrix products, arithmetic and copies ran while one was open for 0% -> 0% of each run, Pallas kernels for 29% -> 29%
where the time goes in v3:
time: 91.5 us; the launch traced here: 89.9 us
  starting transfers between devices  38.7 us (42%)
  Pallas kernels  32.7 us (36%)
  waiting for transfers between devices  16.5 us (18%)
  local copies, waits for them, and re-layouts  1.04 us (1%)
    ppermute x12, starting transfers between devices, quad_shift(): lax.ppermute(value, 'row', [(i, i - i % 4 + (i + by) % 4) for i in range(...  14.4 us
    pallas_call x2, Pallas kernels, draw_noise(): pl.pallas_call(functools.partial(noise_kernel, step, total_x), grid=(fiel...  11.2 us
    ppermute x2, starting transfers between devices, pair_swap(): return lax.ppermute(value, 'row', [(i, i ^ bit) for i in range(count)])  8.13 us
    all_to_all x1, starting transfers between devices, shards(): shared = lax.all_to_all(sums, 'gx', 0, 0)  7.3 us
    pallas_call x1, Pallas kernels, fourth_fields(): pl.pallas_call(functools.partial(fourth_kernel, walls, cells), grid=(fiel...  6.24 us
    ppermute x3, starting transfers between devices, from_left(): lax.ppermute(value, 'gx', [(i, (i + 1) % count) for i in range(count)])  5.41 us
    all_to_all x1, waiting for transfers between devices, shards(): shared = lax.all_to_all(sums, 'gx', 0, 0)  4.73 us
    ppermute x12, waiting for transfers between devices, quad_shift(): lax.ppermute(value, 'row', [(i, i - i % 4 + (i + by) % 4) for i in range(...  4.25 us
  transfers between devices with their start and end apart: 21, of which 7 were waited for; matrix products, arithmetic and copies ran while one was open for 0% of the time, Pallas kernels for 29%

profile of v3, /device:TPU:1, one launch (start us, length us, event | category | flops | bytes accessed | tf_op | source)
XLA Modules:
  0.0 89.9 jit_solution(2978454942604380231)
XLA Ops:
  0.6 0.0 copy-start.7
  0.6 3.9 %pack_ends.1 = (f32[5,3,96,128]{3,2,1,0:T(8,128)}, f32[5,3,96,128]{3,2,1,0:T(8,128)}) custom-call(f32[4,3,4,96,128]{4,3,2,1,0:T(8,128)} %config_ref.2, f32[4,3,4,96,128]{4,3,2,1,0:T(8,128)} %config_ref.2, f32[3,4,96,128]{3,2,1,0:T(8,128)} %flow_ref.3, f32[3,4,96,128]{3,2,1,0:T(8,128)} %flow_ref.3), custom_call_target="tpu_custom_call" | custom-call | tf_op jit(solution)/shard_map/pack_ends/pallas_call | solution.py:467
  4.5 3.1 %collective-permute-start = (f32[5,3,96,128]{3,2,1,0:T(8,128)}, f32[5,3,96,128]{3,2,1,0:T(8,128)S(1)}, u32[]{:S(2)}, u32[]{:S(2)}) collective-permute-start(f32[5,3,96,128]{3,2,1,0:T(8,128)} %get-tuple-element.41), channel_id=1, source_target_pairs={{0,8},{8,16},{16,24},{24,32},{32,40},{40,48},{48,56},{56,64},{64,7... | collective-permute-start | bytes 2211848 | tf_op jit(solution)/shard_map/ppermute | solution.py:480
  7.6 0.3 collective-permute-start.1
  7.9 0.0 copy-done.7
  7.9 0.1 copy.6
  8.0 0.1 reshape.13.keys_ref
  8.1 5.2 %draw_noise.2.noise_ref = f32[4,3,4,96,128]{4,3,2,1,0:T(8,128)S(1)} custom-call(s32[8]{0:T(128)S(1)} %reshape.13.keys_ref), custom_call_target="tpu_custom_call" | custom-call | tf_op jit(solution)/shard_map/draw_noise/pallas_call | solution.py:74
  13.2 0.0 copy-done
  13.3 0.0 copy-start.1
  13.3 0.7 inner_stress.2.stress_ref
  14.0 2.3 %collective-permute-done.before_ref.fbefore_ref = f32[5,3,96,128]{3,2,1,0:T(8,128)S(1)} collective-permute-done((f32[5,3,96,128]{3,2,1,0:T(8,128)}, f32[5,3,96,128]{3,2,1,0:T(8,128)S(1)}, u32[]{:S(2)}, u32[]{:S(2)}) %collective-permute-start) | collective-permute-done | bytes 737312 | tf_op jit(solution)/shard_map/ppermute | solution.py:480
  16.3 2.7 %collective-permute-done.1.after_ref.fafter_ref = f32[5,3,96,128]{3,2,1,0:T(8,128)} collective-permute-done((f32[5,3,96,128]{3,2,1,0:T(8,128)}, f32[5,3,96,128]{3,2,1,0:T(8,128)}, u32[]{:S(2)}, u32[]{:S(2)}) %collective-permute-start.1) | collective-permute-done | bytes 737312 | tf_op jit(solution)/shard_map/ppermute | solution.py:485
  19.0 1.6 %stress_parts.2 = (f32[3,96,128]{2,1,0:T(8,128)S(1)}, f32[3,96,128]{2,1,0:T(8,128)S(1)}, f32[3,96,128]{2,1,0:T(8,128)S(1)}, f32[3,96,128]{2,1,0:T(8,128)S(1)}) custom-call(f32[6,4,96,128]{3,2,1,0:T(8,128)S(1)} %inner_stress.2.stress_ref, f32[5,3,96,128]{3,2,1,0:T(8,128)S(1)} %collective-permute-done.before_ref.fbefore_ref, ...), custom_call_target="tpu_custom_call" | custom-call | tf_op jit(solution)/shard_map/stress_parts/pallas_call | solution.py:189
  20.6 1.3 %collective-permute-start.4 = (f32[3,96,128]{2,1,0:T(8,128)S(1)}, f32[3,96,128]{2,1,0:T(8,128)S(1)}, u32[]{:S(2)}, u32[]{:S(2)}) collective-permute-start(f32[3,96,128]{2,1,0:T(8,128)S(1)} %get-tuple-element.51), channel_id=1, source_target_pairs={{0,1},{1,2},{2,3},{3,0},{4,5},{5,6},{6,7},{7,4},{8,9},{9,10},{10,1... | collective-permute-start | bytes 442376 | tf_op jit(solution)/shard_map/ppermute | solution.py:490
  21.9 2.5 %collective-permute-start.5 = (f32[3,96,128]{2,1,0:T(8,128)S(1)}, f32[3,96,128]{2,1,0:T(8,128)S(1)}, u32[]{:S(2)}, u32[]{:S(2)}) collective-permute-start(f32[3,96,128]{2,1,0:T(8,128)S(1)} %get-tuple-element.53), channel_id=1, source_target_pairs={{0,2},{1,3},{2,0},{3,1},{4,6},{5,7},{6,4},{7,5},{8,10},{9,11},{10,... | collective-permute-start | bytes 442376 | tf_op jit(solution)/shard_map/ppermute | solution.py:490
  24.3 1.1 %collective-permute-start.6 = (f32[3,96,128]{2,1,0:T(8,128)S(1)}, f32[3,96,128]{2,1,0:T(8,128)S(1)}, u32[]{:S(2)}, u32[]{:S(2)}) collective-permute-start(f32[3,96,128]{2,1,0:T(8,128)S(1)} %get-tuple-element.55), channel_id=1, source_target_pairs={{0,3},{1,0},{2,1},{3,2},{4,7},{5,4},{6,5},{7,6},{8,11},{9,8},{10,9... | collective-permute-start | bytes 442376 | tf_op jit(solution)/shard_map/ppermute | solution.py:490
  25.5 0.0 copy-done.1
  25.5 4.0 %second_fields.1 = (f32[4,3,4,96,128]{4,3,2,1,0:T(8,128)S(1)}, f32[4,3,96,128]{3,2,1,0:T(8,128)S(1)}, f32[4,3,96,128]{3,2,1,0:T(8,128)S(1)}, f32[8,128]{1,0:T(8,128)S(1)}) custom-call(f32[4,3,4,96,128]{4,3,2,1,0:T(8,128)S(1)} %copy-done, f32[5,3,96,128]{3,2,1,0:T(8,128)S(1)} %collective-permute-done.before_ref.fbefore_ref, ...), custom_call_target="tpu_custom_call" | custom-call | tf_op jit(solution)/shard_map/second_fields/pallas_call | solution.py:264
  29.5 0.0 copy-start.2
  29.5 0.6 collective-permute-start.2
  30.1 3.2 %collective-permute-start.3 = (f32[4,3,96,128]{3,2,1,0:T(8,128)S(1)}, f32[4,3,96,128]{3,2,1,0:T(8,128)S(1)}, u32[]{:S(2)}, u32[]{:S(2)}) collective-permute-start(f32[4,3,96,128]{3,2,1,0:T(8,128)S(1)} %get-tuple-element.50), channel_id=1, source_target_pairs={{8,0},{16,8},{24,16},{32,24},{40,32},{48,40},{56,48},{64,56},{72,6... | collective-permute-start | bytes 1769480 | tf_op jit(solution)/shard_map/ppermute | solution.py:485
  33.3 0.0 collective-permute-done.4
  33.3 0.0 collective-permute-done.5
  33.3 0.0 collective-permute-done.6
  33.4 2.7 %collective-permute-start.7 = (f32[296,128]{1,0:T(8,128)S(1)}, f32[296,128]{1,0:T(8,128)S(1)}, u32[]{:S(2)}, u32[]{:S(2)}) collective-permute-start(f32[296,128]{1,0:T(8,128)S(1)} %pad_maximum_fusion), channel_id=1, source_target_pairs={{0,4},{1,5},{2,6},{3,7},{4,0},{5,1},{6,2},{7,3},{8,12},{9,13},{10,... | collective-permute-start | bytes 454664 | tf_op jit(solution)/shard_map/ppermute | solution.py:495
  36.1 6.0 %draw_noise.3.noise_ref = f32[4,3,4,96,128]{4,3,2,1,0:T(8,128)} custom-call(s32[8]{0:T(128)S(1)} %reshape.13.keys_ref), custom_call_target="tpu_custom_call" | custom-call | tf_op jit(solution)/shard_map/draw_noise/pallas_call | solution.py:74
  42.1 0.7 inner_stress.3.stress_ref
  42.8 2.5 %collective-permute-done.7 = f32[296,128]{1,0:T(8,128)S(1)} collective-permute-done((f32[296,128]{1,0:T(8,128)S(1)}, f32[296,128]{1,0:T(8,128)S(1)}, u32[]{:S(2)}, u32[]{:S(2)}) %collective-permute-start.7) | collective-permute-done | bytes 151584 | tf_op jit(solution)/shard_map/ppermute | solution.py:495
  45.4 0.1 collective-permute-start.10
  45.4 2.1 %collective-permute-start.9 = (f32[296,128]{1,0:T(8,128)S(1)}, f32[296,128]{1,0:T(8,128)S(1)}, u32[]{:S(2)}, u32[]{:S(2)}) collective-permute-start(f32[296,128]{1,0:T(8,128)S(1)} %fusion.p0), channel_id=1, source_target_pairs={{0,2},{1,3},{2,0},{3,1},{4,6},{5,7},{6,4},{7,5},{8,10},{9,11},{10,... | collective-permute-start | bytes 454664 | tf_op jit(solution)/shard_map/ppermute | solution.py:490
  47.5 0.0 collective-permute-start.8
  47.6 0.0 collective-permute-done.2.before_ref
  47.6 0.0 collective-permute-done.3.after_ref
  47.6 0.5 stress_parts.3
  48.1 2.8 %collective-permute-start.15 = (f32[3,96,128]{2,1,0:T(8,128)S(1)}, f32[3,96,128]{2,1,0:T(8,128)S(1)}, u32[]{:S(2)}, u32[]{:S(2)}) collective-permute-start(f32[3,96,128]{2,1,0:T(8,128)S(1)} %get-tuple-element.73), channel_id=1, source_target_pairs={{0,3},{1,0},{2,1},{3,2},{4,7},{5,4},{6,5},{7,6},{8,11},{9,8},{10,9... | collective-permute-start | bytes 442376 | tf_op jit(solution)/shard_map/ppermute | solution.py:490
  50.9 0.0 collective-permute-start.13
  50.9 0.0 collective-permute-done.10.p3
  50.9 1.7 %collective-permute-start.14 = (f32[3,96,128]{2,1,0:T(8,128)S(1)}, f32[3,96,128]{2,1,0:T(8,128)S(1)}, u32[]{:S(2)}, u32[]{:S(2)}) collective-permute-start(f32[3,96,128]{2,1,0:T(8,128)S(1)} %get-tuple-element.72), channel_id=1, source_target_pairs={{0,2},{1,3},{2,0},{3,1},{4,6},{5,7},{6,4},{7,5},{8,10},{9,11},{10,... | collective-permute-start | bytes 442376 | tf_op jit(solution)/shard_map/ppermute | solution.py:490
  52.6 0.0 collective-permute-done.9.p2
  52.6 0.9 collective-permute-done.8.p1
  53.5 2.3 %third_flow.1 = (f32[3,4,96,128]{3,2,1,0:T(8,128)S(1)}, f32[3,96,128]{2,1,0:T(8,128)S(1)}, f32[3,96,128]{2,1,0:T(8,128)S(1)}, f32[32,8,128]{2,1,0:T(8,128)}) custom-call(f32[3,4,96,128]{3,2,1,0:T(8,128)S(1)} %copy-done.1, f32[5,3,96,128]{3,2,1,0:T(8,128)S(1)} %collective-permute-done.before_ref.fbefore_ref, ...), custom_call_target="tpu_custom_call" | custom-call | tf_op jit(solution)/shard_map/third_flow/pallas_call | solution.py:354
  55.8 0.0 copy-done.4
  55.8 0.8 copy-done.5
  56.6 0.0 collective-permute-done.15
  56.6 3.1 %collective-permute-done.13 = f32[3,96,128]{2,1,0:T(8,128)S(1)} collective-permute-done((f32[3,96,128]{2,1,0:T(8,128)S(1)}, f32[3,96,128]{2,1,0:T(8,128)S(1)}, u32[]{:S(2)}, u32[]{:S(2)}) %collective-permute-start.13) | collective-permute-done | bytes 147488 | tf_op jit(solution)/shard_map/ppermute | solution.py:490
  59.7 0.2 collective-permute-done.14
  60.0 5.4 %collective-permute-start.16 = (f32[288,128]{1,0:T(8,128)S(1)}, f32[288,128]{1,0:T(8,128)S(1)}, u32[]{:S(2)}, u32[]{:S(2)}) collective-permute-start(f32[288,128]{1,0:T(8,128)S(1)} %bitcast.5), channel_id=1, source_target_pairs={{0,4},{1,5},{2,6},{3,7},{4,0},{5,1},{6,2},{7,3},{8,12},{9,13},{10,... | collective-permute-start | bytes 442376 | tf_op jit(solution)/shard_map/ppermute | solution.py:495
  65.4 7.3 %all-to-all-start = ((f32[32,8,128]{2,1,0:T(8,128)}), f32[32,8,128]{2,1,0:T(8,128)S(1)}, u32[]{:S(2)}, u32[]{:S(2)}) async-start(f32[32,8,128]{2,1,0:T(8,128)} %get-tuple-element.70), calls=%async_computation | async-start | bytes 262144 | tf_op jit(solution)/shard_map/all_to_all | solution.py:542
  72.7 1.7 %collective-permute-start.11 = (f32[3,96,128]{2,1,0:T(8,128)S(1)}, f32[3,96,128]{2,1,0:T(8,128)S(1)}, u32[]{:S(2)}, u32[]{:S(2)}) collective-permute-start(f32[3,96,128]{2,1,0:T(8,128)S(1)} %get-tuple-element.68), channel_id=1, source_target_pairs={{0,8},{8,16},{16,24},{24,32},{32,40},{40,48},{48,56},{56,64},{64,7... | collective-permute-start | bytes 442376 | tf_op jit(solution)/shard_map/ppermute | solution.py:480
  74.5 0.0 collective-permute-start.12
  74.5 0.0 collective-permute-done.16
  74.5 0.2 collective-permute-start.19
  74.7 2.4 %collective-permute-start.18 = (f32[288,128]{1,0:T(8,128)S(1)}, f32[288,128]{1,0:T(8,128)S(1)}, u32[]{:S(2)}, u32[]{:S(2)}) collective-permute-start(f32[288,128]{1,0:T(8,128)S(1)} %bitcast_add_fusion.p0), channel_id=1, source_target_pairs={{0,2},{1,3},{2,0},{3,1},{4,6},{5,7},{6,4},{7,5},{8,10},{9,11},{10,... | collective-permute-start | bytes 442376 | tf_op jit(solution)/shard_map/ppermute | solution.py:490
  77.1 4.7 %all-to-all-done.shared_ref = f32[32,8,128]{2,1,0:T(8,128)S(1)} async-done(((f32[32,8,128]{2,1,0:T(8,128)}), f32[32,8,128]{2,1,0:T(8,128)S(1)}, u32[]{:S(2)}, u32[]{:S(2)}) %all-to-all-start) | async-done | bytes 131104 | tf_op jit(solution)/shard_map/all_to_all | solution.py:542
  81.8 0.3 collective-permute-start.17
  82.1 0.0 collective-permute-done.11.sbefore_ref
  82.1 0.0 collective-permute-done.12.safter_ref
  82.1 6.2 %fourth_fields.1 = f32[4,3,4,96,128]{4,3,2,1,0:T(8,128)} custom-call(f32[4,3,4,96,128]{4,3,2,1,0:T(8,128)} %copy-done.2, f32[4,3,96,128]{3,2,1,0:T(8,128)} %copy-done.3, f32[4,3,96,128]{3,2,1,0:T(8,128)} %copy-done.4, f32[3,4,96,128]{3,2,1,0:T(8,128)} %copy-done.5, f32[3,96,128]{2,1,0:T(8,128)S(1)} %collective-permute-done.11.sbefore_ref, ...), custom_call_target="tpu_custom_call" | custom-call | tf_op jit(solution)/shard_map/fourth_fields/pallas_call | solution.py:394
  88.3 0.0 collective-permute-done.19.p3
  88.3 0.0 collective-permute-done.18.p2
  88.4 0.0 collective-permute-done.17.p1
  88.4 0.0 copy-done.6
  88.4 1.5 %fifth_flow.1 = f32[3,4,96,128]{3,2,1,0:T(8,128)} custom-call(f32[3,4,96,128]{3,2,1,0:T(8,128)S(1)} %copy-done.6, f32[3,96,128]{2,1,0:T(8,128)S(1)} %collective-permute-done.11.sbefore_ref, f32[3,96,128]{2,1,0:T(8,128)S(1)} %collective-permute-done.12.safter_ref, f32[288,128]{1,0:T(8,128)S(1)} %bitcast_add_fusion.p0, ...), custom_call_target="tpu_custom_call" | custom-call | tf_op jit(solution)/shard_map/fifth_flow/pallas_call | solution.py:431
  (12 shorter events, 0.1 us)
Async XLA Ops:
  0.6 7.3 %copy-start.7 = (s32[4,2]{0,1:T(2,128)S(1)}, s32[4,2]{0,1:T(2,128)}, u32[]{:S(2)}) copy-start(s32[4,2]{0,1:T(2,128)} %param.5) | copy-start | bytes 100
  4.5 8.7 %copy-start = (f32[4,3,4,96,128]{4,3,2,1,0:T(8,128)S(1)}, f32[4,3,4,96,128]{4,3,2,1,0:T(8,128)}, u32[]{:S(2)}) copy-start(f32[4,3,4,96,128]{4,3,2,1,0:T(8,128)} %config_ref.2) | copy-start | bytes 7077892
  4.5 11.8 %collective-permute-start = (f32[5,3,96,128]{3,2,1,0:T(8,128)}, f32[5,3,96,128]{3,2,1,0:T(8,128)S(1)}, u32[]{:S(2)}, u32[]{:S(2)}) collective-permute-start(f32[5,3,96,128]{3,2,1,0:T(8,128)} %get-tuple-element.41), channel_id=1, source_target_pairs={{0,8},{8,16},{16,24},{24,32},{32,40},{40,48},{48,56},{56,64},{64,7... | collective-permute-start | bytes 2211848 | tf_op jit(solution)/shard_map/ppermute | solution.py:480
  7.6 11.4 %collective-permute-start.1 = (f32[5,3,96,128]{3,2,1,0:T(8,128)}, f32[5,3,96,128]{3,2,1,0:T(8,128)}, u32[]{:S(2)}, u32[]{:S(2)}) collective-permute-start(f32[5,3,96,128]{3,2,1,0:T(8,128)} %get-tuple-element.44), channel_id=1, source_target_pairs={{8,0},{16,8},{24,16},{32,24},{40,32},{48,40},{56,48},{64,56},{72,6... | collective-permute-start | bytes 2211848 | tf_op jit(solution)/shard_map/ppermute | solution.py:485
  13.3 12.2 %copy-start.1 = (f32[3,4,96,128]{3,2,1,0:T(8,128)S(1)}, f32[3,4,96,128]{3,2,1,0:T(8,128)}, u32[]{:S(2)}) copy-start(f32[3,4,96,128]{3,2,1,0:T(8,128)} %flow_ref.3) | copy-start | bytes 1769476
  20.6 12.7 %collective-permute-start.4 = (f32[3,96,128]{2,1,0:T(8,128)S(1)}, f32[3,96,128]{2,1,0:T(8,128)S(1)}, u32[]{:S(2)}, u32[]{:S(2)}) collective-permute-start(f32[3,96,128]{2,1,0:T(8,128)S(1)} %get-tuple-element.51), channel_id=1, source_target_pairs={{0,1},{1,2},{2,3},{3,0},{4,5},{5,6},{6,7},{7,4},{8,9},{9,10},{10,1... | collective-permute-start | bytes 442376 | tf_op jit(solution)/shard_map/ppermute | solution.py:490
  21.9 11.4 %collective-permute-start.5 = (f32[3,96,128]{2,1,0:T(8,128)S(1)}, f32[3,96,128]{2,1,0:T(8,128)S(1)}, u32[]{:S(2)}, u32[]{:S(2)}) collective-permute-start(f32[3,96,128]{2,1,0:T(8,128)S(1)} %get-tuple-element.53), channel_id=1, source_target_pairs={{0,2},{1,3},{2,0},{3,1},{4,6},{5,7},{6,4},{7,5},{8,10},{9,11},{10,... | collective-permute-start | bytes 442376 | tf_op jit(solution)/shard_map/ppermute | solution.py:490
  24.3 9.0 %collective-permute-start.6 = (f32[3,96,128]{2,1,0:T(8,128)S(1)}, f32[3,96,128]{2,1,0:T(8,128)S(1)}, u32[]{:S(2)}, u32[]{:S(2)}) collective-permute-start(f32[3,96,128]{2,1,0:T(8,128)S(1)} %get-tuple-element.55), channel_id=1, source_target_pairs={{0,3},{1,0},{2,1},{3,2},{4,7},{5,4},{6,5},{7,6},{8,11},{9,8},{10,9... | collective-permute-start | bytes 442376 | tf_op jit(solution)/shard_map/ppermute | solution.py:490
  29.5 13.3 %copy-start.2 = (f32[4,3,4,96,128]{4,3,2,1,0:T(8,128)}, f32[4,3,4,96,128]{4,3,2,1,0:T(8,128)S(1)}, u32[]{:S(2)}) copy-start(f32[4,3,4,96,128]{4,3,2,1,0:T(8,128)S(1)} %get-tuple-element.59.config_ref) | copy-start | bytes 7077892
  29.5 18.1 %collective-permute-start.2 = (f32[4,3,96,128]{3,2,1,0:T(8,128)S(1)}, f32[4,3,96,128]{3,2,1,0:T(8,128)S(1)}, u32[]{:S(2)}, u32[]{:S(2)}) collective-permute-start(f32[4,3,96,128]{3,2,1,0:T(8,128)S(1)} %get-tuple-element.49), channel_id=1, source_target_pairs={{0,8},{8,16},{16,24},{24,32},{32,40},{40,48},{48,56},{56,64},{64,7... | collective-permute-start | bytes 1769480 | tf_op jit(solution)/shard_map/ppermute | solution.py:480
  30.1 17.4 %collective-permute-start.3 = (f32[4,3,96,128]{3,2,1,0:T(8,128)S(1)}, f32[4,3,96,128]{3,2,1,0:T(8,128)S(1)}, u32[]{:S(2)}, u32[]{:S(2)}) collective-permute-start(f32[4,3,96,128]{3,2,1,0:T(8,128)S(1)} %get-tuple-element.50), channel_id=1, source_target_pairs={{8,0},{16,8},{24,16},{32,24},{40,32},{48,40},{56,48},{64,56},{72,6... | collective-permute-start | bytes 1769480 | tf_op jit(solution)/shard_map/ppermute | solution.py:485
  33.4 12.0 %collective-permute-start.7 = (f32[296,128]{1,0:T(8,128)S(1)}, f32[296,128]{1,0:T(8,128)S(1)}, u32[]{:S(2)}, u32[]{:S(2)}) collective-permute-start(f32[296,128]{1,0:T(8,128)S(1)} %pad_maximum_fusion), channel_id=1, source_target_pairs={{0,4},{1,5},{2,6},{3,7},{4,0},{5,1},{6,2},{7,3},{8,12},{9,13},{10,... | collective-permute-start | bytes 454664 | tf_op jit(solution)/shard_map/ppermute | solution.py:495
  45.4 5.5 %collective-permute-start.10 = (f32[296,128]{1,0:T(8,128)S(1)}, f32[296,128]{1,0:T(8,128)S(1)}, u32[]{:S(2)}, u32[]{:S(2)}) collective-permute-start(f32[296,128]{1,0:T(8,128)S(1)} %fusion.p0), channel_id=1, source_target_pairs={{0,3},{1,0},{2,1},{3,2},{4,7},{5,4},{6,5},{7,6},{8,11},{9,8},{10,9... | collective-permute-start | bytes 454664 | tf_op jit(solution)/shard_map/ppermute | solution.py:490
  45.4 7.1 %collective-permute-start.9 = (f32[296,128]{1,0:T(8,128)S(1)}, f32[296,128]{1,0:T(8,128)S(1)}, u32[]{:S(2)}, u32[]{:S(2)}) collective-permute-start(f32[296,128]{1,0:T(8,128)S(1)} %fusion.p0), channel_id=1, source_target_pairs={{0,2},{1,3},{2,0},{3,1},{4,6},{5,7},{6,4},{7,5},{8,10},{9,11},{10,... | collective-permute-start | bytes 454664 | tf_op jit(solution)/shard_map/ppermute | solution.py:490
  47.5 5.9 %collective-permute-start.8 = (f32[296,128]{1,0:T(8,128)S(1)}, f32[296,128]{1,0:T(8,128)S(1)}, u32[]{:S(2)}, u32[]{:S(2)}) collective-permute-start(f32[296,128]{1,0:T(8,128)S(1)} %fusion.p0), channel_id=1, source_target_pairs={{0,1},{1,2},{2,3},{3,0},{4,5},{5,6},{6,7},{7,4},{8,9},{9,10},{10,1... | collective-permute-start | bytes 454664 | tf_op jit(solution)/shard_map/ppermute | solution.py:490
  47.6 8.2 %copy-start.3 = (f32[4,3,96,128]{3,2,1,0:T(8,128)}, f32[4,3,96,128]{3,2,1,0:T(8,128)S(1)}, u32[]{:S(2)}) copy-start(f32[4,3,96,128]{3,2,1,0:T(8,128)S(1)} %collective-permute-done.2.before_ref) | copy-start | bytes 1769476
  47.6 8.2 %copy-start.4 = (f32[4,3,96,128]{3,2,1,0:T(8,128)}, f32[4,3,96,128]{3,2,1,0:T(8,128)S(1)}, u32[]{:S(2)}) copy-start(f32[4,3,96,128]{3,2,1,0:T(8,128)S(1)} %collective-permute-done.3.after_ref) | copy-start | bytes 1769476
  48.1 8.5 %collective-permute-start.15 = (f32[3,96,128]{2,1,0:T(8,128)S(1)}, f32[3,96,128]{2,1,0:T(8,128)S(1)}, u32[]{:S(2)}, u32[]{:S(2)}) collective-permute-start(f32[3,96,128]{2,1,0:T(8,128)S(1)} %get-tuple-element.73), channel_id=1, source_target_pairs={{0,3},{1,0},{2,1},{3,2},{4,7},{5,4},{6,5},{7,6},{8,11},{9,8},{10,9... | collective-permute-start | bytes 442376 | tf_op jit(solution)/shard_map/ppermute | solution.py:490
  50.9 8.9 %collective-permute-start.13 = (f32[3,96,128]{2,1,0:T(8,128)S(1)}, f32[3,96,128]{2,1,0:T(8,128)S(1)}, u32[]{:S(2)}, u32[]{:S(2)}) collective-permute-start(f32[3,96,128]{2,1,0:T(8,128)S(1)} %get-tuple-element.71), channel_id=1, source_target_pairs={{0,1},{1,2},{2,3},{3,0},{4,5},{5,6},{6,7},{7,4},{8,9},{9,10},{10,1... | collective-permute-start | bytes 442376 | tf_op jit(solution)/shard_map/ppermute | solution.py:490
  50.9 9.1 %collective-permute-start.14 = (f32[3,96,128]{2,1,0:T(8,128)S(1)}, f32[3,96,128]{2,1,0:T(8,128)S(1)}, u32[]{:S(2)}, u32[]{:S(2)}) collective-permute-start(f32[3,96,128]{2,1,0:T(8,128)S(1)} %get-tuple-element.72), channel_id=1, source_target_pairs={{0,2},{1,3},{2,0},{3,1},{4,6},{5,7},{6,4},{7,5},{8,10},{9,11},{10,... | collective-permute-start | bytes 442376 | tf_op jit(solution)/shard_map/ppermute | solution.py:490
  55.8 0.8 copy-start.5
  60.0 14.4 %collective-permute-start.16 = (f32[288,128]{1,0:T(8,128)S(1)}, f32[288,128]{1,0:T(8,128)S(1)}, u32[]{:S(2)}, u32[]{:S(2)}) collective-permute-start(f32[288,128]{1,0:T(8,128)S(1)} %bitcast.5), channel_id=1, source_target_pairs={{0,4},{1,5},{2,6},{3,7},{4,0},{5,1},{6,2},{7,3},{8,12},{9,13},{10,... | collective-permute-start | bytes 442376 | tf_op jit(solution)/shard_map/ppermute | solution.py:495
  65.4 16.4 %all-to-all-start = ((f32[32,8,128]{2,1,0:T(8,128)}), f32[32,8,128]{2,1,0:T(8,128)S(1)}, u32[]{:S(2)}, u32[]{:S(2)}) async-start(f32[32,8,128]{2,1,0:T(8,128)} %get-tuple-element.70), calls=%async_computation | async-start | bytes 262144 | tf_op jit(solution)/shard_map/all_to_all | solution.py:542
  72.7 9.3 %collective-permute-start.11 = (f32[3,96,128]{2,1,0:T(8,128)S(1)}, f32[3,96,128]{2,1,0:T(8,128)S(1)}, u32[]{:S(2)}, u32[]{:S(2)}) collective-permute-start(f32[3,96,128]{2,1,0:T(8,128)S(1)} %get-tuple-element.68), channel_id=1, source_target_pairs={{0,8},{8,16},{16,24},{24,32},{32,40},{40,48},{48,56},{56,64},{64,7... | collective-permute-start | bytes 442376 | tf_op jit(solution)/shard_map/ppermute | solution.py:480
  74.5 7.6 %collective-permute-start.12 = (f32[3,96,128]{2,1,0:T(8,128)S(1)}, f32[3,96,128]{2,1,0:T(8,128)S(1)}, u32[]{:S(2)}, u32[]{:S(2)}) collective-permute-start(f32[3,96,128]{2,1,0:T(8,128)S(1)} %get-tuple-element.69), channel_id=1, source_target_pairs={{8,0},{16,8},{24,16},{32,24},{40,32},{48,40},{56,48},{64,56},{72,6... | collective-permute-start | bytes 442376 | tf_op jit(solution)/shard_map/ppermute | solution.py:485
  74.5 13.9 %copy-start.6 = (f32[3,4,96,128]{3,2,1,0:T(8,128)S(1)}, f32[3,4,96,128]{3,2,1,0:T(8,128)}, u32[]{:S(2)}) copy-start(f32[3,4,96,128]{3,2,1,0:T(8,128)} %copy-done.5) | copy-start | bytes 1769476
  74.5 13.8 %collective-permute-start.19 = (f32[288,128]{1,0:T(8,128)S(1)}, f32[288,128]{1,0:T(8,128)S(1)}, u32[]{:S(2)}, u32[]{:S(2)}) collective-permute-start(f32[288,128]{1,0:T(8,128)S(1)} %bitcast_add_fusion.p0), channel_id=1, source_target_pairs={{0,3},{1,0},{2,1},{3,2},{4,7},{5,4},{6,5},{7,6},{8,11},{9,8},{10,9... | collective-permute-start | bytes 442376 | tf_op jit(solution)/shard_map/ppermute | solution.py:490
  74.7 13.6 %collective-permute-start.18 = (f32[288,128]{1,0:T(8,128)S(1)}, f32[288,128]{1,0:T(8,128)S(1)}, u32[]{:S(2)}, u32[]{:S(2)}) collective-permute-start(f32[288,128]{1,0:T(8,128)S(1)} %bitcast_add_fusion.p0), channel_id=1, source_target_pairs={{0,2},{1,3},{2,0},{3,1},{4,6},{5,7},{6,4},{7,5},{8,10},{9,11},{10,... | collective-permute-start | bytes 442376 | tf_op jit(solution)/shard_map/ppermute | solution.py:490
  81.8 6.5 %collective-permute-start.17 = (f32[288,128]{1,0:T(8,128)S(1)}, f32[288,128]{1,0:T(8,128)S(1)}, u32[]{:S(2)}, u32[]{:S(2)}) collective-permute-start(f32[288,128]{1,0:T(8,128)S(1)} %bitcast_add_fusion.p0), channel_id=1, source_target_pairs={{0,1},{1,2},{2,3},{3,0},{4,5},{5,6},{6,7},{7,4},{8,9},{9,10},{10,1... | collective-permute-start | bytes 442376 | tf_op jit(solution)/shard_map/ppermute | solution.py:490

commit v4 on v3

--- a/solution.py
+++ b/solution.py
@@ -329,16 +329,16 @@
             bend = bend + term[8 * r:8 * r + 8]
         edge = edge + (s[0:1] + s[rows - 1:rows])
         gain = gain + (v[0:1] - v[rows - 1:rows])
-    row = lax.broadcasted_iota(jnp.int32, (8, depth), 0)
+    lane = lax.broadcasted_iota(jnp.int32, (1, depth), 1)
     sums = [
         jnp.sum(total, axis=0, keepdims=True),
         jnp.sum(bend, axis=0, keepdims=True) + viscosity * edge,
         0.5 * gain,
         jnp.sum((wall_ref[0] + wall_ref[1]) + (wall_ref[2] + wall_ref[3]), axis=0, keepdims=True),
     ]
-    tile = jnp.zeros((8, depth), jnp.float32)
+    tile = jnp.zeros((1, depth), jnp.float32)
     for n, value in enumerate(sums):
-        tile = jnp.where(row == n, value, tile)
+        tile = jnp.where(lane == n, jnp.sum(value, axis=1, keepdims=True), tile)
     for n in range(sums_ref.shape[0]):
         sums_ref[n] = tile
     for i in range(3):
@@ -349,7 +349,7 @@
 def third_flow(flow, left, right, parts, slabs):
     _, width, rows, depth = flow.shape
     end = jax.ShapeDtypeStruct((3, rows, depth), jnp.float32)
-    sums = jax.ShapeDtypeStruct((slabs, 8, depth), jnp.float32)
+    sums = jax.ShapeDtypeStruct((slabs, 1, depth), jnp.float32)
     at = left.shape[0] - 1
     return pl.pallas_call(
         third_kernel,
@@ -365,9 +365,11 @@
 
 
 def lifts_of(shared_ref, walls, cells):
-    sums = jnp.sum(jnp.sum(shared_ref[...], axis=0), axis=1, keepdims=True)
-    lift = bulk_target - sums[0:1] / cells
-    change = time_step * (stress_coef * sums[3:4] - sums[1:2] - lift * (sums[2:3] + 2.0 * viscosity * walls))
+    row = jnp.sum(shared_ref[...], axis=0)
+    lane = lax.broadcasted_iota(jnp.int32, row.shape, 1)
+    flux, bend, gain, wall = [jnp.sum(jnp.where(lane == n, row, 0.0), axis=1, keepdims=True) for n in range(4)]
+    lift = bulk_target - flux / cells
+    change = time_step * (stress_coef * wall - bend - lift * (gain + 2.0 * viscosity * walls))
     return lift, -change / cells
 
 
@@ -441,17 +443,14 @@
 
 
 def pack_kernel(first_ref, last_ref, ffirst_ref, flast_ref, head_ref, tail_ref):
-    velocity = pl.program_id(0) == pl.num_programs(0) - 1
-
-    @pl.when(velocity)
-    def _():
-        head_ref[0] = ffirst_ref[:, 0]
-        tail_ref[0] = flast_ref[:, 0]
-
-    @pl.when(jnp.logical_not(velocity))
-    def _():
-        head_ref[0] = first_ref[0, :, 0]
-        tail_ref[0] = last_ref[0, :, 0]
+    fields = first_ref.shape[0]
+    for k in range(fields):
+        for i in range(3):
+            head_ref[k, i] = first_ref[k, i, 0]
+            tail_ref[k, i] = last_ref[k, i, 0]
+    for i in range(3):
+        head_ref[fields, i] = ffirst_ref[i, 0]
+        tail_ref[fields, i] = flast_ref[i, 0]
 
 
 def pack_ends(config, flow):
@@ -459,17 +458,17 @@
     rim = jax.ShapeDtypeStruct((fields + 1, 3, rows, depth), jnp.float32)
 
     def layer(x):
-        return pl.BlockSpec((1, 3, 1, rows, depth), lambda k: (jnp.minimum(k, fields - 1), 0, x, 0, 0))
+        return pl.BlockSpec((fields, 3, 1, rows, depth), lambda k: (0, 0, x, 0, 0))
 
     def flow_layer(x):
         return pl.BlockSpec((3, 1, rows, depth), lambda k: (0, x, 0, 0))
 
     return pl.pallas_call(
         pack_kernel,
-        grid=(fields + 1,),
+        grid=(1,),
         out_shape=[rim, rim],
         in_specs=[layer(0), layer(width - 1), flow_layer(0), flow_layer(width - 1)],
-        out_specs=[rim_block(rim.shape)] * 2,
+        out_specs=[whole_block(rim.shape)] * 2,
         compiler_params=params(),
         name="pack_ends",
     )(config, config, flow, flow)

time: 91.5 us -> 89.4 us (0.977); the launches traced: 89.9 us -> 88.9 us
  Pallas kernels: 32.7 us -> 31.4 us
    ppermute x3, starting transfers between devices: 5.41 us -> 3.66 us  [from_left(): lax.ppermute(value, 'gx', [(i, (i + 1) % count) for i in range(count)])]
    ppermute x3, starting transfers between devices: 3.47 us -> 4.97 us  [from_right(): lax.ppermute(value, 'gx', [((i + 1) % count, i) for i in range(count)])]
    pallas_call x1, Pallas kernels: 3.87 us -> 2.55 us  [pack_ends(): pl.pallas_call(pack_kernel, grid=(1,), out_shape=[rim, rim], in_specs=[la...]
where the time goes in v4:
time: 89.4 us; the launch traced here: 88.9 us
  starting transfers between devices  38.6 us (43%)
  Pallas kernels  31.4 us (35%)
  waiting for transfers between devices  16.9 us (19%)
  local copies, waits for them, and re-layouts  1.04 us (1%)
    ppermute x12, starting transfers between devices, quad_shift(): lax.ppermute(value, 'row', [(i, i - i % 4 + (i + by) % 4) for i in range(...  14.4 us
    pallas_call x2, Pallas kernels, draw_noise(): pl.pallas_call(functools.partial(noise_kernel, step, total_x), grid=(fiel...  11.2 us
    ppermute x2, starting transfers between devices, pair_swap(): return lax.ppermute(value, 'row', [(i, i ^ bit) for i in range(count)])  8.13 us
    all_to_all x1, starting transfers between devices, shards(): shared = lax.all_to_all(sums, 'gx', 0, 0)  7.43 us
    pallas_call x1, Pallas kernels, fourth_fields(): pl.pallas_call(functools.partial(fourth_kernel, walls, cells), grid=(fiel...  6.24 us
    all_to_all x1, waiting for transfers between devices, shards(): shared = lax.all_to_all(sums, 'gx', 0, 0)  5.14 us
    ppermute x3, starting transfers between devices, from_right(): lax.ppermute(value, 'gx', [((i + 1) % count, i) for i in range(count)])  4.97 us
    ppermute x12, waiting for transfers between devices, quad_shift(): lax.ppermute(value, 'row', [(i, i - i % 4 + (i + by) % 4) for i in range(...  4.22 us
  transfers between devices with their start and end apart: 21, of which 7 were waited for; matrix products, arithmetic and copies ran while one was open for 0% of the time, Pallas kernels for 29%

profile of v4, /device:TPU:1, one launch (start us, length us, event | category | flops | bytes accessed | tf_op | source)
XLA Modules:
  0.0 88.9 jit_solution(1832507812950769457)
XLA Ops:
  0.6 0.0 copy-start.7
  0.6 2.5 %pack_ends.1 = (f32[5,3,96,128]{3,2,1,0:T(8,128)}, f32[5,3,96,128]{3,2,1,0:T(8,128)}) custom-call(f32[4,3,4,96,128]{4,3,2,1,0:T(8,128)} %config_ref.2, f32[4,3,4,96,128]{4,3,2,1,0:T(8,128)} %config_ref.2, f32[3,4,96,128]{3,2,1,0:T(8,128)} %flow_ref.3, f32[3,4,96,128]{3,2,1,0:T(8,128)} %flow_ref.3), custom_call_target="tpu_custom_call" | custom-call | tf_op jit(solution)/shard_map/pack_ends/pallas_call | solution.py:466
  3.2 3.0 %collective-permute-start = (f32[5,3,96,128]{3,2,1,0:T(8,128)}, f32[5,3,96,128]{3,2,1,0:T(8,128)S(1)}, u32[]{:S(2)}, u32[]{:S(2)}) collective-permute-start(f32[5,3,96,128]{3,2,1,0:T(8,128)} %get-tuple-element.41), channel_id=1, source_target_pairs={{0,8},{8,16},{16,24},{24,32},{32,40},{40,48},{48,56},{56,64},{64,7... | collective-permute-start | bytes 2211848 | tf_op jit(solution)/shard_map/ppermute | solution.py:479
  6.2 0.2 collective-permute-start.1
  6.4 0.0 copy-done.7
  6.4 0.1 copy.6
  6.5 0.1 reshape.13.keys_ref
  6.6 5.2 %draw_noise.2.noise_ref = f32[4,3,4,96,128]{4,3,2,1,0:T(8,128)S(1)} custom-call(s32[8]{0:T(128)S(1)} %reshape.13.keys_ref), custom_call_target="tpu_custom_call" | custom-call | tf_op jit(solution)/shard_map/draw_noise/pallas_call | solution.py:74
  11.8 0.0 copy-done
  11.8 0.0 copy-start.1
  11.8 0.7 inner_stress.2.stress_ref
  12.6 2.4 %collective-permute-done.before_ref.fbefore_ref = f32[5,3,96,128]{3,2,1,0:T(8,128)S(1)} collective-permute-done((f32[5,3,96,128]{3,2,1,0:T(8,128)}, f32[5,3,96,128]{3,2,1,0:T(8,128)S(1)}, u32[]{:S(2)}, u32[]{:S(2)}) %collective-permute-start) | collective-permute-done | bytes 737312 | tf_op jit(solution)/shard_map/ppermute | solution.py:479
  14.9 2.7 %collective-permute-done.1.after_ref.fafter_ref = f32[5,3,96,128]{3,2,1,0:T(8,128)} collective-permute-done((f32[5,3,96,128]{3,2,1,0:T(8,128)}, f32[5,3,96,128]{3,2,1,0:T(8,128)}, u32[]{:S(2)}, u32[]{:S(2)}) %collective-permute-start.1) | collective-permute-done | bytes 737312 | tf_op jit(solution)/shard_map/ppermute | solution.py:484
  17.6 1.6 %stress_parts.2 = (f32[3,96,128]{2,1,0:T(8,128)S(1)}, f32[3,96,128]{2,1,0:T(8,128)S(1)}, f32[3,96,128]{2,1,0:T(8,128)S(1)}, f32[3,96,128]{2,1,0:T(8,128)S(1)}) custom-call(f32[6,4,96,128]{3,2,1,0:T(8,128)S(1)} %inner_stress.2.stress_ref, f32[5,3,96,128]{3,2,1,0:T(8,128)S(1)} %collective-permute-done.before_ref.fbefore_ref, ...), custom_call_target="tpu_custom_call" | custom-call | tf_op jit(solution)/shard_map/stress_parts/pallas_call | solution.py:189
  19.2 1.3 %collective-permute-start.4 = (f32[3,96,128]{2,1,0:T(8,128)S(1)}, f32[3,96,128]{2,1,0:T(8,128)S(1)}, u32[]{:S(2)}, u32[]{:S(2)}) collective-permute-start(f32[3,96,128]{2,1,0:T(8,128)S(1)} %get-tuple-element.51), channel_id=1, source_target_pairs={{0,1},{1,2},{2,3},{3,0},{4,5},{5,6},{6,7},{7,4},{8,9},{9,10},{10,1... | collective-permute-start | bytes 442376 | tf_op jit(solution)/shard_map/ppermute | solution.py:489
  20.5 2.5 %collective-permute-start.5 = (f32[3,96,128]{2,1,0:T(8,128)S(1)}, f32[3,96,128]{2,1,0:T(8,128)S(1)}, u32[]{:S(2)}, u32[]{:S(2)}) collective-permute-start(f32[3,96,128]{2,1,0:T(8,128)S(1)} %get-tuple-element.53), channel_id=1, source_target_pairs={{0,2},{1,3},{2,0},{3,1},{4,6},{5,7},{6,4},{7,5},{8,10},{9,11},{10,... | collective-permute-start | bytes 442376 | tf_op jit(solution)/shard_map/ppermute | solution.py:489
  23.0 1.1 %collective-permute-start.6 = (f32[3,96,128]{2,1,0:T(8,128)S(1)}, f32[3,96,128]{2,1,0:T(8,128)S(1)}, u32[]{:S(2)}, u32[]{:S(2)}) collective-permute-start(f32[3,96,128]{2,1,0:T(8,128)S(1)} %get-tuple-element.55), channel_id=1, source_target_pairs={{0,3},{1,0},{2,1},{3,2},{4,7},{5,4},{6,5},{7,6},{8,11},{9,8},{10,9... | collective-permute-start | bytes 442376 | tf_op jit(solution)/shard_map/ppermute | solution.py:489
  24.1 0.0 copy-done.1
  24.1 4.0 %second_fields.1 = (f32[4,3,4,96,128]{4,3,2,1,0:T(8,128)S(1)}, f32[4,3,96,128]{3,2,1,0:T(8,128)S(1)}, f32[4,3,96,128]{3,2,1,0:T(8,128)S(1)}, f32[8,128]{1,0:T(8,128)S(1)}) custom-call(f32[4,3,4,96,128]{4,3,2,1,0:T(8,128)S(1)} %copy-done, f32[5,3,96,128]{3,2,1,0:T(8,128)S(1)} %collective-permute-done.before_ref.fbefore_ref, ...), custom_call_target="tpu_custom_call" | custom-call | tf_op jit(solution)/shard_map/second_fields/pallas_call | solution.py:264
  28.1 0.0 copy-start.2
  28.1 0.6 collective-permute-start.2
  28.7 3.1 %collective-permute-start.3 = (f32[4,3,96,128]{3,2,1,0:T(8,128)S(1)}, f32[4,3,96,128]{3,2,1,0:T(8,128)S(1)}, u32[]{:S(2)}, u32[]{:S(2)}) collective-permute-start(f32[4,3,96,128]{3,2,1,0:T(8,128)S(1)} %get-tuple-element.50), channel_id=1, source_target_pairs={{8,0},{16,8},{24,16},{32,24},{40,32},{48,40},{56,48},{64,56},{72,6... | collective-permute-start | bytes 1769480 | tf_op jit(solution)/shard_map/ppermute | solution.py:484
  31.9 0.0 collective-permute-done.4
  31.9 0.0 collective-permute-done.5
  31.9 0.0 collective-permute-done.6
  32.0 2.7 %collective-permute-start.7 = (f32[296,128]{1,0:T(8,128)S(1)}, f32[296,128]{1,0:T(8,128)S(1)}, u32[]{:S(2)}, u32[]{:S(2)}) collective-permute-start(f32[296,128]{1,0:T(8,128)S(1)} %pad_maximum_fusion), channel_id=1, source_target_pairs={{0,4},{1,5},{2,6},{3,7},{4,0},{5,1},{6,2},{7,3},{8,12},{9,13},{10,... | collective-permute-start | bytes 454664 | tf_op jit(solution)/shard_map/ppermute | solution.py:494
  34.7 6.0 %draw_noise.3.noise_ref = f32[4,3,4,96,128]{4,3,2,1,0:T(8,128)} custom-call(s32[8]{0:T(128)S(1)} %reshape.13.keys_ref), custom_call_target="tpu_custom_call" | custom-call | tf_op jit(solution)/shard_map/draw_noise/pallas_call | solution.py:74
  40.7 0.7 inner_stress.3.stress_ref
  41.4 2.5 %collective-permute-done.7 = f32[296,128]{1,0:T(8,128)S(1)} collective-permute-done((f32[296,128]{1,0:T(8,128)S(1)}, f32[296,128]{1,0:T(8,128)S(1)}, u32[]{:S(2)}, u32[]{:S(2)}) %collective-permute-start.7) | collective-permute-done | bytes 151584 | tf_op jit(solution)/shard_map/ppermute | solution.py:494
  44.0 0.1 collective-permute-start.10
  44.0 2.1 %collective-permute-start.9 = (f32[296,128]{1,0:T(8,128)S(1)}, f32[296,128]{1,0:T(8,128)S(1)}, u32[]{:S(2)}, u32[]{:S(2)}) collective-permute-start(f32[296,128]{1,0:T(8,128)S(1)} %fusion.p0), channel_id=1, source_target_pairs={{0,2},{1,3},{2,0},{3,1},{4,6},{5,7},{6,4},{7,5},{8,10},{9,11},{10,... | collective-permute-start | bytes 454664 | tf_op jit(solution)/shard_map/ppermute | solution.py:489
  46.1 0.0 collective-permute-start.8
  46.2 0.0 collective-permute-done.2.before_ref
  46.2 0.0 collective-permute-done.3.after_ref
  46.2 0.0 copy-start.4
  46.2 0.5 stress_parts.3
  46.7 2.8 %collective-permute-start.15 = (f32[3,96,128]{2,1,0:T(8,128)S(1)}, f32[3,96,128]{2,1,0:T(8,128)S(1)}, u32[]{:S(2)}, u32[]{:S(2)}) collective-permute-start(f32[3,96,128]{2,1,0:T(8,128)S(1)} %get-tuple-element.73), channel_id=1, source_target_pairs={{0,3},{1,0},{2,1},{3,2},{4,7},{5,4},{6,5},{7,6},{8,11},{9,8},{10,9... | collective-permute-start | bytes 442376 | tf_op jit(solution)/shard_map/ppermute | solution.py:489
  49.5 0.0 collective-permute-start.13
  49.5 0.0 collective-permute-done.10.p3
  49.5 1.7 %collective-permute-start.14 = (f32[3,96,128]{2,1,0:T(8,128)S(1)}, f32[3,96,128]{2,1,0:T(8,128)S(1)}, u32[]{:S(2)}, u32[]{:S(2)}) collective-permute-start(f32[3,96,128]{2,1,0:T(8,128)S(1)} %get-tuple-element.72), channel_id=1, source_target_pairs={{0,2},{1,3},{2,0},{3,1},{4,6},{5,7},{6,4},{7,5},{8,10},{9,11},{10,... | collective-permute-start | bytes 442376 | tf_op jit(solution)/shard_map/ppermute | solution.py:489
  51.2 0.0 collective-permute-done.9.p2
  51.2 0.9 collective-permute-done.8.p1
  52.1 2.4 %third_flow.1 = (f32[3,4,96,128]{3,2,1,0:T(8,128)S(1)}, f32[3,96,128]{2,1,0:T(8,128)S(1)}, f32[3,96,128]{2,1,0:T(8,128)S(1)}, f32[32,1,128]{2,1,0:T(1,128)}) custom-call(f32[3,4,96,128]{3,2,1,0:T(8,128)S(1)} %copy-done.1, f32[5,3,96,128]{3,2,1,0:T(8,128)S(1)} %collective-permute-done.before_ref.fbefore_ref, ...), custom_call_target="tpu_custom_call" | custom-call | tf_op jit(solution)/shard_map/third_flow/pallas_call | solution.py:354
  54.4 0.0 copy-done.3
  54.4 0.8 copy-done.5
  55.2 0.0 collective-permute-done.15
  55.3 3.1 %collective-permute-done.13 = f32[3,96,128]{2,1,0:T(8,128)S(1)} collective-permute-done((f32[3,96,128]{2,1,0:T(8,128)S(1)}, f32[3,96,128]{2,1,0:T(8,128)S(1)}, u32[]{:S(2)}, u32[]{:S(2)}) %collective-permute-start.13) | collective-permute-done | bytes 147488 | tf_op jit(solution)/shard_map/ppermute | solution.py:489
  58.3 0.2 collective-permute-done.14
  58.6 5.4 %collective-permute-start.16 = (f32[288,128]{1,0:T(8,128)S(1)}, f32[288,128]{1,0:T(8,128)S(1)}, u32[]{:S(2)}, u32[]{:S(2)}) collective-permute-start(f32[288,128]{1,0:T(8,128)S(1)} %bitcast.5), channel_id=1, source_target_pairs={{0,4},{1,5},{2,6},{3,7},{4,0},{5,1},{6,2},{7,3},{8,12},{9,13},{10,... | collective-permute-start | bytes 442376 | tf_op jit(solution)/shard_map/ppermute | solution.py:494
  64.0 0.0 collective-permute-start.11
  64.0 1.6 %collective-permute-start.12 = (f32[3,96,128]{2,1,0:T(8,128)S(1)}, f32[3,96,128]{2,1,0:T(8,128)S(1)}, u32[]{:S(2)}, u32[]{:S(2)}) collective-permute-start(f32[3,96,128]{2,1,0:T(8,128)S(1)} %get-tuple-element.69), channel_id=1, source_target_pairs={{8,0},{16,8},{24,16},{32,24},{40,32},{48,40},{56,48},{64,56},{72,6... | collective-permute-start | bytes 442376 | tf_op jit(solution)/shard_map/ppermute | solution.py:484
  65.7 7.4 %all-to-all-start = ((f32[32,1,128]{2,1,0:T(1,128)}), f32[32,1,128]{2,1,0:T(1,128)S(1)}, u32[]{:S(2)}, u32[]{:S(2)}) async-start(f32[32,1,128]{2,1,0:T(1,128)} %get-tuple-element.70), calls=%async_computation | async-start | bytes 32768 | tf_op jit(solution)/shard_map/all_to_all | solution.py:541
  73.1 0.0 collective-permute-done.16
  73.1 0.8 collective-permute-start.19
  73.9 1.8 %collective-permute-start.18 = (f32[288,128]{1,0:T(8,128)S(1)}, f32[288,128]{1,0:T(8,128)S(1)}, u32[]{:S(2)}, u32[]{:S(2)}) collective-permute-start(f32[288,128]{1,0:T(8,128)S(1)} %bitcast_add_fusion.p0), channel_id=1, source_target_pairs={{0,2},{1,3},{2,0},{3,1},{4,6},{5,7},{6,4},{7,5},{8,10},{9,11},{10,... | collective-permute-start | bytes 442376 | tf_op jit(solution)/shard_map/ppermute | solution.py:489
  75.7 5.1 %all-to-all-done.shared_ref = f32[32,1,128]{2,1,0:T(1,128)S(1)} async-done(((f32[32,1,128]{2,1,0:T(1,128)}), f32[32,1,128]{2,1,0:T(1,128)S(1)}, u32[]{:S(2)}, u32[]{:S(2)}) %all-to-all-start) | async-done | bytes 16416 | tf_op jit(solution)/shard_map/all_to_all | solution.py:541
  80.9 0.3 collective-permute-start.17
  81.1 0.0 collective-permute-done.11.sbefore_ref
  81.1 0.0 collective-permute-done.12.safter_ref
  81.1 6.2 %fourth_fields.1 = f32[4,3,4,96,128]{4,3,2,1,0:T(8,128)} custom-call(f32[4,3,4,96,128]{4,3,2,1,0:T(8,128)} %copy-done.2, f32[4,3,96,128]{3,2,1,0:T(8,128)} %copy-done.3, f32[4,3,96,128]{3,2,1,0:T(8,128)} %copy-done.4, f32[3,4,96,128]{3,2,1,0:T(8,128)} %copy-done.5, f32[3,96,128]{2,1,0:T(8,128)S(1)} %collective-permute-done.11.sbefore_ref, ...), custom_call_target="tpu_custom_call" | custom-call | tf_op jit(solution)/shard_map/fourth_fields/pallas_call | solution.py:396
  87.4 0.0 collective-permute-done.19.p3
  87.4 0.0 collective-permute-done.18.p2
  87.4 0.0 collective-permute-done.17.p1
  87.4 1.5 %fifth_flow.1 = f32[3,4,96,128]{3,2,1,0:T(8,128)} custom-call(f32[3,4,96,128]{3,2,1,0:T(8,128)S(1)} %copy-done.6, f32[3,96,128]{2,1,0:T(8,128)S(1)} %collective-permute-done.11.sbefore_ref, f32[3,96,128]{2,1,0:T(8,128)S(1)} %collective-permute-done.12.safter_ref, f32[288,128]{1,0:T(8,128)S(1)} %bitcast_add_fusion.p0, ...), custom_call_target="tpu_custom_call" | custom-call | tf_op jit(solution)/shard_map/fifth_flow/pallas_call | solution.py:433
  (12 shorter events, 0.1 us)
Async XLA Ops:
  0.6 5.8 %copy-start.7 = (s32[4,2]{0,1:T(2,128)S(1)}, s32[4,2]{0,1:T(2,128)}, u32[]{:S(2)}) copy-start(s32[4,2]{0,1:T(2,128)} %param.5) | copy-start | bytes 100
  3.2 8.6 %copy-start = (f32[4,3,4,96,128]{4,3,2,1,0:T(8,128)S(1)}, f32[4,3,4,96,128]{4,3,2,1,0:T(8,128)}, u32[]{:S(2)}) copy-start(f32[4,3,4,96,128]{4,3,2,1,0:T(8,128)} %config_ref.2) | copy-start | bytes 7077892
  3.2 11.8 %collective-permute-start = (f32[5,3,96,128]{3,2,1,0:T(8,128)}, f32[5,3,96,128]{3,2,1,0:T(8,128)S(1)}, u32[]{:S(2)}, u32[]{:S(2)}) collective-permute-start(f32[5,3,96,128]{3,2,1,0:T(8,128)} %get-tuple-element.41), channel_id=1, source_target_pairs={{0,8},{8,16},{16,24},{24,32},{32,40},{40,48},{48,56},{56,64},{64,7... | collective-permute-start | bytes 2211848 | tf_op jit(solution)/shard_map/ppermute | solution.py:479
  6.2 11.4 %collective-permute-start.1 = (f32[5,3,96,128]{3,2,1,0:T(8,128)}, f32[5,3,96,128]{3,2,1,0:T(8,128)}, u32[]{:S(2)}, u32[]{:S(2)}) collective-permute-start(f32[5,3,96,128]{3,2,1,0:T(8,128)} %get-tuple-element.44), channel_id=1, source_target_pairs={{8,0},{16,8},{24,16},{32,24},{40,32},{48,40},{56,48},{64,56},{72,6... | collective-permute-start | bytes 2211848 | tf_op jit(solution)/shard_map/ppermute | solution.py:484
  11.8 12.3 %copy-start.1 = (f32[3,4,96,128]{3,2,1,0:T(8,128)S(1)}, f32[3,4,96,128]{3,2,1,0:T(8,128)}, u32[]{:S(2)}) copy-start(f32[3,4,96,128]{3,2,1,0:T(8,128)} %flow_ref.3) | copy-start | bytes 1769476
  19.2 12.7 %collective-permute-start.4 = (f32[3,96,128]{2,1,0:T(8,128)S(1)}, f32[3,96,128]{2,1,0:T(8,128)S(1)}, u32[]{:S(2)}, u32[]{:S(2)}) collective-permute-start(f32[3,96,128]{2,1,0:T(8,128)S(1)} %get-tuple-element.51), channel_id=1, source_target_pairs={{0,1},{1,2},{2,3},{3,0},{4,5},{5,6},{6,7},{7,4},{8,9},{9,10},{10,1... | collective-permute-start | bytes 442376 | tf_op jit(solution)/shard_map/ppermute | solution.py:489
  20.5 11.4 %collective-permute-start.5 = (f32[3,96,128]{2,1,0:T(8,128)S(1)}, f32[3,96,128]{2,1,0:T(8,128)S(1)}, u32[]{:S(2)}, u32[]{:S(2)}) collective-permute-start(f32[3,96,128]{2,1,0:T(8,128)S(1)} %get-tuple-element.53), channel_id=1, source_target_pairs={{0,2},{1,3},{2,0},{3,1},{4,6},{5,7},{6,4},{7,5},{8,10},{9,11},{10,... | collective-permute-start | bytes 442376 | tf_op jit(solution)/shard_map/ppermute | solution.py:489
  23.0 8.9 %collective-permute-start.6 = (f32[3,96,128]{2,1,0:T(8,128)S(1)}, f32[3,96,128]{2,1,0:T(8,128)S(1)}, u32[]{:S(2)}, u32[]{:S(2)}) collective-permute-start(f32[3,96,128]{2,1,0:T(8,128)S(1)} %get-tuple-element.55), channel_id=1, source_target_pairs={{0,3},{1,0},{2,1},{3,2},{4,7},{5,4},{6,5},{7,6},{8,11},{9,8},{10,9... | collective-permute-start | bytes 442376 | tf_op jit(solution)/shard_map/ppermute | solution.py:489
  28.1 13.3 %copy-start.2 = (f32[4,3,4,96,128]{4,3,2,1,0:T(8,128)}, f32[4,3,4,96,128]{4,3,2,1,0:T(8,128)S(1)}, u32[]{:S(2)}) copy-start(f32[4,3,4,96,128]{4,3,2,1,0:T(8,128)S(1)} %get-tuple-element.59.config_ref) | copy-start | bytes 7077892
  28.1 18.0 %collective-permute-start.2 = (f32[4,3,96,128]{3,2,1,0:T(8,128)S(1)}, f32[4,3,96,128]{3,2,1,0:T(8,128)S(1)}, u32[]{:S(2)}, u32[]{:S(2)}) collective-permute-start(f32[4,3,96,128]{3,2,1,0:T(8,128)S(1)} %get-tuple-element.49), channel_id=1, source_target_pairs={{0,8},{8,16},{16,24},{24,32},{32,40},{40,48},{48,56},{56,64},{64,7... | collective-permute-start | bytes 1769480 | tf_op jit(solution)/shard_map/ppermute | solution.py:479
  28.7 17.4 %collective-permute-start.3 = (f32[4,3,96,128]{3,2,1,0:T(8,128)S(1)}, f32[4,3,96,128]{3,2,1,0:T(8,128)S(1)}, u32[]{:S(2)}, u32[]{:S(2)}) collective-permute-start(f32[4,3,96,128]{3,2,1,0:T(8,128)S(1)} %get-tuple-element.50), channel_id=1, source_target_pairs={{8,0},{16,8},{24,16},{32,24},{40,32},{48,40},{56,48},{64,56},{72,6... | collective-permute-start | bytes 1769480 | tf_op jit(solution)/shard_map/ppermute | solution.py:484
  32.0 12.0 %collective-permute-start.7 = (f32[296,128]{1,0:T(8,128)S(1)}, f32[296,128]{1,0:T(8,128)S(1)}, u32[]{:S(2)}, u32[]{:S(2)}) collective-permute-start(f32[296,128]{1,0:T(8,128)S(1)} %pad_maximum_fusion), channel_id=1, source_target_pairs={{0,4},{1,5},{2,6},{3,7},{4,0},{5,1},{6,2},{7,3},{8,12},{9,13},{10,... | collective-permute-start | bytes 454664 | tf_op jit(solution)/shard_map/ppermute | solution.py:494
  44.0 5.5 %collective-permute-start.10 = (f32[296,128]{1,0:T(8,128)S(1)}, f32[296,128]{1,0:T(8,128)S(1)}, u32[]{:S(2)}, u32[]{:S(2)}) collective-permute-start(f32[296,128]{1,0:T(8,128)S(1)} %fusion.p0), channel_id=1, source_target_pairs={{0,3},{1,0},{2,1},{3,2},{4,7},{5,4},{6,5},{7,6},{8,11},{9,8},{10,9... | collective-permute-start | bytes 454664 | tf_op jit(solution)/shard_map/ppermute | solution.py:489
  44.0 7.1 %collective-permute-start.9 = (f32[296,128]{1,0:T(8,128)S(1)}, f32[296,128]{1,0:T(8,128)S(1)}, u32[]{:S(2)}, u32[]{:S(2)}) collective-permute-start(f32[296,128]{1,0:T(8,128)S(1)} %fusion.p0), channel_id=1, source_target_pairs={{0,2},{1,3},{2,0},{3,1},{4,6},{5,7},{6,4},{7,5},{8,10},{9,11},{10,... | collective-permute-start | bytes 454664 | tf_op jit(solution)/shard_map/ppermute | solution.py:489
  46.1 5.9 %collective-permute-start.8 = (f32[296,128]{1,0:T(8,128)S(1)}, f32[296,128]{1,0:T(8,128)S(1)}, u32[]{:S(2)}, u32[]{:S(2)}) collective-permute-start(f32[296,128]{1,0:T(8,128)S(1)} %fusion.p0), channel_id=1, source_target_pairs={{0,1},{1,2},{2,3},{3,0},{4,5},{5,6},{6,7},{7,4},{8,9},{9,10},{10,1... | collective-permute-start | bytes 454664 | tf_op jit(solution)/shard_map/ppermute | solution.py:489
  46.2 8.3 %copy-start.3 = (f32[4,3,96,128]{3,2,1,0:T(8,128)}, f32[4,3,96,128]{3,2,1,0:T(8,128)S(1)}, u32[]{:S(2)}) copy-start(f32[4,3,96,128]{3,2,1,0:T(8,128)S(1)} %collective-permute-done.2.before_ref) | copy-start | bytes 1769476
  46.2 8.2 %copy-start.4 = (f32[4,3,96,128]{3,2,1,0:T(8,128)}, f32[4,3,96,128]{3,2,1,0:T(8,128)S(1)}, u32[]{:S(2)}) copy-start(f32[4,3,96,128]{3,2,1,0:T(8,128)S(1)} %collective-permute-done.3.after_ref) | copy-start | bytes 1769476
  46.7 8.5 %collective-permute-start.15 = (f32[3,96,128]{2,1,0:T(8,128)S(1)}, f32[3,96,128]{2,1,0:T(8,128)S(1)}, u32[]{:S(2)}, u32[]{:S(2)}) collective-permute-start(f32[3,96,128]{2,1,0:T(8,128)S(1)} %get-tuple-element.73), channel_id=1, source_target_pairs={{0,3},{1,0},{2,1},{3,2},{4,7},{5,4},{6,5},{7,6},{8,11},{9,8},{10,9... | collective-permute-start | bytes 442376 | tf_op jit(solution)/shard_map/ppermute | solution.py:489
  49.5 8.9 %collective-permute-start.13 = (f32[3,96,128]{2,1,0:T(8,128)S(1)}, f32[3,96,128]{2,1,0:T(8,128)S(1)}, u32[]{:S(2)}, u32[]{:S(2)}) collective-permute-start(f32[3,96,128]{2,1,0:T(8,128)S(1)} %get-tuple-element.71), channel_id=1, source_target_pairs={{0,1},{1,2},{2,3},{3,0},{4,5},{5,6},{6,7},{7,4},{8,9},{9,10},{10,1... | collective-permute-start | bytes 442376 | tf_op jit(solution)/shard_map/ppermute | solution.py:489
  49.5 9.1 %collective-permute-start.14 = (f32[3,96,128]{2,1,0:T(8,128)S(1)}, f32[3,96,128]{2,1,0:T(8,128)S(1)}, u32[]{:S(2)}, u32[]{:S(2)}) collective-permute-start(f32[3,96,128]{2,1,0:T(8,128)S(1)} %get-tuple-element.72), channel_id=1, source_target_pairs={{0,2},{1,3},{2,0},{3,1},{4,6},{5,7},{6,4},{7,5},{8,10},{9,11},{10,... | collective-permute-start | bytes 442376 | tf_op jit(solution)/shard_map/ppermute | solution.py:489
  54.4 0.8 copy-start.5
  58.6 14.5 %collective-permute-start.16 = (f32[288,128]{1,0:T(8,128)S(1)}, f32[288,128]{1,0:T(8,128)S(1)}, u32[]{:S(2)}, u32[]{:S(2)}) collective-permute-start(f32[288,128]{1,0:T(8,128)S(1)} %bitcast.5), channel_id=1, source_target_pairs={{0,4},{1,5},{2,6},{3,7},{4,0},{5,1},{6,2},{7,3},{8,12},{9,13},{10,... | collective-permute-start | bytes 442376 | tf_op jit(solution)/shard_map/ppermute | solution.py:494
  64.0 17.1 %collective-permute-start.11 = (f32[3,96,128]{2,1,0:T(8,128)S(1)}, f32[3,96,128]{2,1,0:T(8,128)S(1)}, u32[]{:S(2)}, u32[]{:S(2)}) collective-permute-start(f32[3,96,128]{2,1,0:T(8,128)S(1)} %get-tuple-element.68), channel_id=1, source_target_pairs={{0,8},{8,16},{16,24},{24,32},{32,40},{40,48},{48,56},{56,64},{64,7... | collective-permute-start | bytes 442376 | tf_op jit(solution)/shard_map/ppermute | solution.py:479
  64.0 17.1 %collective-permute-start.12 = (f32[3,96,128]{2,1,0:T(8,128)S(1)}, f32[3,96,128]{2,1,0:T(8,128)S(1)}, u32[]{:S(2)}, u32[]{:S(2)}) collective-permute-start(f32[3,96,128]{2,1,0:T(8,128)S(1)} %get-tuple-element.69), channel_id=1, source_target_pairs={{8,0},{16,8},{24,16},{32,24},{40,32},{48,40},{56,48},{64,56},{72,6... | collective-permute-start | bytes 442376 | tf_op jit(solution)/shard_map/ppermute | solution.py:484
  65.7 15.2 %all-to-all-start = ((f32[32,1,128]{2,1,0:T(1,128)}), f32[32,1,128]{2,1,0:T(1,128)S(1)}, u32[]{:S(2)}, u32[]{:S(2)}) async-start(f32[32,1,128]{2,1,0:T(1,128)} %get-tuple-element.70), calls=%async_computation | async-start | bytes 32768 | tf_op jit(solution)/shard_map/all_to_all | solution.py:541
  73.1 14.3 %copy-start.6 = (f32[3,4,96,128]{3,2,1,0:T(8,128)S(1)}, f32[3,4,96,128]{3,2,1,0:T(8,128)}, u32[]{:S(2)}) copy-start(f32[3,4,96,128]{3,2,1,0:T(8,128)} %copy-done.5) | copy-start | bytes 1769476
  73.1 14.2 %collective-permute-start.19 = (f32[288,128]{1,0:T(8,128)S(1)}, f32[288,128]{1,0:T(8,128)S(1)}, u32[]{:S(2)}, u32[]{:S(2)}) collective-permute-start(f32[288,128]{1,0:T(8,128)S(1)} %bitcast_add_fusion.p0), channel_id=1, source_target_pairs={{0,3},{1,0},{2,1},{3,2},{4,7},{5,4},{6,5},{7,6},{8,11},{9,8},{10,9... | collective-permute-start | bytes 442376 | tf_op jit(solution)/shard_map/ppermute | solution.py:489
  73.9 13.5 %collective-permute-start.18 = (f32[288,128]{1,0:T(8,128)S(1)}, f32[288,128]{1,0:T(8,128)S(1)}, u32[]{:S(2)}, u32[]{:S(2)}) collective-permute-start(f32[288,128]{1,0:T(8,128)S(1)} %bitcast_add_fusion.p0), channel_id=1, source_target_pairs={{0,2},{1,3},{2,0},{3,1},{4,6},{5,7},{6,4},{7,5},{8,10},{9,11},{10,... | collective-permute-start | bytes 442376 | tf_op jit(solution)/shard_map/ppermute | solution.py:489
  80.9 6.5 %collective-permute-start.17 = (f32[288,128]{1,0:T(8,128)S(1)}, f32[288,128]{1,0:T(8,128)S(1)}, u32[]{:S(2)}, u32[]{:S(2)}) collective-permute-start(f32[288,128]{1,0:T(8,128)S(1)} %bitcast_add_fusion.p0), channel_id=1, source_target_pairs={{0,1},{1,2},{2,3},{3,0},{4,5},{5,6},{6,7},{7,4},{8,9},{9,10},{10,1... | collective-permute-start | bytes 442376 | tf_op jit(solution)/shard_map/ppermute | solution.py:489

commit v5 on v4

--- a/solution.py
+++ b/solution.py
@@ -373,7 +373,7 @@
     return lift, -change / cells
 
 
-def fourth_kernel(walls, cells, config_ref, before_ref, after_ref, start_ref, sbefore_ref, safter_ref, noise_ref, shared_ref, new_ref, slope_ref):
+def fourth_kernel(config_ref, before_ref, after_ref, start_ref, sbefore_ref, safter_ref, noise_ref, new_ref, slope_ref):
     width = config_ref.shape[2]
 
     def flow_at(i, x):
@@ -385,27 +385,54 @@
 
     @pl.when(pl.program_id(0) == 0)
     def _():
-        lift = lifts_of(shared_ref, walls, cells)[0]
-        fill_slopes(lambda i, x: flow_at(i, x) + lift if i == 0 else flow_at(i, x), slope_ref, width)
+        fill_slopes(flow_at, slope_ref, width)
 
     advance_field(config_ref, before_ref, after_ref, noise_ref, new_ref, slope_ref)
 
 
-def fourth_fields(config, before, after, start, sbefore, safter, noise, shared, walls, cells):
+def fourth_fields(config, before, after, start, sbefore, safter, noise):
     fields, _, width, rows, depth = config.shape
     return pl.pallas_call(
-        functools.partial(fourth_kernel, walls, cells),
+        fourth_kernel,
         grid=(fields,),
         out_shape=jax.ShapeDtypeStruct(config.shape, jnp.float32),
         in_specs=[
             field_block(config.shape), rim_block(before.shape), rim_block(after.shape), whole_block(start.shape),
-            whole_block(sbefore.shape), whole_block(safter.shape), field_block(noise.shape), whole_block(shared.shape),
+            whole_block(sbefore.shape), whole_block(safter.shape), field_block(noise.shape),
         ],
         out_specs=field_block(config.shape),
         scratch_shapes=[pltpu.VMEM((width, 12, rows, depth), jnp.float32)],
         compiler_params=params(),
         name="fourth_fields",
-    )(config, before, after, start, sbefore, safter, noise, shared)
+    )(config, before, after, start, sbefore, safter, noise)
+
+
+def lift_kernel(walls, cells, rough_ref, config_ref, before_ref, after_ref, shared_ref, out_ref):
+    _, _, width, rows, depth = config_ref.shape
+    half = (0.5 * time_step) * lifts_of(shared_ref, walls, cells)[0]
+    row = lax.broadcasted_iota(jnp.int32, (rows, depth), 0)
+    slope = jnp.where(row == 0, half, jnp.where(row == rows - 1, -half, 0.0))
+    for x in range(width):
+        for i in range(3):
+            below = config_ref[0, i, x - 1] if x > 0 else before_ref[0, i]
+            above = config_ref[0, i, x + 1] if x + 1 < width else after_ref[0, i]
+            value = rough_ref[0, i, x] - half * (above - below)
+            out_ref[0, i, x] = value + slope * config_ref[0, 1, x] if i == 0 else value
+
+
+def lift_fields(rough, config, before, after, shared, walls, cells):
+    return pl.pallas_call(
+        functools.partial(lift_kernel, walls, cells),
+        grid=(config.shape[0],),
+        out_shape=jax.ShapeDtypeStruct(config.shape, jnp.float32),
+        in_specs=[
+            field_block(config.shape), field_block(config.shape), rim_block(before.shape), rim_block(after.shape),
+            whole_block(shared.shape),
+        ],
+        out_specs=field_block(config.shape),
+        compiler_params=params(),
+        name="lift_fields",
+    )(rough, config, before, after, shared)
 
 
 def fifth_kernel(walls, cells, start_ref, sbefore_ref, safter_ref, p0, p1, p2, p3, shared_ref, out_ref, div_ref):
@@ -541,11 +568,16 @@
     shared = lax.all_to_all(sums, "gx", 0, 0)
     own = flat(parts[0] + got[0] + got[1] + after(got[2], start))
     own = own + pair_swap(own, 4)
-    next_div = [own, quad_shift(after(own, shared), 1), quad_shift(own, 2), quad_shift(own, 3)]
+    next_div = [own] + [quad_shift(own, n) for n in (1, 2, 3)]
+    rough = fourth_fields(
+        in_hbm(config), in_hbm(before), in_hbm(behind), in_hbm(start), after(sleft, own), sright, in_hbm(later)
+    )
+    shared = after(shared, rough)
 
     walls = total_x * depth
-    config = fourth_fields(in_hbm(config), in_hbm(before), in_hbm(behind), in_hbm(start), sleft, sright, in_hbm(later), shared, walls, cells)
-    flow = fifth_flow(start, sleft, sright, [after(d, config) for d in next_div], shared, walls, cells)
+    rolls = [after(d, rough) for d in next_div]
+    config = lift_fields(rough, in_hbm(config), in_hbm(before), in_hbm(behind), shared, walls, cells)
+    flow = fifth_flow(start, sleft, sright, [after(d, config) for d in rolls], shared, walls, cells)
     return config, flow
 
 

time: 89.4 us -> 97.2 us (1.087)
  starting transfers between devices: 38.6 us -> 43.1 us
  Pallas kernels: 31.4 us -> 35.6 us
  waiting for transfers between devices: 16.9 us -> 15.3 us
    all_to_all x1, starting transfers between devices: 7.43 us -> 12.7 us  [shards(): shared = lax.all_to_all(sums, 'gx', 0, 0)]
    pallas_call x1 -> x2, Pallas kernels: 6.24 us -> 9.43 us  [the longest x1 5.04 us: fourth_fields(): pl.pallas_call(fourth_kernel, grid=(fields,), out_shape=jax.ShapeDtypeStr...]
    all_to_all x1, waiting for transfers between devices: 5.14 us -> 2.76 us  [shards(): shared = lax.all_to_all(sums, 'gx', 0, 0)]
    pallas_call x1, Pallas kernels: 1.51 us -> 2.49 us  [fifth_flow(): pl.pallas_call(functools.partial(fifth_kernel, walls, cells), grid=(1,),...]
  transfers between devices with their start and end apart: 21 -> 21, of which waited for: 7 -> 8; matrix products, arithmetic and copies ran while one was open for 0% -> 0% of each run, Pallas kernels for 29% -> 30%
where the time goes in v5:
time: 97.2 us; the launch traced here: 96.8 us
  starting transfers between devices  43.1 us (44%)
  Pallas kernels  35.6 us (37%)
  waiting for transfers between devices  15.3 us (16%)
  local copies, waits for them, and re-layouts  1.84 us (2%)
    ppermute x12, starting transfers between devices, quad_shift(): lax.ppermute(value, 'row', [(i, i - i % 4 + (i + by) % 4) for i in range(...  14.2 us
    all_to_all x1, starting transfers between devices, shards(): shared = lax.all_to_all(sums, 'gx', 0, 0)  12.7 us
    pallas_call x2, Pallas kernels, draw_noise(): pl.pallas_call(functools.partial(noise_kernel, step, total_x), grid=(fiel...  11.2 us
    ppermute x2, starting transfers between devices, pair_swap(): return lax.ppermute(value, 'row', [(i, i ^ bit) for i in range(count)])  7.63 us
    pallas_call x1, Pallas kernels, fourth_fields(): pl.pallas_call(fourth_kernel, grid=(fields,), out_shape=jax.ShapeDtypeStr...  5.04 us
    ppermute x3, starting transfers between devices, from_right(): lax.ppermute(value, 'gx', [((i + 1) % count, i) for i in range(count)])  4.97 us
    pallas_call x1, Pallas kernels, lift_fields(): pl.pallas_call(functools.partial(lift_kernel, walls, cells), grid=(config...  4.39 us
    ppermute x12, waiting for transfers between devices, quad_shift(): lax.ppermute(value, 'row', [(i, i - i % 4 + (i + by) % 4) for i in range(...  4.01 us
  transfers between devices with their start and end apart: 21, of which 8 were waited for; matrix products, arithmetic and copies ran while one was open for 0% of the time, Pallas kernels for 30%

profile of v5, /device:TPU:1, one launch (start us, length us, event | category | flops | bytes accessed | tf_op | source)
XLA Modules:
  0.0 96.8 jit_solution(5778524606268148655)
XLA Ops:
  0.6 0.0 copy-start.7
  0.6 2.5 %pack_ends.1 = (f32[5,3,96,128]{3,2,1,0:T(8,128)}, f32[5,3,96,128]{3,2,1,0:T(8,128)}) custom-call(f32[4,3,4,96,128]{4,3,2,1,0:T(8,128)} %config_ref.2, f32[4,3,4,96,128]{4,3,2,1,0:T(8,128)} %config_ref.2, f32[3,4,96,128]{3,2,1,0:T(8,128)} %flow_ref.3, f32[3,4,96,128]{3,2,1,0:T(8,128)} %flow_ref.3), custom_call_target="tpu_custom_call" | custom-call | tf_op jit(solution)/shard_map/pack_ends/pallas_call | solution.py:493
  3.2 3.0 %collective-permute-start = (f32[5,3,96,128]{3,2,1,0:T(8,128)}, f32[5,3,96,128]{3,2,1,0:T(8,128)S(1)}, u32[]{:S(2)}, u32[]{:S(2)}) collective-permute-start(f32[5,3,96,128]{3,2,1,0:T(8,128)} %get-tuple-element.46), channel_id=1, source_target_pairs={{0,8},{8,16},{16,24},{24,32},{32,40},{40,48},{48,56},{56,64},{64,7... | collective-permute-start | bytes 2211848 | tf_op jit(solution)/shard_map/ppermute | solution.py:506
  6.2 0.2 collective-permute-start.1
  6.4 0.0 copy-done.7
  6.4 0.1 copy.6
  6.5 0.1 reshape.13.keys_ref
  6.6 5.2 %draw_noise.2.noise_ref = f32[4,3,4,96,128]{4,3,2,1,0:T(8,128)S(1)} custom-call(s32[8]{0:T(128)S(1)} %reshape.13.keys_ref), custom_call_target="tpu_custom_call" | custom-call | tf_op jit(solution)/shard_map/draw_noise/pallas_call | solution.py:74
  11.8 0.0 copy-done
  11.8 0.0 copy-start.2
  11.8 0.7 inner_stress.2.stress_ref
  12.6 2.4 %collective-permute-done.before_ref.fbefore_ref = f32[5,3,96,128]{3,2,1,0:T(8,128)S(1)} collective-permute-done((f32[5,3,96,128]{3,2,1,0:T(8,128)}, f32[5,3,96,128]{3,2,1,0:T(8,128)S(1)}, u32[]{:S(2)}, u32[]{:S(2)}) %collective-permute-start) | collective-permute-done | bytes 737312 | tf_op jit(solution)/shard_map/ppermute | solution.py:506
  14.9 2.7 %collective-permute-done.1.after_ref.fafter_ref = f32[5,3,96,128]{3,2,1,0:T(8,128)} collective-permute-done((f32[5,3,96,128]{3,2,1,0:T(8,128)}, f32[5,3,96,128]{3,2,1,0:T(8,128)}, u32[]{:S(2)}, u32[]{:S(2)}) %collective-permute-start.1) | collective-permute-done | bytes 737312 | tf_op jit(solution)/shard_map/ppermute | solution.py:511
  17.6 1.6 %stress_parts.2 = (f32[3,96,128]{2,1,0:T(8,128)S(1)}, f32[3,96,128]{2,1,0:T(8,128)S(1)}, f32[3,96,128]{2,1,0:T(8,128)S(1)}, f32[3,96,128]{2,1,0:T(8,128)S(1)}) custom-call(f32[6,4,96,128]{3,2,1,0:T(8,128)S(1)} %inner_stress.2.stress_ref, f32[5,3,96,128]{3,2,1,0:T(8,128)S(1)} %collective-permute-done.before_ref.fbefore_ref, ...), custom_call_target="tpu_custom_call" | custom-call | tf_op jit(solution)/shard_map/stress_parts/pallas_call | solution.py:189
  19.2 1.3 %collective-permute-start.4 = (f32[3,96,128]{2,1,0:T(8,128)S(1)}, f32[3,96,128]{2,1,0:T(8,128)S(1)}, u32[]{:S(2)}, u32[]{:S(2)}) collective-permute-start(f32[3,96,128]{2,1,0:T(8,128)S(1)} %get-tuple-element.56), channel_id=1, source_target_pairs={{0,1},{1,2},{2,3},{3,0},{4,5},{5,6},{6,7},{7,4},{8,9},{9,10},{10,1... | collective-permute-start | bytes 442376 | tf_op jit(solution)/shard_map/ppermute | solution.py:516
  20.5 2.5 %collective-permute-start.5 = (f32[3,96,128]{2,1,0:T(8,128)S(1)}, f32[3,96,128]{2,1,0:T(8,128)S(1)}, u32[]{:S(2)}, u32[]{:S(2)}) collective-permute-start(f32[3,96,128]{2,1,0:T(8,128)S(1)} %get-tuple-element.58), channel_id=1, source_target_pairs={{0,2},{1,3},{2,0},{3,1},{4,6},{5,7},{6,4},{7,5},{8,10},{9,11},{10,... | collective-permute-start | bytes 442376 | tf_op jit(solution)/shard_map/ppermute | solution.py:516
  23.0 1.1 %collective-permute-start.6 = (f32[3,96,128]{2,1,0:T(8,128)S(1)}, f32[3,96,128]{2,1,0:T(8,128)S(1)}, u32[]{:S(2)}, u32[]{:S(2)}) collective-permute-start(f32[3,96,128]{2,1,0:T(8,128)S(1)} %get-tuple-element.60), channel_id=1, source_target_pairs={{0,3},{1,0},{2,1},{3,2},{4,7},{5,4},{6,5},{7,6},{8,11},{9,8},{10,9... | collective-permute-start | bytes 442376 | tf_op jit(solution)/shard_map/ppermute | solution.py:516
  24.1 4.0 %second_fields.1 = (f32[4,3,4,96,128]{4,3,2,1,0:T(8,128)S(1)}, f32[4,3,96,128]{3,2,1,0:T(8,128)S(1)}, f32[4,3,96,128]{3,2,1,0:T(8,128)S(1)}, f32[8,128]{1,0:T(8,128)S(1)}) custom-call(f32[4,3,4,96,128]{4,3,2,1,0:T(8,128)S(1)} %copy-done, f32[5,3,96,128]{3,2,1,0:T(8,128)S(1)} %collective-permute-done.before_ref.fbefore_ref, ...), custom_call_target="tpu_custom_call" | custom-call | tf_op jit(solution)/shard_map/second_fields/pallas_call | solution.py:264
  28.1 0.6 collective-permute-start.2
  28.7 3.1 %collective-permute-start.3 = (f32[4,3,96,128]{3,2,1,0:T(8,128)S(1)}, f32[4,3,96,128]{3,2,1,0:T(8,128)S(1)}, u32[]{:S(2)}, u32[]{:S(2)}) collective-permute-start(f32[4,3,96,128]{3,2,1,0:T(8,128)S(1)} %get-tuple-element.55), channel_id=1, source_target_pairs={{8,0},{16,8},{24,16},{32,24},{40,32},{48,40},{56,48},{64,56},{72,6... | collective-permute-start | bytes 1769480 | tf_op jit(solution)/shard_map/ppermute | solution.py:511
  31.9 0.0 collective-permute-done.4
  31.9 0.0 collective-permute-done.5
  31.9 0.0 collective-permute-done.6
  32.0 2.7 %collective-permute-start.7 = (f32[296,128]{1,0:T(8,128)S(1)}, f32[296,128]{1,0:T(8,128)S(1)}, u32[]{:S(2)}, u32[]{:S(2)}) collective-permute-start(f32[296,128]{1,0:T(8,128)S(1)} %pad_maximum_fusion), channel_id=1, source_target_pairs={{0,4},{1,5},{2,6},{3,7},{4,0},{5,1},{6,2},{7,3},{8,12},{9,13},{10,... | collective-permute-start | bytes 454664 | tf_op jit(solution)/shard_map/ppermute | solution.py:521
  34.7 6.0 %draw_noise.3.noise_ref = f32[4,3,4,96,128]{4,3,2,1,0:T(8,128)} custom-call(s32[8]{0:T(128)S(1)} %reshape.13.keys_ref), custom_call_target="tpu_custom_call" | custom-call | tf_op jit(solution)/shard_map/draw_noise/pallas_call | solution.py:74
  40.7 0.7 inner_stress.3.stress_ref
  41.4 2.5 %collective-permute-done.7 = f32[296,128]{1,0:T(8,128)S(1)} collective-permute-done((f32[296,128]{1,0:T(8,128)S(1)}, f32[296,128]{1,0:T(8,128)S(1)}, u32[]{:S(2)}, u32[]{:S(2)}) %collective-permute-start.7) | collective-permute-done | bytes 151584 | tf_op jit(solution)/shard_map/ppermute | solution.py:521
  44.0 0.1 collective-permute-start.10
  44.0 2.1 %collective-permute-start.9 = (f32[296,128]{1,0:T(8,128)S(1)}, f32[296,128]{1,0:T(8,128)S(1)}, u32[]{:S(2)}, u32[]{:S(2)}) collective-permute-start(f32[296,128]{1,0:T(8,128)S(1)} %fusion.p0), channel_id=1, source_target_pairs={{0,2},{1,3},{2,0},{3,1},{4,6},{5,7},{6,4},{7,5},{8,10},{9,11},{10,... | collective-permute-start | bytes 454664 | tf_op jit(solution)/shard_map/ppermute | solution.py:516
  46.1 0.0 collective-permute-start.8
  46.2 0.0 collective-permute-done.2.before_ref
  46.2 0.0 collective-permute-done.3.after_ref
  46.2 0.5 stress_parts.3
  46.7 0.0 copy-start.4
  46.7 0.8 copy-done.4
  47.5 2.7 %collective-permute-start.14 = (f32[3,96,128]{2,1,0:T(8,128)S(1)}, f32[3,96,128]{2,1,0:T(8,128)S(1)}, u32[]{:S(2)}, u32[]{:S(2)}) collective-permute-start(f32[3,96,128]{2,1,0:T(8,128)S(1)} %get-tuple-element.76), channel_id=1, source_target_pairs={{0,3},{1,0},{2,1},{3,2},{4,7},{5,4},{6,5},{7,6},{8,11},{9,8},{10,9... | collective-permute-start | bytes 442376 | tf_op jit(solution)/shard_map/ppermute | solution.py:516
  50.2 0.0 collective-permute-start.12
  50.2 0.0 collective-permute-done.10.p3
  50.2 1.7 %collective-permute-start.13 = (f32[3,96,128]{2,1,0:T(8,128)S(1)}, f32[3,96,128]{2,1,0:T(8,128)S(1)}, u32[]{:S(2)}, u32[]{:S(2)}) collective-permute-start(f32[3,96,128]{2,1,0:T(8,128)S(1)} %get-tuple-element.75), channel_id=1, source_target_pairs={{0,2},{1,3},{2,0},{3,1},{4,6},{5,7},{6,4},{7,5},{8,10},{9,11},{10,... | collective-permute-start | bytes 442376 | tf_op jit(solution)/shard_map/ppermute | solution.py:516
  51.9 0.0 collective-permute-done.9.p2
  51.9 0.1 collective-permute-done.8.p1
  52.1 2.3 %third_flow.1 = (f32[3,4,96,128]{3,2,1,0:T(8,128)S(1)}, f32[3,96,128]{2,1,0:T(8,128)S(1)}, f32[3,96,128]{2,1,0:T(8,128)S(1)}, f32[32,1,128]{2,1,0:T(1,128)}) custom-call(f32[3,4,96,128]{3,2,1,0:T(8,128)S(1)} %copy-done.2, f32[5,3,96,128]{3,2,1,0:T(8,128)S(1)} %collective-permute-done.before_ref.fbefore_ref, ...), custom_call_target="tpu_custom_call" | custom-call | tf_op jit(solution)/shard_map/third_flow/pallas_call | solution.py:354
  54.4 0.0 copy-done.3
  54.4 0.8 copy-done.5
  55.2 0.0 collective-permute-done.14
  55.2 2.2 %collective-permute-done.12 = f32[3,96,128]{2,1,0:T(8,128)S(1)} collective-permute-done((f32[3,96,128]{2,1,0:T(8,128)S(1)}, f32[3,96,128]{2,1,0:T(8,128)S(1)}, u32[]{:S(2)}, u32[]{:S(2)}) %collective-permute-start.12) | collective-permute-done | bytes 147488 | tf_op jit(solution)/shard_map/ppermute | solution.py:516
  57.4 1.7 %collective-permute-done.13 = f32[3,96,128]{2,1,0:T(8,128)S(1)} collective-permute-done((f32[3,96,128]{2,1,0:T(8,128)S(1)}, f32[3,96,128]{2,1,0:T(8,128)S(1)}, u32[]{:S(2)}, u32[]{:S(2)}) %collective-permute-start.13) | collective-permute-done | bytes 147488 | tf_op jit(solution)/shard_map/ppermute | solution.py:516
  59.1 4.9 %collective-permute-start.15 = (f32[288,128]{1,0:T(8,128)S(1)}, f32[288,128]{1,0:T(8,128)S(1)}, u32[]{:S(2)}, u32[]{:S(2)}) collective-permute-start(f32[288,128]{1,0:T(8,128)S(1)} %bitcast.5), channel_id=1, source_target_pairs={{0,4},{1,5},{2,6},{3,7},{4,0},{5,1},{6,2},{7,3},{8,12},{9,13},{10,... | collective-permute-start | bytes 442376 | tf_op jit(solution)/shard_map/ppermute | solution.py:521
  64.1 0.0 collective-permute-start.11
  64.1 1.6 %collective-permute-start.16 = (f32[3,96,128]{2,1,0:T(8,128)S(1)}, f32[3,96,128]{2,1,0:T(8,128)S(1)}, u32[]{:S(2)}, u32[]{:S(2)}) collective-permute-start(f32[3,96,128]{2,1,0:T(8,128)S(1)} %get-tuple-element.79), channel_id=1, source_target_pairs={{8,0},{16,8},{24,16},{32,24},{40,32},{48,40},{56,48},{64,56},{72,6... | collective-permute-start | bytes 442376 | tf_op jit(solution)/shard_map/ppermute | solution.py:511
  65.7 0.9 collective-permute-done.15
  66.6 0.9 collective-permute-start.19
  67.5 1.1 %collective-permute-start.18 = (f32[288,128]{1,0:T(8,128)S(1)}, f32[288,128]{1,0:T(8,128)}, u32[]{:S(2)}, u32[]{:S(2)}) collective-permute-start(f32[288,128]{1,0:T(8,128)S(1)} %bitcast_add_fusion.p0), channel_id=1, source_target_pairs={{0,2},{1,3},{2,0},{3,1},{4,6},{5,7},{6,4},{7,5},{8,10},{9,11},{10,... | collective-permute-start | bytes 442376 | tf_op jit(solution)/shard_map/ppermute | solution.py:516
  68.6 0.8 collective-permute-start.17
  69.3 12.7 %all-to-all-start = ((f32[32,1,128]{2,1,0:T(1,128)}), f32[32,1,128]{2,1,0:T(1,128)S(1)}, u32[]{:S(2)}, u32[]{:S(2)}) async-start(f32[32,1,128]{2,1,0:T(1,128)} %get-tuple-element.80), calls=%async_computation | async-start | bytes 32768 | tf_op jit(solution)/shard_map/all_to_all | solution.py:568
  82.0 0.0 collective-permute-done.11.sbefore_ref
  82.1 0.0 collective-permute-done.16.safter_ref
  82.1 5.0 %fourth_fields.1.rough_ref = f32[4,3,4,96,128]{4,3,2,1,0:T(8,128)S(1)} custom-call(f32[4,3,4,96,128]{4,3,2,1,0:T(8,128)} %copy-done.1, f32[4,3,96,128]{3,2,1,0:T(8,128)} %copy-done.3, f32[4,3,96,128]{3,2,1,0:T(8,128)} %copy-done.4, f32[3,4,96,128]{3,2,1,0:T(8,128)} %copy-done.5, f32[3,96,128]{2,1,0:T(8,128)S(1)} %collective-permute-done.11.sbefore_ref, ...), custom_call_target="tpu_custom_call" | custom-call | tf_op jit(solution)/shard_map/fourth_fields/pallas_call | solution.py:395
  87.1 2.8 %all-to-all-done.shared_ref = f32[32,1,128]{2,1,0:T(1,128)S(1)} async-done(((f32[32,1,128]{2,1,0:T(1,128)}), f32[32,1,128]{2,1,0:T(1,128)S(1)}, u32[]{:S(2)}, u32[]{:S(2)}) %all-to-all-start) | async-done | bytes 16416 | tf_op jit(solution)/shard_map/all_to_all | solution.py:568
  89.9 4.4 %lift_fields.1 = f32[4,3,4,96,128]{4,3,2,1,0:T(8,128)} custom-call(f32[4,3,4,96,128]{4,3,2,1,0:T(8,128)S(1)} %fourth_fields.1.rough_ref, f32[4,3,4,96,128]{4,3,2,1,0:T(8,128)} %copy-done.1, f32[4,3,96,128]{3,2,1,0:T(8,128)} %copy-done.3, f32[4,3,96,128]{3,2,1,0:T(8,128)} %copy-done.4, f32[32,1,128]{2,1,0:T(1,128)S(1)} %all-to-all-done.shared_ref), custom_call_target="tpu_custom_call" | custom-call | tf_op jit(solution)/shard_map/lift_fields/pallas_call | solution.py:424
  94.3 0.0 collective-permute-done.19.p3
  94.3 0.0 collective-permute-done.18.p2
  94.3 0.0 collective-permute-done.17.p1
  94.3 2.5 %fifth_flow.1 = f32[3,4,96,128]{3,2,1,0:T(8,128)} custom-call(f32[3,4,96,128]{3,2,1,0:T(8,128)S(1)} %copy-done.6, f32[3,96,128]{2,1,0:T(8,128)S(1)} %collective-permute-done.11.sbefore_ref, f32[3,96,128]{2,1,0:T(8,128)S(1)} %collective-permute-done.16.safter_ref, f32[288,128]{1,0:T(8,128)S(1)} %bitcast_add_fusion.p0, f32[288,128]{1,0:T(8,128)} %collective-permute-done.17.p1, ...), custom_call_target="tpu_custom_call" | custom-call | tf_op jit(solution)/shard_map/fifth_flow/pallas_call | solution.py:460
  (13 shorter events, 0.1 us)
Async XLA Ops:
  0.6 5.8 %copy-start.7 = (s32[4,2]{0,1:T(2,128)S(1)}, s32[4,2]{0,1:T(2,128)}, u32[]{:S(2)}) copy-start(s32[4,2]{0,1:T(2,128)} %param.5) | copy-start | bytes 100
  3.2 8.6 %copy-start = (f32[4,3,4,96,128]{4,3,2,1,0:T(8,128)S(1)}, f32[4,3,4,96,128]{4,3,2,1,0:T(8,128)}, u32[]{:S(2)}) copy-start(f32[4,3,4,96,128]{4,3,2,1,0:T(8,128)} %config_ref.2) | copy-start | bytes 7077892
  3.2 11.8 %collective-permute-start = (f32[5,3,96,128]{3,2,1,0:T(8,128)}, f32[5,3,96,128]{3,2,1,0:T(8,128)S(1)}, u32[]{:S(2)}, u32[]{:S(2)}) collective-permute-start(f32[5,3,96,128]{3,2,1,0:T(8,128)} %get-tuple-element.46), channel_id=1, source_target_pairs={{0,8},{8,16},{16,24},{24,32},{32,40},{40,48},{48,56},{56,64},{64,7... | collective-permute-start | bytes 2211848 | tf_op jit(solution)/shard_map/ppermute | solution.py:506
  6.2 11.4 %collective-permute-start.1 = (f32[5,3,96,128]{3,2,1,0:T(8,128)}, f32[5,3,96,128]{3,2,1,0:T(8,128)}, u32[]{:S(2)}, u32[]{:S(2)}) collective-permute-start(f32[5,3,96,128]{3,2,1,0:T(8,128)} %get-tuple-element.49), channel_id=1, source_target_pairs={{8,0},{16,8},{24,16},{32,24},{40,32},{48,40},{56,48},{64,56},{72,6... | collective-permute-start | bytes 2211848 | tf_op jit(solution)/shard_map/ppermute | solution.py:511
  11.8 12.3 %copy-start.2 = (f32[3,4,96,128]{3,2,1,0:T(8,128)S(1)}, f32[3,4,96,128]{3,2,1,0:T(8,128)}, u32[]{:S(2)}) copy-start(f32[3,4,96,128]{3,2,1,0:T(8,128)} %flow_ref.3) | copy-start | bytes 1769476
  19.2 12.7 %collective-permute-start.4 = (f32[3,96,128]{2,1,0:T(8,128)S(1)}, f32[3,96,128]{2,1,0:T(8,128)S(1)}, u32[]{:S(2)}, u32[]{:S(2)}) collective-permute-start(f32[3,96,128]{2,1,0:T(8,128)S(1)} %get-tuple-element.56), channel_id=1, source_target_pairs={{0,1},{1,2},{2,3},{3,0},{4,5},{5,6},{6,7},{7,4},{8,9},{9,10},{10,1... | collective-permute-start | bytes 442376 | tf_op jit(solution)/shard_map/ppermute | solution.py:516
  20.5 11.4 %collective-permute-start.5 = (f32[3,96,128]{2,1,0:T(8,128)S(1)}, f32[3,96,128]{2,1,0:T(8,128)S(1)}, u32[]{:S(2)}, u32[]{:S(2)}) collective-permute-start(f32[3,96,128]{2,1,0:T(8,128)S(1)} %get-tuple-element.58), channel_id=1, source_target_pairs={{0,2},{1,3},{2,0},{3,1},{4,6},{5,7},{6,4},{7,5},{8,10},{9,11},{10,... | collective-permute-start | bytes 442376 | tf_op jit(solution)/shard_map/ppermute | solution.py:516
  23.0 8.9 %collective-permute-start.6 = (f32[3,96,128]{2,1,0:T(8,128)S(1)}, f32[3,96,128]{2,1,0:T(8,128)S(1)}, u32[]{:S(2)}, u32[]{:S(2)}) collective-permute-start(f32[3,96,128]{2,1,0:T(8,128)S(1)} %get-tuple-element.60), channel_id=1, source_target_pairs={{0,3},{1,0},{2,1},{3,2},{4,7},{5,4},{6,5},{7,6},{8,11},{9,8},{10,9... | collective-permute-start | bytes 442376 | tf_op jit(solution)/shard_map/ppermute | solution.py:516
  28.1 13.3 %copy-start.1 = (f32[4,3,4,96,128]{4,3,2,1,0:T(8,128)}, f32[4,3,4,96,128]{4,3,2,1,0:T(8,128)S(1)}, u32[]{:S(2)}) copy-start(f32[4,3,4,96,128]{4,3,2,1,0:T(8,128)S(1)} %get-tuple-element.64.config_ref) | copy-start | bytes 7077892
  28.1 18.0 %collective-permute-start.2 = (f32[4,3,96,128]{3,2,1,0:T(8,128)S(1)}, f32[4,3,96,128]{3,2,1,0:T(8,128)S(1)}, u32[]{:S(2)}, u32[]{:S(2)}) collective-permute-start(f32[4,3,96,128]{3,2,1,0:T(8,128)S(1)} %get-tuple-element.54), channel_id=1, source_target_pairs={{0,8},{8,16},{16,24},{24,32},{32,40},{40,48},{48,56},{56,64},{64,7... | collective-permute-start | bytes 1769480 | tf_op jit(solution)/shard_map/ppermute | solution.py:506
  28.7 17.4 %collective-permute-start.3 = (f32[4,3,96,128]{3,2,1,0:T(8,128)S(1)}, f32[4,3,96,128]{3,2,1,0:T(8,128)S(1)}, u32[]{:S(2)}, u32[]{:S(2)}) collective-permute-start(f32[4,3,96,128]{3,2,1,0:T(8,128)S(1)} %get-tuple-element.55), channel_id=1, source_target_pairs={{8,0},{16,8},{24,16},{32,24},{40,32},{48,40},{56,48},{64,56},{72,6... | collective-permute-start | bytes 1769480 | tf_op jit(solution)/shard_map/ppermute | solution.py:511
  32.0 12.0 %collective-permute-start.7 = (f32[296,128]{1,0:T(8,128)S(1)}, f32[296,128]{1,0:T(8,128)S(1)}, u32[]{:S(2)}, u32[]{:S(2)}) collective-permute-start(f32[296,128]{1,0:T(8,128)S(1)} %pad_maximum_fusion), channel_id=1, source_target_pairs={{0,4},{1,5},{2,6},{3,7},{4,0},{5,1},{6,2},{7,3},{8,12},{9,13},{10,... | collective-permute-start | bytes 454664 | tf_op jit(solution)/shard_map/ppermute | solution.py:521
  44.0 6.2 %collective-permute-start.10 = (f32[296,128]{1,0:T(8,128)S(1)}, f32[296,128]{1,0:T(8,128)S(1)}, u32[]{:S(2)}, u32[]{:S(2)}) collective-permute-start(f32[296,128]{1,0:T(8,128)S(1)} %fusion.p0), channel_id=1, source_target_pairs={{0,3},{1,0},{2,1},{3,2},{4,7},{5,4},{6,5},{7,6},{8,11},{9,8},{10,9... | collective-permute-start | bytes 454664 | tf_op jit(solution)/shard_map/ppermute | solution.py:516
  44.0 7.9 %collective-permute-start.9 = (f32[296,128]{1,0:T(8,128)S(1)}, f32[296,128]{1,0:T(8,128)S(1)}, u32[]{:S(2)}, u32[]{:S(2)}) collective-permute-start(f32[296,128]{1,0:T(8,128)S(1)} %fusion.p0), channel_id=1, source_target_pairs={{0,2},{1,3},{2,0},{3,1},{4,6},{5,7},{6,4},{7,5},{8,10},{9,11},{10,... | collective-permute-start | bytes 454664 | tf_op jit(solution)/shard_map/ppermute | solution.py:516
  46.1 5.9 %collective-permute-start.8 = (f32[296,128]{1,0:T(8,128)S(1)}, f32[296,128]{1,0:T(8,128)S(1)}, u32[]{:S(2)}, u32[]{:S(2)}) collective-permute-start(f32[296,128]{1,0:T(8,128)S(1)} %fusion.p0), channel_id=1, source_target_pairs={{0,1},{1,2},{2,3},{3,0},{4,5},{5,6},{6,7},{7,4},{8,9},{9,10},{10,1... | collective-permute-start | bytes 454664 | tf_op jit(solution)/shard_map/ppermute | solution.py:516
  46.2 8.3 %copy-start.3 = (f32[4,3,96,128]{3,2,1,0:T(8,128)}, f32[4,3,96,128]{3,2,1,0:T(8,128)S(1)}, u32[]{:S(2)}) copy-start(f32[4,3,96,128]{3,2,1,0:T(8,128)S(1)} %collective-permute-done.2.before_ref) | copy-start | bytes 1769476
  46.7 0.8 copy-start.4
  47.5 7.7 %collective-permute-start.14 = (f32[3,96,128]{2,1,0:T(8,128)S(1)}, f32[3,96,128]{2,1,0:T(8,128)S(1)}, u32[]{:S(2)}, u32[]{:S(2)}) collective-permute-start(f32[3,96,128]{2,1,0:T(8,128)S(1)} %get-tuple-element.76), channel_id=1, source_target_pairs={{0,3},{1,0},{2,1},{3,2},{4,7},{5,4},{6,5},{7,6},{8,11},{9,8},{10,9... | collective-permute-start | bytes 442376 | tf_op jit(solution)/shard_map/ppermute | solution.py:516
  50.2 7.2 %collective-permute-start.12 = (f32[3,96,128]{2,1,0:T(8,128)S(1)}, f32[3,96,128]{2,1,0:T(8,128)S(1)}, u32[]{:S(2)}, u32[]{:S(2)}) collective-permute-start(f32[3,96,128]{2,1,0:T(8,128)S(1)} %get-tuple-element.74), channel_id=1, source_target_pairs={{0,1},{1,2},{2,3},{3,0},{4,5},{5,6},{6,7},{7,4},{8,9},{9,10},{10,1... | collective-permute-start | bytes 442376 | tf_op jit(solution)/shard_map/ppermute | solution.py:516
  50.2 8.9 %collective-permute-start.13 = (f32[3,96,128]{2,1,0:T(8,128)S(1)}, f32[3,96,128]{2,1,0:T(8,128)S(1)}, u32[]{:S(2)}, u32[]{:S(2)}) collective-permute-start(f32[3,96,128]{2,1,0:T(8,128)S(1)} %get-tuple-element.75), channel_id=1, source_target_pairs={{0,2},{1,3},{2,0},{3,1},{4,6},{5,7},{6,4},{7,5},{8,10},{9,11},{10,... | collective-permute-start | bytes 442376 | tf_op jit(solution)/shard_map/ppermute | solution.py:516
  54.4 0.8 copy-start.5
  59.1 7.5 %collective-permute-start.15 = (f32[288,128]{1,0:T(8,128)S(1)}, f32[288,128]{1,0:T(8,128)S(1)}, u32[]{:S(2)}, u32[]{:S(2)}) collective-permute-start(f32[288,128]{1,0:T(8,128)S(1)} %bitcast.5), channel_id=1, source_target_pairs={{0,4},{1,5},{2,6},{3,7},{4,0},{5,1},{6,2},{7,3},{8,12},{9,13},{10,... | collective-permute-start | bytes 442376 | tf_op jit(solution)/shard_map/ppermute | solution.py:521
  64.1 18.0 %collective-permute-start.11 = (f32[3,96,128]{2,1,0:T(8,128)S(1)}, f32[3,96,128]{2,1,0:T(8,128)S(1)}, u32[]{:S(2)}, u32[]{:S(2)}) collective-permute-start(f32[3,96,128]{2,1,0:T(8,128)S(1)} %get-tuple-element.73), channel_id=1, source_target_pairs={{0,8},{8,16},{16,24},{24,32},{32,40},{40,48},{48,56},{56,64},{64,7... | collective-permute-start | bytes 442376 | tf_op jit(solution)/shard_map/ppermute | solution.py:506
  64.1 18.0 %collective-permute-start.16 = (f32[3,96,128]{2,1,0:T(8,128)S(1)}, f32[3,96,128]{2,1,0:T(8,128)S(1)}, u32[]{:S(2)}, u32[]{:S(2)}) collective-permute-start(f32[3,96,128]{2,1,0:T(8,128)S(1)} %get-tuple-element.79), channel_id=1, source_target_pairs={{8,0},{16,8},{24,16},{32,24},{40,32},{48,40},{56,48},{64,56},{72,6... | collective-permute-start | bytes 442376 | tf_op jit(solution)/shard_map/ppermute | solution.py:511
  66.6 27.7 %collective-permute-start.19 = (f32[288,128]{1,0:T(8,128)S(1)}, f32[288,128]{1,0:T(8,128)S(1)}, u32[]{:S(2)}, u32[]{:S(2)}) collective-permute-start(f32[288,128]{1,0:T(8,128)S(1)} %bitcast_add_fusion.p0), channel_id=1, source_target_pairs={{0,3},{1,0},{2,1},{3,2},{4,7},{5,4},{6,5},{7,6},{8,11},{9,8},{10,9... | collective-permute-start | bytes 442376 | tf_op jit(solution)/shard_map/ppermute | solution.py:516
  67.5 26.8 %collective-permute-start.18 = (f32[288,128]{1,0:T(8,128)S(1)}, f32[288,128]{1,0:T(8,128)}, u32[]{:S(2)}, u32[]{:S(2)}) collective-permute-start(f32[288,128]{1,0:T(8,128)S(1)} %bitcast_add_fusion.p0), channel_id=1, source_target_pairs={{0,2},{1,3},{2,0},{3,1},{4,6},{5,7},{6,4},{7,5},{8,10},{9,11},{10,... | collective-permute-start | bytes 442376 | tf_op jit(solution)/shard_map/ppermute | solution.py:516
  68.6 25.7 %collective-permute-start.17 = (f32[288,128]{1,0:T(8,128)S(1)}, f32[288,128]{1,0:T(8,128)}, u32[]{:S(2)}, u32[]{:S(2)}) collective-permute-start(f32[288,128]{1,0:T(8,128)S(1)} %bitcast_add_fusion.p0), channel_id=1, source_target_pairs={{0,1},{1,2},{2,3},{3,0},{4,5},{5,6},{6,7},{7,4},{8,9},{9,10},{10,1... | collective-permute-start | bytes 442376 | tf_op jit(solution)/shard_map/ppermute | solution.py:516
  69.3 20.6 %all-to-all-start = ((f32[32,1,128]{2,1,0:T(1,128)}), f32[32,1,128]{2,1,0:T(1,128)S(1)}, u32[]{:S(2)}, u32[]{:S(2)}) async-start(f32[32,1,128]{2,1,0:T(1,128)} %get-tuple-element.80), calls=%async_computation | async-start | bytes 32768 | tf_op jit(solution)/shard_map/all_to_all | solution.py:568
  87.1 7.2 %copy-start.6 = (f32[3,4,96,128]{3,2,1,0:T(8,128)S(1)}, f32[3,4,96,128]{3,2,1,0:T(8,128)}, u32[]{:S(2)}) copy-start(f32[3,4,96,128]{3,2,1,0:T(8,128)} %copy-done.5) | copy-start | bytes 1769476
